TPU v7x, 768 devices: a whole 4x8x12 slice. The times are simulated.
768 devices in a mesh: fsdp: 64 (over z_hi, y, core), dp: 12 (over z_lo, x).
Axes of the slice: x: 4, y: 8, z: 12 (z_hi: 4, z_lo: 3; z = z_hi * 3 + z_lo), core: 2. Of those that a mesh axis runs over, the one named last changes fastest.
Arguments:
- inputs: bfloat16 [147456, 4096], P(('fsdp', 'dp')), may hold values from -6 to 6
- output_gradient_rows: bfloat16 [147456, 512], P(('fsdp', 'dp')), may hold values from -6 to 6
- fixed_value_weight: bfloat16 [4096, 512], P('fsdp'), may hold values from -0.09375 to 0.09375
- task_down_adapters: bfloat16 [12, 4096, 64], P('dp'), may hold values from -0.09375 to 0.09375
- task_up_adapters: bfloat16 [12, 64, 512], P('dp'), may hold values from -0.75 to 0.75
- live_row_counts: int32 [768, 12], P(('fsdp', 'dp')), may hold values from 0 to 16, as said below
- row_packing_order: int32 [768, 192], P(('fsdp', 'dp')), may hold values from 0 to 191, each once within a row
Outputs:
- input_grad: bfloat16 [147456, 4096], P(('fsdp', 'dp'))
- down_grad: float32 [12, 4096, 64], P('dp', 'fsdp')
- up_grad: float32 [12, 64, 512], P('dp', None, 'fsdp')
Inputs may be any that keep to these rules, and one draw needn't show every extreme that they name: `live_row_counts`: for some task, every device of one fsdp index holds 16 live rows of it. Each row of row_packing_order is a permutation.
All inputs are finite; a program needn't handle non-finite values.
Results may differ from a plain program's by a relative error of at most 0.007.
Values may be sent and summed in bfloat16 or wider, within the bound.
No kernel may reach another device: no remote copies, remote signals or barrier semaphores. Data moves between devices by JAX's collectives and lax.ppermute only.
A program may use at most 64 MiB of HBM per device.

v0:
```python
import jax
import jax.numpy as jnp
from jax import lax
from jax.sharding import PartitionSpec as P

ADAPTER_SCALING = 2.0


def on_device(
    inputs,
    output_gradient_rows,
    fixed_value_weight,
    task_down_adapters,
    task_up_adapters,
    live_row_counts,
    row_packing_order,
):
    per_device, features = inputs.shape
    kv_width = output_gradient_rows.shape[1]
    task_groupings = lax.axis_size("dp")
    slot_rows = per_device // task_groupings
    packing = row_packing_order[0]
    counts = live_row_counts[0]
    local_down_adapter = task_down_adapters[0]
    slot_index = lax.broadcasted_iota(jnp.int32, (task_groupings, slot_rows), 1)
    is_live = slot_index < counts[:, None]
    packed_rows = jnp.take(inputs, packing, axis=0)
    packed_grads = jnp.take(output_gradient_rows, packing, axis=0).reshape(
        task_groupings, slot_rows, kv_width
    )
    packed_grads = jnp.where(is_live[:, :, None], packed_grads, jnp.zeros((), packed_grads.dtype))
    frozen_dx = lax.dot_general(
        output_gradient_rows,
        lax.all_gather(fixed_value_weight, "fsdp", axis=0, tiled=True),
        (((1,), (1,)), ((), ())),
        preferred_element_type=jnp.float32,
    ).astype(jnp.bfloat16)
    recv_rows, received_gradients = (
        lax.all_to_all(packed_rows, "dp", split_axis=0, concat_axis=0, tiled=True),
        lax.all_to_all(
            packed_grads.reshape(per_device, kv_width),
            "dp",
            split_axis=0,
            concat_axis=0,
            tiled=True,
        ),
    )
    down_projected_rows = jnp.dot(
        recv_rows, local_down_adapter, preferred_element_type=jnp.float32
    ).astype(jnp.bfloat16)
    gradient_projected = lax.dot_general(
        received_gradients,
        task_up_adapters[0],
        (((1,), (1,)), ((), ())),
        preferred_element_type=jnp.float32,
    ).astype(jnp.bfloat16)
    adapter_input_gradient = (
        ADAPTER_SCALING
        * lax.dot_general(
            gradient_projected,
            local_down_adapter,
            (((1,), (1,)), ((), ())),
            preferred_element_type=jnp.float32,
        )
    ).astype(jnp.bfloat16)
    down_weight_gradient = ADAPTER_SCALING * lax.dot_general(
        recv_rows, gradient_projected, (((0,), (0,)), ((), ())), preferred_element_type=jnp.float32
    )
    up_gradient_turned = ADAPTER_SCALING * lax.dot_general(
        received_gradients,
        down_projected_rows,
        (((0,), (0,)), ((), ())),
        preferred_element_type=jnp.float32,
    )
    returned = lax.all_to_all(adapter_input_gradient, "dp", split_axis=0, concat_axis=0, tiled=True)
    down_share, up_turned_share = (
        lax.psum_scatter(down_weight_gradient, "fsdp", scatter_dimension=0, tiled=True),
        lax.psum_scatter(up_gradient_turned, "fsdp", scatter_dimension=0, tiled=True),
    )
    up_share = up_turned_share.T
    placed = jnp.zeros((per_device, features), jnp.bfloat16).at[packing].set(returned)
    input_grad = (frozen_dx.astype(jnp.float32) + placed.astype(jnp.float32)).astype(jnp.bfloat16)
    return (input_grad, down_share[None], up_share[None])


def solution(mesh):
    in_specs = (
        P(("fsdp", "dp"), None),
        P(("fsdp", "dp"), None),
        P("fsdp", None),
        P("dp", None, None),
        P("dp", None, None),
        P(("fsdp", "dp"), None),
        P(("fsdp", "dp"), None),
    )
    out_specs = (P(("fsdp", "dp"), None), P("dp", "fsdp", None), P("dp", None, "fsdp"))
    return jax.shard_map(
        on_device, mesh=mesh, in_specs=in_specs, out_specs=out_specs, check_vma=False
    )
```

profile of v0, /device:TPU:6, one launch (start us, length us, event | category | flops | bytes accessed | tf_op | source)
XLA Modules:
  0.0 913.3 jit_solution(14370974991969763525)
XLA Ops:
  7.2 0.0 copy-start
  7.2 0.0 copy-start.3
  7.2 0.8 compare_select_fusion.1
  8.0 0.5 broadcast.61
  8.5 1.3 reduce.3
  9.9 0.1 squeeze.12
  9.9 2.0 gather_fusion
  11.9 0.0 copy-done.3
  12.0 0.1 iota_compare_fusion
  12.0 0.8 select_select_fusion
  12.8 12.9 %all-to-all-start = ((bf16[12,16,512]{2,1,0:T(8,128)(2,1)}), bf16[12,16,512]{2,1,0:T(8,128)(2,1)S(1)}, u32[]{:S(2)}, u32[]{:S(2)}) async-start(bf16[12,16,512]{2,1,0:T(8,128)(2,1)} %select_select_fusion), calls=%async_computation | async-start | bytes 393216 | tf_op jit(solution)/shard_map/all_to_all | solution.py:40
  25.7 0.0 all-reduce.3.cloned.1.call-start
  25.7 0.0 copy-done
  25.7 1.5 gather_fusion.1
  27.2 1.4 broadcast_select_fusion
  28.6 3.6 all-to-all-done
  32.1 25.5 %all_to_all.30 = bf16[12,16,4096]{2,1,0:T(8,128)(2,1)S(1)} all-to-all(bf16[12,16,4096]{2,1,0:T(8,128)(2,1)} %broadcast_select_fusion), channel_id=1, replica_groups=mesh['fsdp'=64,'dp'=12] {'dp'}, dimensions={0} | all-to-all | bytes 3145728 | tf_op jit(solution)/shard_map/all_to_all | solution.py:39
  57.6 0.0 copy-start.2
  57.6 2.7 convolution_multiply_fusion.2
  60.4 0.0 all-reduce.3.cloned.1.call-update
  60.4 0.0 all-gather.2.cloned.1.call-start
  60.4 0.7 all-gather.2.cloned.1.call-update
  61.1 0.0 copy-done.2
  61.1 0.2 convolution_convert_fusion.2
  61.3 2.8 fusion
  64.1 4.9 all-to-all-start.1
  69.0 0.0 reduce-scatter.2.cloned.1.call-start
  69.0 2.1 convolution_multiply_fusion.1
  71.1 0.0 copy-start.1
  71.1 0.0 reduce-scatter.2.cloned.1.call-update
  71.1 1.3 dynamic-slice
  73.1 564.7 %all-reduce.3.cloned.1.call-done = f32[512,64]{1,0:T(8,128)} async-done(((f32[512,64]{1,0:T(8,128)}), f32[512,64]{1,0:T(8,128)}) %all-reduce.3.cloned.1.call-update) | async-done | bytes 131088
  637.8 1.3 dynamic-slice_bitcast_fusion
  639.1 0.0 all-to-all-done.1
  639.1 4.0 scatter_custom_fusion
  643.2 100.3 %all-gather.2.cloned.1.call-done = bf16[4096,512]{1,0:T(8,128)(2,1)} async-done(((bf16[64,512]{1,0:T(8,128)(2,1)}), bf16[4096,512]{1,0:T(8,128)(2,1)}) %all-gather.2.cloned.1.call-update) | async-done | bytes 4194320 | tf_op jit(solution)/shard_map/all_gather | solution.py:34
  743.4 0.0 copy-done.1
  743.4 4.8 fusion.3
  748.3 158.5 %reduce-scatter.2.cloned.1.call-done = f32[64,64]{1,0:T(8,128)} async-done(((f32[4096,64]{1,0:T(8,128)}), f32[64,64]{1,0:T(8,128)}) %reduce-scatter.2.cloned.1.call-update) | async-done | bytes 16400 | tf_op jit(solution)/shard_map/reduce_scatter | solution.py:77
  (1 shorter events, 0.0 us)
Async XLA Ops:
  7.2 18.5 %copy-start = (bf16[192,4096]{1,0:T(8,128)(2,1)S(1)}, bf16[192,4096]{1,0:T(8,128)(2,1)}, u32[]{:S(2)}) copy-start(bf16[192,4096]{1,0:T(8,128)(2,1)} %param.7) | copy-start | bytes 4718596
  7.2 4.8 copy-start.3
  12.8 19.3 %all-to-all-start = ((bf16[12,16,512]{2,1,0:T(8,128)(2,1)}), bf16[12,16,512]{2,1,0:T(8,128)(2,1)S(1)}, u32[]{:S(2)}, u32[]{:S(2)}) async-start(bf16[12,16,512]{2,1,0:T(8,128)(2,1)} %select_select_fusion), calls=%async_computation | async-start | bytes 393216 | tf_op jit(solution)/shard_map/all_to_all | solution.py:40
  25.7 612.1 %all-reduce.3.cloned.1.call-start = ((), (), s32[]{:S(2)}) async-start(), calls=%async_computation.6 | async-start | bytes 524288
  57.6 3.5 copy-start.2
  60.4 683.0 %all-gather.2.cloned.1.call-start = ((), (), s32[]{:S(2)}) async-start(), calls=%async_computation.4 | async-start | bytes 4259840 | tf_op jit(solution)/shard_map/all_gather | solution.py:34
  64.1 575.0 %all-to-all-start.1 = ((bf16[12,16,4096]{2,1,0:T(8,128)(2,1)}), bf16[12,16,4096]{2,1,0:T(8,128)(2,1)}, u32[]{:S(2)}, u32[]{:S(2)}) async-start(bf16[12,16,4096]{2,1,0:T(8,128)(2,1)} %bitcast.35), calls=%async_computation.1 | async-start | bytes 3145728 | tf_op jit(solution)/shard_map/all_to_all | solution.py:75
  69.0 837.8 %reduce-scatter.2.cloned.1.call-start = ((), (), s32[]{:S(2)}) async-start(), calls=%async_computation.5 | async-start | bytes 2129920 | tf_op jit(solution)/shard_map/reduce_scatter | solution.py:77
  71.1 672.3 %copy-start.1 = (bf16[192,512]{1,0:T(8,128)(2,1)S(1)}, bf16[192,512]{1,0:T(8,128)(2,1)}, u32[]{:S(2)}) copy-start(bf16[192,512]{1,0:T(8,128)(2,1)} %param.8) | copy-start | bytes 589828
Sparse Core Ops, SparseCore 0:
  60.5 577.2 all-reduce.2
  642.5 100.9 all-gather.1
  750.1 156.6 reduce-scatter.1
where the time goes:
time: 914 us; the launch traced here: 913 us
  waiting for transfers between devices  828 us (91%)
  blocking collectives  25.5 us (3%)
  starting transfers between devices  17.8 us (2%)
  between operations  14.5 us (2%)
  matrix products  12.6 us (1%)
  local copies, waits for them, and re-layouts  10.8 us (1%)
    unnamed x4, waiting for transfers between devices  565 us
    reduce_scatter x1, waiting for transfers between devices, on_device(): lax.psum_scatter(down_weight_gradient, 'fsdp', scatter_dimension=0, tiled...  158 us
    all_gather x1, waiting for transfers between devices, on_device(): lax.all_gather(fixed_value_weight, 'fsdp', axis=0, tiled=True)  100 us
    all_to_all x1, blocking collectives, on_device(): lax.all_to_all(packed_rows, 'dp', split_axis=0, concat_axis=0, tiled=True)  25.5 us
  transfers between devices with their start and end apart: 5, of which 4 were waited for; matrix products, arithmetic and copies ran while one was open for 2% of the time, Pallas kernels for 0%

commit v1 on v0

v1 whole, which is shorter than its diff:
```python
import functools

import jax
import jax.numpy as jnp
import numpy as np
from jax import lax
from jax.experimental import pallas as pl
from jax.experimental.pallas import tpu as pltpu
from jax.sharding import Mesh, PartitionSpec as P

ADAPTER_SCALING = 2.0
FSDP = ("zh", "y", "c")
DP = ("zl", "x")
VMEM_LIMIT = 48 * 1024 * 1024
NT = (((1,), (1,)), ((), ()))
NN = (((1,), (0,)), ((), ()))
TN = (((0,), (0,)), ((), ()))


def dot(a, b, dims):
    return lax.dot_general(a, b, dims, preferred_element_type=jnp.float32)


def live_one_hot(counts_ref, packing_ref):
    per_device = packing_ref.shape[1]
    tasks = counts_ref.shape[1]
    slot = per_device // tasks
    lane = lax.broadcasted_iota(jnp.int32, (1, per_device), 1)
    key = jnp.full((1, per_device), -1, jnp.int32)
    packing = packing_ref[...]
    for t in range(tasks):
        mine = (lane >= t * slot) & (lane < t * slot + counts_ref[0, t])
        key = jnp.where(mine, packing, key)
    row = lax.broadcasted_iota(jnp.int32, (per_device, per_device), 0)
    return jnp.where(row == key, 1.0, 0.0).astype(jnp.bfloat16)


def pack_kernel(counts_ref, packing_ref, rows_ref, grads_ref, out_ref):
    chosen = live_one_hot(counts_ref, packing_ref)
    features = rows_ref.shape[1]
    step = 1024
    for at in range(0, features, step):
        out_ref[:, at : at + step] = dot(chosen, rows_ref[:, at : at + step], TN).astype(jnp.bfloat16)
    out_ref[:, features:] = dot(chosen, grads_ref[...], TN).astype(jnp.bfloat16)


def input_grad_kernel(grads_ref, down_t_ref, up_ref, dx_ref, proj_ref):
    proj = dot(grads_ref[...], up_ref[...], NT).astype(jnp.bfloat16)
    proj_ref[...] = proj
    features = down_t_ref.shape[1]
    step = 1024
    for at in range(0, features, step):
        dx = ADAPTER_SCALING * dot(proj, down_t_ref[:, at : at + step], NN)
        dx_ref[:, at : at + step] = dx.astype(jnp.bfloat16)


def weight_grad_kernel(core_ref, recv_ref, down_t_ref, proj_ref, keep_ref, send_ref):
    rank, features = down_t_ref.shape
    blocks = keep_ref.shape[0]
    first = core_ref[0] == 0
    wide = features // blocks
    half = wide // 2
    quarter = half // 2
    proj = proj_ref[...]
    total = jnp.zeros((recv_ref.shape[0], rank), jnp.float32)
    step = 1024
    for at in range(0, features, step):
        rows = recv_ref[:, at : at + step]
        total = total + dot(rows, down_t_ref[:, at : at + step], NT)
        down = ADAPTER_SCALING * dot(rows, proj, TN)
        for b in range(step // wide):
            pair = []
            for c in range(2):
                lo = b * wide + c * half
                pair.append(jnp.concatenate([down[lo : lo + quarter], down[lo + quarter : lo + half]], axis=1))
            keep_ref[at // wide + b, :quarter, :] = jnp.where(first, pair[0], pair[1])
            send_ref[at // wide + b, :quarter, :] = jnp.where(first, pair[1], pair[0])
    grads = recv_ref[:, features:]
    up_t = ADAPTER_SCALING * dot(grads, total.astype(jnp.bfloat16), TN)
    up_t = jnp.concatenate([up_t, jnp.zeros_like(up_t)], axis=1)
    few = grads.shape[1] // (2 * blocks)
    for b in range(blocks):
        low, high = up_t[2 * b * few : (2 * b + 1) * few], up_t[(2 * b + 1) * few : (2 * b + 2) * few]
        keep_ref[b, quarter:, :] = jnp.where(first, low, high)
        send_ref[b, quarter:, :] = jnp.where(first, high, low)


def final_kernel(core_ref, counts_ref, packing_ref, grads_ref, own_ref, other_ref, back_ref, out_ref, chosen_ref):
    @pl.when(pl.program_id(0) == 0)
    def _():
        chosen_ref[...] = live_one_hot(counts_ref, packing_ref)

    first = core_ref[0] == 0
    several, _, part, depth = own_ref.shape
    own, other = own_ref[:, 0], other_ref[:, 0]
    low = jnp.where(first, own, other)
    high = jnp.where(first, other, own)
    weight = jnp.concatenate([low, high], axis=1).reshape(several * 2 * part, depth)
    frozen = dot(grads_ref[...], weight, NT).astype(jnp.bfloat16)
    placed = dot(chosen_ref[...], back_ref[...], NN)
    out_ref[...] = (frozen.astype(jnp.float32) + placed).astype(jnp.bfloat16)


def whole():
    return pl.BlockSpec(memory_space=pltpu.VMEM)


def scalars():
    return pl.BlockSpec(memory_space=pltpu.SMEM)


def params():
    return pltpu.CompilerParams(vmem_limit_bytes=VMEM_LIMIT)


def on_device(
    inputs,
    output_gradient_rows,
    fixed_value_weight,
    task_down_adapters,
    task_up_adapters,
    live_row_counts,
    row_packing_order,
):
    per_device, features = inputs.shape
    kv_width = output_gradient_rows.shape[1]
    tasks = lax.axis_size("zl") * lax.axis_size("x")
    slot = per_device // tasks
    n_zh, n_y = lax.axis_size("zh"), lax.axis_size("y")
    blocks = n_zh * n_y
    part = fixed_value_weight.shape[0]
    down_t = task_down_adapters[0].T
    up = task_up_adapters[0]
    rank = up.shape[0]
    bf16, f32 = jnp.bfloat16, jnp.float32
    core = lax.axis_index("c").astype(jnp.int32).reshape(1)

    with jax.named_scope("pack"):
        packed = pl.pallas_call(
            pack_kernel,
            out_shape=jax.ShapeDtypeStruct((per_device, features + kv_width), bf16),
            in_specs=[scalars(), whole(), whole(), whole()],
            out_specs=whole(),
            compiler_params=params(),
        )(live_row_counts, row_packing_order, inputs, output_gradient_rows)
        recv = lax.all_to_all(packed.reshape(tasks, slot, features + kv_width), DP, 0, 0, tiled=True)
        recv = recv.reshape(per_device, features + kv_width)

    with jax.named_scope("frozen_gather"):
        along_z = lax.all_gather(fixed_value_weight, "zh", axis=0, tiled=True)
        own = lax.all_gather(along_z, "y", axis=0, tiled=True)

    with jax.named_scope("adapter_input_grad"):
        dx, proj = pl.pallas_call(
            input_grad_kernel,
            out_shape=(
                jax.ShapeDtypeStruct((per_device, features), bf16),
                jax.ShapeDtypeStruct((per_device, rank), bf16),
            ),
            grid=(1,),
            in_specs=[
                pl.BlockSpec((per_device, kv_width), lambda i: (0, features // kv_width)),
                pl.BlockSpec((rank, features), lambda i: (0, 0)),
                pl.BlockSpec((rank, kv_width), lambda i: (0, 0)),
            ],
            out_specs=(
                pl.BlockSpec((per_device, features), lambda i: (0, 0)),
                pl.BlockSpec((per_device, rank), lambda i: (0, 0)),
            ),
            compiler_params=params(),
        )(recv, down_t, up)
        back = lax.all_to_all(dx.reshape(tasks, slot, features), DP, 0, 0, tiled=True)
        back = back.reshape(per_device, features)

    with jax.named_scope("weight_grads"):
        quarter = features // (4 * blocks)
        few = kv_width // (2 * blocks)
        terms = jax.ShapeDtypeStruct((blocks, quarter + few, 2 * rank), f32)
        keep, send = pl.pallas_call(
            weight_grad_kernel,
            out_shape=(terms, terms),
            in_specs=[scalars(), whole(), whole(), whole()],
            out_specs=(whole(), whole()),
            compiler_params=params(),
        )(core, recv, down_t, proj)
        chip = (keep + lax.ppermute(send, "c", [(0, 1), (1, 0)])).astype(bf16)
        chip, own = lax.optimization_barrier((chip, own))
        other = lax.ppermute(own, "c", [(0, 1), (1, 0)])
        chip, back = lax.optimization_barrier((chip, back))
        shares = lax.all_to_all(chip, ("zh", "y"), 0, 0, tiled=True)
        share = jnp.sum(shares.astype(f32), axis=0)
        down_share = jnp.concatenate([share[:quarter, :rank], share[:quarter, rank:]], axis=0)
        up_share = share[quarter:, :rank].T

    with jax.named_scope("input_grad"):
        halves = 2
        several = n_y // halves
        wide = several * 2 * part
        order = (n_y, n_zh, part, kv_width)
        weight_spec = pl.BlockSpec((several, 1, part, kv_width), lambda i: (i % halves, i // halves, 0, 0))
        input_grad = pl.pallas_call(
            final_kernel,
            out_shape=jax.ShapeDtypeStruct((per_device, features), bf16),
            grid=(features // wide,),
            in_specs=[
                scalars(),
                scalars(),
                pl.BlockSpec((1, per_device), lambda i: (0, 0)),
                pl.BlockSpec((per_device, kv_width), lambda i: (0, 0)),
                weight_spec,
                weight_spec,
                pl.BlockSpec((per_device, wide), lambda i: (0, i)),
            ],
            out_specs=pl.BlockSpec((per_device, wide), lambda i: (0, i)),
            scratch_shapes=[pltpu.VMEM((per_device, per_device), bf16)],
            compiler_params=params(),
        )(
            core,
            live_row_counts,
            row_packing_order,
            output_gradient_rows,
            own.reshape(order),
            other.reshape(order),
            back,
        )
    return (input_grad, down_share[None], up_share[None])


def solution(mesh, parts=(4, 8, 2, 3, 4)):
    fine = Mesh(np.asarray(mesh.devices).reshape(parts), FSDP + DP)
    rows = P(FSDP + DP, None)
    in_specs = (
        rows,
        rows,
        P(FSDP, None),
        P(DP, None, None),
        P(DP, None, None),
        rows,
        rows,
    )
    out_specs = (rows, P(DP, FSDP, None), P(DP, None, FSDP))
    return jax.shard_map(on_device, mesh=fine, in_specs=in_specs, out_specs=out_specs, check_vma=False)
```

time: 914 us -> 158 us (0.17)
  waiting for transfers between devices: 828 us -> 38.7 us
  starting transfers between devices: 17.8 us -> 37.8 us
  blocking collectives: 25.5 us -> 43.2 us
  matrix products: 12.6 us -> 0 us
  Pallas kernels: 0 us -> 11.5 us
    unnamed x4 -> x1, waiting for transfers between devices: 565 us -> 0.02 us
    reduce_scatter x1 -> x0, waiting for transfers between devices: 158 us -> none  [on_device(): lax.psum_scatter(down_weight_gradient, 'fsdp', scatter_dimension=0, tiled...]
    all_gather x1, waiting for transfers between devices: 100 us -> 26.3 us  [on_device(): own = lax.all_gather(along_z, 'y', axis=0, tiled=True)]
    all_gather x0 -> x1, blocking collectives: none -> 43.2 us  [on_device(): along_z = lax.all_gather(fixed_value_weight, 'zh', axis=0, tiled=True)]
    all_to_all x1 -> x0, blocking collectives: 25.5 us -> none  [on_device(): lax.all_to_all(packed_rows, 'dp', split_axis=0, concat_axis=0, tiled=True)]
    all_to_all x2 -> x3, starting transfers between devices: 17.8 us -> 34 us  [the longest x1 13.2 us: on_device(): lax.all_to_all(packed.reshape(tasks, slot, features + kv_width), DP, 0, 0...]
    dot_general x5 -> x0, matrix products: 12.6 us -> none  [the longest x1 4.84 us: on_device(): lax.dot_general(output_gradient_rows, lax.all_gather(fixed_value_weight,...]
    pallas_call x0 -> x4, Pallas kernels: none -> 11.5 us  [the longest x1 7.04 us: on_device(): pl.pallas_call(final_kernel, out_shape=jax.ShapeDtypeStruct((per_device,...]
  transfers between devices with their start and end apart: 5 -> 6, of which waited for: 4 -> 3; matrix products, arithmetic and copies ran while one was open for 2% -> 1% of each run, Pallas kernels for 0% -> 6%
where the time goes in v1:
time: 158 us; the launch traced here: 156 us
  blocking collectives  43.2 us (27%)
  waiting for transfers between devices  38.7 us (24%)
  starting transfers between devices  37.8 us (24%)
  between operations  14.2 us (9%)
  Pallas kernels  11.5 us (7%)
  local copies, waits for them, and re-layouts  9.53 us (6%)
    all_gather x1, blocking collectives, on_device(): along_z = lax.all_gather(fixed_value_weight, 'zh', axis=0, tiled=True)  43.2 us
    all_gather x1, waiting for transfers between devices, on_device(): own = lax.all_gather(along_z, 'y', axis=0, tiled=True)  26.3 us
    all_to_all x1, starting transfers between devices, on_device(): lax.all_to_all(packed.reshape(tasks, slot, features + kv_width), DP, 0, 0...  13.2 us
    all_to_all x1, starting transfers between devices, on_device(): shares = lax.all_to_all(chip, ('zh', 'y'), 0, 0, tiled=True)  13 us
    all_to_all x1, waiting for transfers between devices, on_device(): shares = lax.all_to_all(chip, ('zh', 'y'), 0, 0, tiled=True)  10.3 us
    unnamed x30, local copies, waits for them, and re-layouts  8.86 us
    all_to_all x1, starting transfers between devices, on_device(): lax.all_to_all(dx.reshape(tasks, slot, features), DP, 0, 0, tiled=True)  7.74 us
    pallas_call x1, Pallas kernels, on_device(): pl.pallas_call(final_kernel, out_shape=jax.ShapeDtypeStruct((per_device,...  7.04 us
  transfers between devices with their start and end apart: 6, of which 3 were waited for; matrix products, arithmetic and copies ran while one was open for 1% of the time, Pallas kernels for 6%

profile of v1, /device:TPU:6, one launch (start us, length us, event | category | flops | bytes accessed | tf_op | source)
XLA Modules:
  0.0 156.4 jit_solution(2409468882572766226)
XLA Ops:
  7.2 0.0 copy-start.3
  7.2 1.4 copy-done.3
  8.6 0.0 copy-start.5
  8.6 0.9 copy-done.5
  9.5 0.0 copy-start.10
  9.5 0.7 copy-done.10
  10.2 0.0 copy-start.12
  10.2 0.7 copy-done.12
  10.8 2.4 %pack.1 = bf16[192,4608]{1,0:T(8,128)(2,1)} custom-call(s32[1,12]{1,0:T(1,128)S(1)} %copy-done.12, s32[1,192]{1,0:T(1,128)S(1)} %copy-done.10, bf16[192,4096]{1,0:T(8,128)(2,1)S(1)} %copy-done.3, bf16[192,512]{1,0:T(8,128)(2,1)S(1)} %copy-done.5), custom_call_target="tpu_custom_call" | custom-call | tf_op jit(solution)/shard_map/pack/pallas_call | solution.py:139
  13.2 0.0 copy-start.14
  13.2 0.0 copy-start
  13.2 0.0 copy-start.7
  13.2 13.2 %all-to-all-start = ((bf16[12,16,4608]{2,1,0:T(8,128)(2,1)}), bf16[12,16,4608]{2,1,0:T(8,128)(2,1)S(1)}, u32[]{:S(2)}, u32[]{:S(2)}) async-start(bf16[12,16,4608]{2,1,0:T(8,128)(2,1)} %bitcast.1), calls=%async_computation | async-start | bytes 3538944 | tf_op jit(solution)/shard_map/pack/all_to_all | solution.py:146
  26.4 0.0 all-gather.2.cloned.1.call-start
  26.4 0.0 copy-done.14
  26.5 43.2 %all_gather.6 = bf16[256,512]{1,0:T(8,128)(2,1)} all-gather(bf16[64,512]{1,0:T(8,128)(2,1)S(1)} %copy-done.14), channel_id=1, replica_groups=mesh['zh'=4,'y'=8,'c'=2,'zl'=3,'x'=4] {'zh'}, dimensions={0}, use_global_device_ids=true | all-gather | bytes 327680 | tf_op jit(solution)/shard_map/frozen_gather/all_gather | solution.py:150
  69.6 0.0 all-gather.2.cloned.1.call-update
  69.6 0.0 all-to-all-done
  69.7 0.0 copy-done
  69.7 0.0 copy-done.7
  69.7 0.8 adapter_input_grad.1
  70.5 0.0 copy-start.4
  70.5 1.1 copy-done.4
  71.6 0.0 copy-start.8
  71.6 0.6 copy-done.8
  72.2 7.7 %all-to-all-start.1 = ((bf16[12,16,4096]{2,1,0:T(8,128)(2,1)}), bf16[12,16,4096]{2,1,0:T(8,128)(2,1)S(1)}, u32[]{:S(2)}, u32[]{:S(2)}) async-start(bf16[12,16,4096]{2,1,0:T(8,128)(2,1)} %bitcast.23), calls=%async_computation.1 | async-start | bytes 3145728 | tf_op jit(solution)/shard_map/adapter_input_grad/all_to_all | solution.py:172
  80.0 0.0 copy-start.1
  80.0 1.0 copy-done.1
  81.0 0.0 copy-start.9
  81.0 0.8 copy-done.9
  81.8 0.0 copy-start.6
  81.8 0.0 copy-start.11
  81.8 0.0 copy-start.13
  81.8 1.3 weight_grads.1
  83.1 1.9 %collective-permute-start = (f32[32,40,128]{2,1,0:T(8,128)S(1)}, f32[32,40,128]{2,1,0:T(8,128)S(1)}, u32[]{:S(2)}, u32[]{:S(2)}) collective-permute-start(f32[32,40,128]{2,1,0:T(8,128)S(1)} %get-tuple-element.13), channel_id=1, source_target_pairs={{0,12},{12,0},{1,13},{13,1},{2,14},{14,2},{3,15},{15,3},{4,16},{16... | collective-permute-start | bytes 1966088 | tf_op jit(solution)/shard_map/weight_grads/ppermute | solution.py:186
  85.0 2.1 %collective-permute-done = f32[32,40,128]{2,1,0:T(8,128)S(1)} collective-permute-done((f32[32,40,128]{2,1,0:T(8,128)S(1)}, f32[32,40,128]{2,1,0:T(8,128)S(1)}, u32[]{:S(2)}, u32[]{:S(2)}) %collective-permute-start) | collective-permute-done | bytes 655392 | tf_op jit(solution)/shard_map/weight_grads/ppermute | solution.py:186
  87.1 0.8 add_convert_fusion
  87.9 26.3 %all-gather.2.cloned.1.call-done = bf16[2048,512]{1,0:T(8,128)(2,1)} async-done(((bf16[256,512]{1,0:T(8,128)(2,1)}), bf16[2048,512]{1,0:T(8,128)(2,1)}) %all-gather.2.cloned.1.call-update) | async-done | bytes 2097168 | tf_op jit(solution)/shard_map/frozen_gather/all_gather | solution.py:151
  114.2 1.9 %collective-permute-start.1 = (bf16[2048,512]{1,0:T(8,128)(2,1)}, bf16[2048,512]{1,0:T(8,128)(2,1)}, u32[]{:S(2)}, u32[]{:S(2)}) collective-permute-start(bf16[2048,512]{1,0:T(8,128)(2,1)} %all-gather.2.cloned.1.call-done), channel_id=1, source_target_pairs={{0,12},{12,0},{1,13},{13,1},{2,14},{14,2},{3,15},{15,3},{4,16},{16... | collective-permute-start | bytes 6291464 | tf_op jit(solution)/shard_map/weight_grads/ppermute | solution.py:188
  116.1 0.0 all-to-all-done.1
  116.1 13.0 %all-to-all-start.2 = ((bf16[32,40,128]{2,1,0:T(8,128)(2,1)}), bf16[32,40,128]{2,1,0:T(8,128)(2,1)S(1)}, u32[]{:S(2)}, u32[]{:S(2)}) async-start(bf16[32,40,128]{2,1,0:T(8,128)(2,1)} %add_convert_fusion), calls=%async_computation.2 | async-start | bytes 655360 | tf_op jit(solution)/shard_map/weight_grads/all_to_all | solution.py:190
  129.2 0.0 collective-permute-done.1
  129.2 0.0 copy-done.6
  129.2 0.0 copy-done.11
  129.2 0.0 copy-done.13
  129.2 0.0 copy-start.2
  129.2 1.6 %copy-done.2 = bf16[2048,512]{1,0:T(8,128)(2,1)S(1)} copy-done((bf16[2048,512]{1,0:T(8,128)(2,1)S(1)}, bf16[2048,512]{1,0:T(8,128)(2,1)}, u32[]{:S(2)}) %copy-start.2) | copy-done | bytes 2097176
  130.8 7.0 %input_grad.1 = bf16[192,4096]{1,0:T(8,128)(2,1)} custom-call(s32[1]{0:T(128)} %bitcast.core_ref, s32[1,12]{1,0:T(1,128)S(1)} %copy-done.13, s32[1,192]{1,0:T(1,128)S(1)} %copy-done.11, bf16[192,512]{1,0:T(8,128)(2,1)S(1)} %copy-done.6, bf16[8,4,64,512]{3,2,1,0:T(8,128)(2,1)S(1)} %bitcast.22, bf16[8,4,64,512]{3,2,1,0:T(8,128)(2,1)} %bitcast.8.other_ref, ...), custom_call_target="tpu_custom_call" | custom-call | tf_op jit(solution)/shard_map/input_grad/pallas_call | solution.py:201
  137.8 10.3 %all-to-all-done.2 = bf16[32,40,128]{2,1,0:T(8,128)(2,1)S(1)} async-done(((bf16[32,40,128]{2,1,0:T(8,128)(2,1)}), bf16[32,40,128]{2,1,0:T(8,128)(2,1)S(1)}, u32[]{:S(2)}, u32[]{:S(2)}) %all-to-all-start.2) | async-done | bytes 327712 | tf_op jit(solution)/shard_map/weight_grads/all_to_all | solution.py:190
  148.2 0.1 convert_reduce_fusion
  148.2 0.6 slice_bitcast_fusion
  148.8 0.1 fusion
  148.9 0.6 maximum_bitcast_fusion
Async XLA Ops:
  7.2 1.4 copy-start.3
  8.6 0.9 copy-start.5
  9.5 0.7 copy-start.10
  10.2 0.7 copy-start.12
  13.2 13.2 %copy-start.14 = (bf16[64,512]{1,0:T(8,128)(2,1)S(1)}, bf16[64,512]{1,0:T(8,128)(2,1)}, u32[]{:S(2)}) copy-start(bf16[64,512]{1,0:T(8,128)(2,1)} %param.9) | copy-start | bytes 196612
  13.2 56.4 %copy-start = (bf16[1,4096,64]{1,2,0:T(8,128)(2,1)S(1)}, bf16[1,4096,64]{1,2,0:T(8,128)(2,1)}, u32[]{:S(2)}) copy-start(bf16[1,4096,64]{1,2,0:T(8,128)(2,1)} %param.10) | copy-start | bytes 1572868
  13.2 56.4 %copy-start.7 = (bf16[1,64,512]{2,1,0:T(8,128)(2,1)S(1)}, bf16[1,64,512]{2,1,0:T(8,128)(2,1)}, u32[]{:S(2)}) copy-start(bf16[1,64,512]{2,1,0:T(8,128)(2,1)} %param.11) | copy-start | bytes 196612
  13.2 56.4 %all-to-all-start = ((bf16[12,16,4608]{2,1,0:T(8,128)(2,1)}), bf16[12,16,4608]{2,1,0:T(8,128)(2,1)S(1)}, u32[]{:S(2)}, u32[]{:S(2)}) async-start(bf16[12,16,4608]{2,1,0:T(8,128)(2,1)} %bitcast.1), calls=%async_computation | async-start | bytes 3538944 | tf_op jit(solution)/shard_map/pack/all_to_all | solution.py:146
  26.4 87.8 %all-gather.2.cloned.1.call-start = ((), (), s32[]{:S(2)}) async-start(), calls=%async_computation.3 | async-start | bytes 2359296 | tf_op jit(solution)/shard_map/frozen_gather/all_gather | solution.py:151
  70.5 1.1 copy-start.4
  71.6 0.6 copy-start.8
  72.2 43.9 %all-to-all-start.1 = ((bf16[12,16,4096]{2,1,0:T(8,128)(2,1)}), bf16[12,16,4096]{2,1,0:T(8,128)(2,1)S(1)}, u32[]{:S(2)}, u32[]{:S(2)}) async-start(bf16[12,16,4096]{2,1,0:T(8,128)(2,1)} %bitcast.23), calls=%async_computation.1 | async-start | bytes 3145728 | tf_op jit(solution)/shard_map/adapter_input_grad/all_to_all | solution.py:172
  80.0 1.0 copy-start.1
  81.0 0.8 copy-start.9
  81.8 47.4 %copy-start.6 = (bf16[192,512]{1,0:T(8,128)(2,1)S(1)}, bf16[192,512]{1,0:T(8,128)(2,1)}, u32[]{:S(2)}) copy-start(bf16[192,512]{1,0:T(8,128)(2,1)} %grads_ref.3) | copy-start | bytes 589828
  81.8 47.4 %copy-start.11 = (s32[1,192]{1,0:T(1,128)S(1)}, s32[1,192]{1,0:T(1,128)}, u32[]{:S(2)}) copy-start(s32[1,192]{1,0:T(1,128)} %packing_ref.3) | copy-start | bytes 2308
  81.8 47.4 %copy-start.13 = (s32[1,12]{1,0:T(1,128)S(1)}, s32[1,12]{1,0:T(1,128)}, u32[]{:S(2)}) copy-start(s32[1,12]{1,0:T(1,128)} %counts_ref.3) | copy-start | bytes 148
  83.1 4.0 %collective-permute-start = (f32[32,40,128]{2,1,0:T(8,128)S(1)}, f32[32,40,128]{2,1,0:T(8,128)S(1)}, u32[]{:S(2)}, u32[]{:S(2)}) collective-permute-start(f32[32,40,128]{2,1,0:T(8,128)S(1)} %get-tuple-element.13), channel_id=1, source_target_pairs={{0,12},{12,0},{1,13},{13,1},{2,14},{14,2},{3,15},{15,3},{4,16},{16... | collective-permute-start | bytes 1966088 | tf_op jit(solution)/shard_map/weight_grads/ppermute | solution.py:186
  114.2 15.0 %collective-permute-start.1 = (bf16[2048,512]{1,0:T(8,128)(2,1)}, bf16[2048,512]{1,0:T(8,128)(2,1)}, u32[]{:S(2)}, u32[]{:S(2)}) collective-permute-start(bf16[2048,512]{1,0:T(8,128)(2,1)} %all-gather.2.cloned.1.call-done), channel_id=1, source_target_pairs={{0,12},{12,0},{1,13},{13,1},{2,14},{14,2},{3,15},{15,3},{4,16},{16... | collective-permute-start | bytes 6291464 | tf_op jit(solution)/shard_map/weight_grads/ppermute | solution.py:188
  116.1 32.0 %all-to-all-start.2 = ((bf16[32,40,128]{2,1,0:T(8,128)(2,1)}), bf16[32,40,128]{2,1,0:T(8,128)(2,1)S(1)}, u32[]{:S(2)}, u32[]{:S(2)}) async-start(bf16[32,40,128]{2,1,0:T(8,128)(2,1)} %add_convert_fusion), calls=%async_computation.2 | async-start | bytes 655360 | tf_op jit(solution)/shard_map/weight_grads/all_to_all | solution.py:190
  129.2 1.6 %copy-start.2 = (bf16[2048,512]{1,0:T(8,128)(2,1)S(1)}, bf16[2048,512]{1,0:T(8,128)(2,1)}, u32[]{:S(2)}) copy-start(bf16[2048,512]{1,0:T(8,128)(2,1)} %all-gather.2.cloned.1.call-done) | copy-start | bytes 6291460
Sparse Core Ops, SparseCore 0:
  69.8 44.3 all-gather.1

commit v2 on v1

--- a/solution.py
+++ b/solution.py
@@ -11,7 +11,8 @@
 ADAPTER_SCALING = 2.0
 FSDP = ("zh", "y", "c")
 DP = ("zl", "x")
-VMEM_LIMIT = 48 * 1024 * 1024
+VMEM_LIMIT = 16 * 1024 * 1024
+WHOLE_VMEM = 60 * 1024 * 1024
 NT = (((1,), (1,)), ((), ()))
 NN = (((1,), (0,)), ((), ()))
 TN = (((0,), (0,)), ((), ()))
@@ -35,18 +36,37 @@
     return jnp.where(row == key, 1.0, 0.0).astype(jnp.bfloat16)
 
 
-def pack_kernel(counts_ref, packing_ref, rows_ref, grads_ref, out_ref):
-    chosen = live_one_hot(counts_ref, packing_ref)
-    features = rows_ref.shape[1]
-    step = 1024
-    for at in range(0, features, step):
-        out_ref[:, at : at + step] = dot(chosen, rows_ref[:, at : at + step], TN).astype(jnp.bfloat16)
-    out_ref[:, features:] = dot(chosen, grads_ref[...], TN).astype(jnp.bfloat16)
-
-
-def input_grad_kernel(grads_ref, down_t_ref, up_ref, dx_ref, proj_ref):
+def pack_kernel(counts_hbm, packing_hbm, rows_hbm, grads_hbm, out_hbm, counts, packing, held, packed, few_sems, in_sems, out_sems):
+    features = rows_hbm.shape[1]
+    width = grads_hbm.shape[1]
+    pieces = in_sems.shape[0]
+    step = features // (pieces - 1)
+    spans = [pl.ds(at * step, step) for at in range(pieces - 1)] + [pl.ds(features, width)]
+    small = (
+        pltpu.make_async_copy(counts_hbm, counts, few_sems.at[0]),
+        pltpu.make_async_copy(packing_hbm, packing, few_sems.at[1]),
+    )
+    loads = []
+    for at, span in enumerate(spans):
+        source = grads_hbm if at == pieces - 1 else rows_hbm.at[:, span]
+        loads.append(pltpu.make_async_copy(source, held.at[:, span], in_sems.at[at]))
+    for copy in (*small, *loads):
+        copy.start()
+    for copy in small:
+        copy.wait()
+    chosen = live_one_hot(counts, packing)
+    stores = []
+    for at, span in enumerate(spans):
+        loads[at].wait()
+        packed[:, span] = dot(chosen, held[:, span], TN).astype(jnp.bfloat16)
+        stores.append(pltpu.make_async_copy(packed.at[:, span], out_hbm.at[:, span], out_sems.at[at]))
+        stores[at].start()
+    for copy in stores:
+        copy.wait()
+
+
+def input_grad_kernel(grads_ref, down_t_ref, up_ref, dx_ref):
     proj = dot(grads_ref[...], up_ref[...], NT).astype(jnp.bfloat16)
-    proj_ref[...] = proj
     features = down_t_ref.shape[1]
     step = 1024
     for at in range(0, features, step):
@@ -54,14 +74,15 @@
         dx_ref[:, at : at + step] = dx.astype(jnp.bfloat16)
 
 
-def weight_grad_kernel(core_ref, recv_ref, down_t_ref, proj_ref, keep_ref, send_ref):
+def weight_grad_kernel(core_ref, recv_ref, down_t_ref, up_ref, keep_ref, send_ref):
     rank, features = down_t_ref.shape
     blocks = keep_ref.shape[0]
     first = core_ref[0] == 0
     wide = features // blocks
     half = wide // 2
     quarter = half // 2
-    proj = proj_ref[...]
+    grads = recv_ref[:, features:]
+    proj = dot(grads, up_ref[...], NT).astype(jnp.bfloat16)
     total = jnp.zeros((recv_ref.shape[0], rank), jnp.float32)
     step = 1024
     for at in range(0, features, step):
@@ -75,7 +96,6 @@
                 pair.append(jnp.concatenate([down[lo : lo + quarter], down[lo + quarter : lo + half]], axis=1))
             keep_ref[at // wide + b, :quarter, :] = jnp.where(first, pair[0], pair[1])
             send_ref[at // wide + b, :quarter, :] = jnp.where(first, pair[1], pair[0])
-    grads = recv_ref[:, features:]
     up_t = ADAPTER_SCALING * dot(grads, total.astype(jnp.bfloat16), TN)
     up_t = jnp.concatenate([up_t, jnp.zeros_like(up_t)], axis=1)
     few = grads.shape[1] // (2 * blocks)
@@ -85,12 +105,12 @@
         send_ref[b, quarter:, :] = jnp.where(first, high, low)
 
 
-def final_kernel(core_ref, counts_ref, packing_ref, grads_ref, own_ref, other_ref, back_ref, out_ref, chosen_ref):
+def final_kernel(place_ref, counts_ref, packing_ref, grads_ref, own_ref, other_ref, back_ref, out_ref, chosen_ref):
     @pl.when(pl.program_id(0) == 0)
     def _():
         chosen_ref[...] = live_one_hot(counts_ref, packing_ref)
 
-    first = core_ref[0] == 0
+    first = place_ref[0] == 0
     several, _, part, depth = own_ref.shape
     own, other = own_ref[:, 0], other_ref[:, 0]
     low = jnp.where(first, own, other)
@@ -101,16 +121,20 @@
     out_ref[...] = (frozen.astype(jnp.float32) + placed).astype(jnp.bfloat16)
 
 
-def whole():
-    return pl.BlockSpec(memory_space=pltpu.VMEM)
+def one(*shape):
+    return pl.BlockSpec(shape, lambda i: (0,) * len(shape))
+
+
+def hbm():
+    return pl.BlockSpec(memory_space=pltpu.HBM)
 
 
 def scalars():
     return pl.BlockSpec(memory_space=pltpu.SMEM)
 
 
-def params():
-    return pltpu.CompilerParams(vmem_limit_bytes=VMEM_LIMIT)
+def params(limit=VMEM_LIMIT):
+    return pltpu.CompilerParams(vmem_limit_bytes=limit)
 
 
 def on_device(
@@ -135,38 +159,44 @@
     bf16, f32 = jnp.bfloat16, jnp.float32
     core = lax.axis_index("c").astype(jnp.int32).reshape(1)
 
+    with jax.named_scope("frozen_gather"):
+        along_z = [fixed_value_weight]
+        for shift in range(1, n_zh):
+            along_z.append(lax.ppermute(fixed_value_weight, "zh", [(i, (i + shift) % n_zh) for i in range(n_zh)]))
+
     with jax.named_scope("pack"):
         packed = pl.pallas_call(
             pack_kernel,
             out_shape=jax.ShapeDtypeStruct((per_device, features + kv_width), bf16),
-            in_specs=[scalars(), whole(), whole(), whole()],
-            out_specs=whole(),
-            compiler_params=params(),
+            in_specs=[hbm(), hbm(), hbm(), hbm()],
+            out_specs=hbm(),
+            scratch_shapes=[
+                pltpu.SMEM((1, tasks), jnp.int32),
+                pltpu.VMEM((1, per_device), jnp.int32),
+                pltpu.VMEM((per_device, features + kv_width), bf16),
+                pltpu.VMEM((per_device, features + kv_width), bf16),
+                pltpu.SemaphoreType.DMA((2,)),
+                pltpu.SemaphoreType.DMA((5,)),
+                pltpu.SemaphoreType.DMA((5,)),
+            ],
+            compiler_params=params(WHOLE_VMEM),
         )(live_row_counts, row_packing_order, inputs, output_gradient_rows)
+        packed, *along_z = lax.optimization_barrier((packed, *along_z))
         recv = lax.all_to_all(packed.reshape(tasks, slot, features + kv_width), DP, 0, 0, tiled=True)
         recv = recv.reshape(per_device, features + kv_width)
-
-    with jax.named_scope("frozen_gather"):
-        along_z = lax.all_gather(fixed_value_weight, "zh", axis=0, tiled=True)
-        own = lax.all_gather(along_z, "y", axis=0, tiled=True)
+        own = lax.all_gather(jnp.concatenate(along_z, axis=0), "y", axis=0, tiled=True)
 
     with jax.named_scope("adapter_input_grad"):
-        dx, proj = pl.pallas_call(
+        dx = pl.pallas_call(
             input_grad_kernel,
-            out_shape=(
-                jax.ShapeDtypeStruct((per_device, features), bf16),
-                jax.ShapeDtypeStruct((per_device, rank), bf16),
-            ),
+            out_shape=jax.ShapeDtypeStruct((per_device, features), bf16),
             grid=(1,),
             in_specs=[
                 pl.BlockSpec((per_device, kv_width), lambda i: (0, features // kv_width)),
-                pl.BlockSpec((rank, features), lambda i: (0, 0)),
-                pl.BlockSpec((rank, kv_width), lambda i: (0, 0)),
+                one(rank, features),
+                one(rank, kv_width),
             ],
-            out_specs=(
-                pl.BlockSpec((per_device, features), lambda i: (0, 0)),
-                pl.BlockSpec((per_device, rank), lambda i: (0, 0)),
-            ),
+            out_specs=one(per_device, features),
             compiler_params=params(),
         )(recv, down_t, up)
         back = lax.all_to_all(dx.reshape(tasks, slot, features), DP, 0, 0, tiled=True)
@@ -179,10 +209,11 @@
         keep, send = pl.pallas_call(
             weight_grad_kernel,
             out_shape=(terms, terms),
-            in_specs=[scalars(), whole(), whole(), whole()],
-            out_specs=(whole(), whole()),
+            grid=(1,),
+            in_specs=[scalars(), one(per_device, features + kv_width), one(rank, features), one(rank, kv_width)],
+            out_specs=(one(*terms.shape), one(*terms.shape)),
             compiler_params=params(),
-        )(core, recv, down_t, proj)
+        )(core, recv, down_t, up)
         chip = (keep + lax.ppermute(send, "c", [(0, 1), (1, 0)])).astype(bf16)
         chip, own = lax.optimization_barrier((chip, own))
         other = lax.ppermute(own, "c", [(0, 1), (1, 0)])
@@ -197,25 +228,36 @@
         several = n_y // halves
         wide = several * 2 * part
         order = (n_y, n_zh, part, kv_width)
-        weight_spec = pl.BlockSpec((several, 1, part, kv_width), lambda i: (i % halves, i // halves, 0, 0))
+
+        def block(*shape):
+            return pl.BlockSpec(shape, lambda i, place: (0,) * len(shape))
+
+        def weight_at(i, place):
+            return i % halves, lax.rem(place[1] - i // halves + n_zh, n_zh), 0, 0
+
+        weight_spec = pl.BlockSpec((several, 1, part, kv_width), weight_at)
+        rows_spec = pl.BlockSpec((per_device, wide), lambda i, place: (0, i))
+        place = jnp.stack([core[0], lax.axis_index("zh").astype(jnp.int32)])
         input_grad = pl.pallas_call(
             final_kernel,
             out_shape=jax.ShapeDtypeStruct((per_device, features), bf16),
-            grid=(features // wide,),
-            in_specs=[
-                scalars(),
-                scalars(),
-                pl.BlockSpec((1, per_device), lambda i: (0, 0)),
-                pl.BlockSpec((per_device, kv_width), lambda i: (0, 0)),
-                weight_spec,
-                weight_spec,
-                pl.BlockSpec((per_device, wide), lambda i: (0, i)),
-            ],
-            out_specs=pl.BlockSpec((per_device, wide), lambda i: (0, i)),
-            scratch_shapes=[pltpu.VMEM((per_device, per_device), bf16)],
+            grid_spec=pltpu.PrefetchScalarGridSpec(
+                num_scalar_prefetch=1,
+                grid=(features // wide,),
+                in_specs=[
+                    scalars(),
+                    block(1, per_device),
+                    block(per_device, kv_width),
+                    weight_spec,
+                    weight_spec,
+                    rows_spec,
+                ],
+                out_specs=rows_spec,
+                scratch_shapes=[pltpu.VMEM((per_device, per_device), bf16)],
+            ),
             compiler_params=params(),
         )(
-            core,
+            place,
             live_row_counts,
             row_packing_order,
             output_gradient_rows,

time: 158 us -> 146 us (0.924)
  blocking collectives: 43.2 us -> 0 us
  starting transfers between devices: 37.8 us -> 55.6 us
  waiting for transfers between devices: 38.7 us -> 53.9 us
  local copies, waits for them, and re-layouts: 9.53 us -> 5.3 us
  Pallas kernels: 11.5 us -> 13.3 us
    all_gather x1 -> x0, blocking collectives: 43.2 us -> none  [on_device(): along_z = lax.all_gather(fixed_value_weight, 'zh', axis=0, tiled=True)]
    all_to_all x1, waiting for transfers between devices: 0.01 us -> 26.1 us  [on_device(): lax.all_to_all(packed.reshape(tasks, slot, features + kv_width), DP, 0, 0...]
    ppermute x0 -> x3, starting transfers between devices: none -> 24 us  [on_device(): lax.ppermute(fixed_value_weight, 'zh', [(i, (i + shift) % n_zh) for i in...]
    all_gather x1, waiting for transfers between devices: 26.3 us -> 3.48 us  [on_device(): lax.all_gather(jnp.concatenate(along_z, axis=0), 'y', axis=0, tiled=True)]
    all_to_all x1, waiting for transfers between devices: 0.01 us -> 12 us  [on_device(): lax.all_to_all(dx.reshape(tasks, slot, features), DP, 0, 0, tiled=True)]
    all_to_all x1, starting transfers between devices: 13.2 us -> 8.65 us  [on_device(): lax.all_to_all(packed.reshape(tasks, slot, features + kv_width), DP, 0, 0...]
    unnamed x30 -> x20, local copies, waits for them, and re-layouts: 8.86 us -> 4.63 us
    all_to_all x1, starting transfers between devices: 7.74 us -> 5.36 us  [on_device(): lax.all_to_all(dx.reshape(tasks, slot, features), DP, 0, 0, tiled=True)]
  transfers between devices with their start and end apart: 6 -> 9, of which waited for: 3 -> 6; matrix products, arithmetic and copies ran while one was open for 1% -> 1% of each run, Pallas kernels for 6% -> 9%
where the time goes in v2:
time: 146 us; the launch traced here: 144 us
  starting transfers between devices  55.6 us (38%)
  waiting for transfers between devices  53.9 us (37%)
  between operations  14.1 us (10%)
  Pallas kernels  13.3 us (9%)
  local copies, waits for them, and re-layouts  5.3 us (4%)
  other arithmetic  2.27 us (2%)
    all_to_all x1, waiting for transfers between devices, on_device(): lax.all_to_all(packed.reshape(tasks, slot, features + kv_width), DP, 0, 0...  26.1 us
    ppermute x3, starting transfers between devices, on_device(): lax.ppermute(fixed_value_weight, 'zh', [(i, (i + shift) % n_zh) for i in...  24 us
    all_to_all x1, starting transfers between devices, on_device(): shares = lax.all_to_all(chip, ('zh', 'y'), 0, 0, tiled=True)  13.7 us
    all_to_all x1, waiting for transfers between devices, on_device(): lax.all_to_all(dx.reshape(tasks, slot, features), DP, 0, 0, tiled=True)  12 us
    all_to_all x1, waiting for transfers between devices, on_device(): shares = lax.all_to_all(chip, ('zh', 'y'), 0, 0, tiled=True)  8.84 us
    all_to_all x1, starting transfers between devices, on_device(): lax.all_to_all(packed.reshape(tasks, slot, features + kv_width), DP, 0, 0...  8.65 us
    pallas_call x1, Pallas kernels, on_device(): pl.pallas_call(final_kernel, out_shape=jax.ShapeDtypeStruct((per_device,...  7.63 us
    all_to_all x1, starting transfers between devices, on_device(): lax.all_to_all(dx.reshape(tasks, slot, features), DP, 0, 0, tiled=True)  5.36 us
  transfers between devices with their start and end apart: 9, of which 6 were waited for; matrix products, arithmetic and copies ran while one was open for 1% of the time, Pallas kernels for 9%

profile of v2, /device:TPU:6, one launch (start us, length us, event | category | flops | bytes accessed | tf_op | source)
XLA Modules:
  0.0 144.4 jit_solution(7967807156528277693)
XLA Ops:
  7.2 15.1 %collective-permute-start.1 = (bf16[64,512]{1,0:T(8,128)(2,1)}, bf16[64,512]{1,0:T(8,128)(2,1)S(1)}, u32[]{:S(2)}, u32[]{:S(2)}) collective-permute-start(bf16[64,512]{1,0:T(8,128)(2,1)} %param.9), channel_id=1, source_target_pairs={{0,384},{192,576},{384,0},{576,192},{1,385},{193,577},{385,1},{577... | collective-permute-start | bytes 196616 | tf_op jit(solution)/shard_map/frozen_gather/ppermute | solution.py:165
  22.3 5.2 %collective-permute-start = (bf16[64,512]{1,0:T(8,128)(2,1)}, bf16[64,512]{1,0:T(8,128)(2,1)S(1)}, u32[]{:S(2)}, u32[]{:S(2)}) collective-permute-start(bf16[64,512]{1,0:T(8,128)(2,1)} %param.9), channel_id=1, source_target_pairs={{0,192},{192,384},{384,576},{576,0},{1,193},{193,385},{385,577},{5... | collective-permute-start | bytes 196616 | tf_op jit(solution)/shard_map/frozen_gather/ppermute | solution.py:165
  27.5 3.7 %collective-permute-start.2 = (bf16[64,512]{1,0:T(8,128)(2,1)}, bf16[64,512]{1,0:T(8,128)(2,1)S(1)}, u32[]{:S(2)}, u32[]{:S(2)}) collective-permute-start(bf16[64,512]{1,0:T(8,128)(2,1)} %param.9), channel_id=1, source_target_pairs={{0,576},{192,0},{384,192},{576,384},{1,577},{193,1},{385,193},{577... | collective-permute-start | bytes 196616 | tf_op jit(solution)/shard_map/frozen_gather/ppermute | solution.py:165
  31.2 3.3 %pack.1 = bf16[192,4608]{1,0:T(8,128)(2,1)} custom-call(s32[1,12]{1,0:T(1,128)} %counts_ref.1, s32[1,192]{1,0:T(1,128)} %packing_ref.1, bf16[192,4096]{1,0:T(8,128)(2,1)} %rows_hbm.1, bf16[192,512]{1,0:T(8,128)(2,1)} %grads_ref.1), custom_call_target="tpu_custom_call" | custom-call | tf_op jit(solution)/shard_map/pack/pallas_call | solution.py:168
  34.5 0.0 collective-permute-done.1
  34.5 0.0 collective-permute-done
  34.5 1.3 collective-permute-done.2
  35.8 0.0 copy-start.9
  35.8 0.0 copy-start.1
  35.8 0.0 copy-start.5
  35.8 8.6 %all-to-all-start = ((bf16[12,16,4608]{2,1,0:T(8,128)(2,1)}), bf16[12,16,4608]{2,1,0:T(8,128)(2,1)S(1)}, u32[]{:S(2)}, u32[]{:S(2)}) async-start(bf16[12,16,4608]{2,1,0:T(8,128)(2,1)} %bitcast.27), calls=%async_computation | async-start | bytes 3538944 | tf_op jit(solution)/shard_map/pack/all_to_all | solution.py:185
  44.5 0.0 all-gather.2.cloned.1.call-start
  44.5 0.0 copy-done.9
  44.5 0.7 pad_maximum_fusion
  45.2 0.0 all-gather.2.cloned.1.call-update
  45.2 26.1 %all-to-all-done = bf16[12,16,4608]{2,1,0:T(8,128)(2,1)S(1)} async-done(((bf16[12,16,4608]{2,1,0:T(8,128)(2,1)}), bf16[12,16,4608]{2,1,0:T(8,128)(2,1)S(1)}, u32[]{:S(2)}, u32[]{:S(2)}) %all-to-all-start) | async-done | bytes 1769504 | tf_op jit(solution)/shard_map/pack/all_to_all | solution.py:185
  71.3 0.0 copy-done.1
  71.3 0.0 copy-done.5
  71.3 0.8 adapter_input_grad.1
  72.1 0.0 copy-start
  72.1 1.1 copy-done
  73.3 5.4 %all-to-all-start.1 = ((bf16[12,16,4096]{2,1,0:T(8,128)(2,1)}), bf16[12,16,4096]{2,1,0:T(8,128)(2,1)S(1)}, u32[]{:S(2)}, u32[]{:S(2)}) async-start(bf16[12,16,4096]{2,1,0:T(8,128)(2,1)} %bitcast.21), calls=%async_computation.1 | async-start | bytes 3145728 | tf_op jit(solution)/shard_map/adapter_input_grad/all_to_all | solution.py:202
  78.6 0.0 copy-start.2
  78.6 1.0 copy-done.2
  79.7 0.0 copy-start.6
  79.7 0.8 copy-done.6
  80.5 0.0 copy-start.4
  80.5 0.0 copy-start.7
  80.5 0.0 copy-start.8
  80.5 1.6 %weight_grads.1 = (f32[32,40,128]{2,1,0:T(8,128)S(1)}, f32[32,40,128]{2,1,0:T(8,128)S(1)}) custom-call(s32[1]{0:T(128)} %bitcast.core_ref, bf16[192,4608]{1,0:T(8,128)(2,1)S(1)} %bitcast.19, bf16[64,4096]{1,0:T(8,128)(2,1)S(1)} %bitcast.23, bf16[64,512]{1,0:T(8,128)(2,1)S(1)} %bitcast.26), custom_call_target="tpu_custom_call" | custom-call | tf_op jit(solution)/shard_map/weight_grads/pallas_call | solution.py:209
  82.1 1.9 %collective-permute-start.3 = (f32[32,40,128]{2,1,0:T(8,128)S(1)}, f32[32,40,128]{2,1,0:T(8,128)S(1)}, u32[]{:S(2)}, u32[]{:S(2)}) collective-permute-start(f32[32,40,128]{2,1,0:T(8,128)S(1)} %get-tuple-element.16), channel_id=1, source_target_pairs={{0,12},{12,0},{1,13},{13,1},{2,14},{14,2},{3,15},{15,3},{4,16},{16... | collective-permute-start | bytes 1966088 | tf_op jit(solution)/shard_map/weight_grads/ppermute | solution.py:217
  84.0 2.1 %collective-permute-done.3 = f32[32,40,128]{2,1,0:T(8,128)S(1)} collective-permute-done((f32[32,40,128]{2,1,0:T(8,128)S(1)}, f32[32,40,128]{2,1,0:T(8,128)S(1)}, u32[]{:S(2)}, u32[]{:S(2)}) %collective-permute-start.3) | collective-permute-done | bytes 655392 | tf_op jit(solution)/shard_map/weight_grads/ppermute | solution.py:217
  86.1 0.8 add_convert_fusion
  86.9 3.5 %all-gather.2.cloned.1.call-done = bf16[2048,512]{1,0:T(8,128)(2,1)} async-done(((bf16[256,512]{1,0:T(8,128)(2,1)}), bf16[2048,512]{1,0:T(8,128)(2,1)}) %all-gather.2.cloned.1.call-update) | async-done | bytes 2097168 | tf_op jit(solution)/shard_map/pack/all_gather | solution.py:187
  90.3 1.9 %collective-permute-start.4 = (bf16[2048,512]{1,0:T(8,128)(2,1)}, bf16[2048,512]{1,0:T(8,128)(2,1)}, u32[]{:S(2)}, u32[]{:S(2)}) collective-permute-start(bf16[2048,512]{1,0:T(8,128)(2,1)} %all-gather.2.cloned.1.call-done), channel_id=1, source_target_pairs={{0,12},{12,0},{1,13},{13,1},{2,14},{14,2},{3,15},{15,3},{4,16},{16... | collective-permute-start | bytes 6291464 | tf_op jit(solution)/shard_map/weight_grads/ppermute | solution.py:219
  92.3 12.0 %all-to-all-done.1 = bf16[12,16,4096]{2,1,0:T(8,128)(2,1)S(1)} async-done(((bf16[12,16,4096]{2,1,0:T(8,128)(2,1)}), bf16[12,16,4096]{2,1,0:T(8,128)(2,1)S(1)}, u32[]{:S(2)}, u32[]{:S(2)}) %all-to-all-start.1) | async-done | bytes 1572896 | tf_op jit(solution)/shard_map/adapter_input_grad/all_to_all | solution.py:202
  104.3 13.7 %all-to-all-start.2 = ((bf16[32,40,128]{2,1,0:T(8,128)(2,1)}), bf16[32,40,128]{2,1,0:T(8,128)(2,1)S(1)}, u32[]{:S(2)}, u32[]{:S(2)}) async-start(bf16[32,40,128]{2,1,0:T(8,128)(2,1)} %add_convert_fusion), calls=%async_computation.2 | async-start | bytes 655360 | tf_op jit(solution)/shard_map/weight_grads/all_to_all | solution.py:221
  118.1 0.1 pad_add_fusion.place_ref
  118.1 0.0 collective-permute-done.4
  118.1 0.0 copy-done.4
  118.1 0.0 copy-done.7
  118.1 0.0 copy-done.8
  118.2 0.0 copy-start.3
  118.2 1.6 %copy-done.3 = bf16[2048,512]{1,0:T(8,128)(2,1)S(1)} copy-done((bf16[2048,512]{1,0:T(8,128)(2,1)S(1)}, bf16[2048,512]{1,0:T(8,128)(2,1)}, u32[]{:S(2)}) %copy-start.3) | copy-done | bytes 2097176
  119.7 7.6 %input_grad.1 = bf16[192,4096]{1,0:T(8,128)(2,1)} custom-call(s32[2]{0:T(128)S(1)} %pad_add_fusion.place_ref, s32[1,12]{1,0:T(1,128)S(1)} %copy-done.8, s32[1,192]{1,0:T(1,128)S(1)} %copy-done.7, bf16[192,512]{1,0:T(8,128)(2,1)S(1)} %copy-done.4, bf16[8,4,64,512]{3,2,1,0:T(8,128)(2,1)S(1)} %bitcast.24, bf16[8,4,64,512]{3,2,1,0:T(8,128)(2,1)} %bitcast.8.other_ref, ...), custom_call_target="tpu_custom_call" | custom-call | tf_op jit(solution)/shard_map/input_grad/pallas_call | solution.py:241
  127.4 8.8 %all-to-all-done.2 = bf16[32,40,128]{2,1,0:T(8,128)(2,1)S(1)} async-done(((bf16[32,40,128]{2,1,0:T(8,128)(2,1)}), bf16[32,40,128]{2,1,0:T(8,128)(2,1)S(1)}, u32[]{:S(2)}, u32[]{:S(2)}) %all-to-all-start.2) | async-done | bytes 327712 | tf_op jit(solution)/shard_map/weight_grads/all_to_all | solution.py:221
  136.2 0.1 convert_reduce_fusion
  136.3 0.6 slice_bitcast_fusion
  136.9 0.1 fusion
  136.9 0.6 maximum_bitcast_fusion
Async XLA Ops:
  7.2 27.3 %collective-permute-start.1 = (bf16[64,512]{1,0:T(8,128)(2,1)}, bf16[64,512]{1,0:T(8,128)(2,1)S(1)}, u32[]{:S(2)}, u32[]{:S(2)}) collective-permute-start(bf16[64,512]{1,0:T(8,128)(2,1)} %param.9), channel_id=1, source_target_pairs={{0,384},{192,576},{384,0},{576,192},{1,385},{193,577},{385,1},{577... | collective-permute-start | bytes 196616 | tf_op jit(solution)/shard_map/frozen_gather/ppermute | solution.py:165
  22.3 12.2 %collective-permute-start = (bf16[64,512]{1,0:T(8,128)(2,1)}, bf16[64,512]{1,0:T(8,128)(2,1)S(1)}, u32[]{:S(2)}, u32[]{:S(2)}) collective-permute-start(bf16[64,512]{1,0:T(8,128)(2,1)} %param.9), channel_id=1, source_target_pairs={{0,192},{192,384},{384,576},{576,0},{1,193},{193,385},{385,577},{5... | collective-permute-start | bytes 196616 | tf_op jit(solution)/shard_map/frozen_gather/ppermute | solution.py:165
  27.5 8.3 %collective-permute-start.2 = (bf16[64,512]{1,0:T(8,128)(2,1)}, bf16[64,512]{1,0:T(8,128)(2,1)S(1)}, u32[]{:S(2)}, u32[]{:S(2)}) collective-permute-start(bf16[64,512]{1,0:T(8,128)(2,1)} %param.9), channel_id=1, source_target_pairs={{0,576},{192,0},{384,192},{576,384},{1,577},{193,1},{385,193},{577... | collective-permute-start | bytes 196616 | tf_op jit(solution)/shard_map/frozen_gather/ppermute | solution.py:165
  35.8 8.7 %copy-start.9 = (bf16[64,512]{1,0:T(8,128)(2,1)S(1)}, bf16[64,512]{1,0:T(8,128)(2,1)}, u32[]{:S(2)}) copy-start(bf16[64,512]{1,0:T(8,128)(2,1)} %param.9) | copy-start | bytes 196612
  35.8 35.5 %copy-start.1 = (bf16[1,4096,64]{1,2,0:T(8,128)(2,1)S(1)}, bf16[1,4096,64]{1,2,0:T(8,128)(2,1)}, u32[]{:S(2)}) copy-start(bf16[1,4096,64]{1,2,0:T(8,128)(2,1)} %param.10) | copy-start | bytes 1572868
  35.8 35.5 %copy-start.5 = (bf16[1,64,512]{2,1,0:T(8,128)(2,1)S(1)}, bf16[1,64,512]{2,1,0:T(8,128)(2,1)}, u32[]{:S(2)}) copy-start(bf16[1,64,512]{2,1,0:T(8,128)(2,1)} %param.11) | copy-start | bytes 196612
  35.8 35.5 %all-to-all-start = ((bf16[12,16,4608]{2,1,0:T(8,128)(2,1)}), bf16[12,16,4608]{2,1,0:T(8,128)(2,1)S(1)}, u32[]{:S(2)}, u32[]{:S(2)}) async-start(bf16[12,16,4608]{2,1,0:T(8,128)(2,1)} %bitcast.27), calls=%async_computation | async-start | bytes 3538944 | tf_op jit(solution)/shard_map/pack/all_to_all | solution.py:185
  44.5 45.9 %all-gather.2.cloned.1.call-start = ((), (), s32[]{:S(2)}) async-start(), calls=%async_computation.3 | async-start | bytes 2359296 | tf_op jit(solution)/shard_map/pack/all_gather | solution.py:187
  72.1 1.1 copy-start
  73.3 31.0 %all-to-all-start.1 = ((bf16[12,16,4096]{2,1,0:T(8,128)(2,1)}), bf16[12,16,4096]{2,1,0:T(8,128)(2,1)S(1)}, u32[]{:S(2)}, u32[]{:S(2)}) async-start(bf16[12,16,4096]{2,1,0:T(8,128)(2,1)} %bitcast.21), calls=%async_computation.1 | async-start | bytes 3145728 | tf_op jit(solution)/shard_map/adapter_input_grad/all_to_all | solution.py:202
  78.6 1.1 copy-start.2
  79.7 0.8 copy-start.6
  80.5 37.6 %copy-start.4 = (bf16[192,512]{1,0:T(8,128)(2,1)S(1)}, bf16[192,512]{1,0:T(8,128)(2,1)}, u32[]{:S(2)}) copy-start(bf16[192,512]{1,0:T(8,128)(2,1)} %grads_ref.1) | copy-start | bytes 589828
  80.5 37.6 %copy-start.7 = (s32[1,192]{1,0:T(1,128)S(1)}, s32[1,192]{1,0:T(1,128)}, u32[]{:S(2)}) copy-start(s32[1,192]{1,0:T(1,128)} %packing_ref.1) | copy-start | bytes 2308
  80.5 37.6 %copy-start.8 = (s32[1,12]{1,0:T(1,128)S(1)}, s32[1,12]{1,0:T(1,128)}, u32[]{:S(2)}) copy-start(s32[1,12]{1,0:T(1,128)} %counts_ref.1) | copy-start | bytes 148
  82.1 4.0 %collective-permute-start.3 = (f32[32,40,128]{2,1,0:T(8,128)S(1)}, f32[32,40,128]{2,1,0:T(8,128)S(1)}, u32[]{:S(2)}, u32[]{:S(2)}) collective-permute-start(f32[32,40,128]{2,1,0:T(8,128)S(1)} %get-tuple-element.16), channel_id=1, source_target_pairs={{0,12},{12,0},{1,13},{13,1},{2,14},{14,2},{3,15},{15,3},{4,16},{16... | collective-permute-start | bytes 1966088 | tf_op jit(solution)/shard_map/weight_grads/ppermute | solution.py:217
  90.3 27.8 %collective-permute-start.4 = (bf16[2048,512]{1,0:T(8,128)(2,1)}, bf16[2048,512]{1,0:T(8,128)(2,1)}, u32[]{:S(2)}, u32[]{:S(2)}) collective-permute-start(bf16[2048,512]{1,0:T(8,128)(2,1)} %all-gather.2.cloned.1.call-done), channel_id=1, source_target_pairs={{0,12},{12,0},{1,13},{13,1},{2,14},{14,2},{3,15},{15,3},{4,16},{16... | collective-permute-start | bytes 6291464 | tf_op jit(solution)/shard_map/weight_grads/ppermute | solution.py:219
  104.3 31.9 %all-to-all-start.2 = ((bf16[32,40,128]{2,1,0:T(8,128)(2,1)}), bf16[32,40,128]{2,1,0:T(8,128)(2,1)S(1)}, u32[]{:S(2)}, u32[]{:S(2)}) async-start(bf16[32,40,128]{2,1,0:T(8,128)(2,1)} %add_convert_fusion), calls=%async_computation.2 | async-start | bytes 655360 | tf_op jit(solution)/shard_map/weight_grads/all_to_all | solution.py:221
  118.2 1.6 %copy-start.3 = (bf16[2048,512]{1,0:T(8,128)(2,1)S(1)}, bf16[2048,512]{1,0:T(8,128)(2,1)}, u32[]{:S(2)}) copy-start(bf16[2048,512]{1,0:T(8,128)(2,1)} %all-gather.2.cloned.1.call-done) | copy-start | bytes 6291460
Sparse Core Ops, SparseCore 0:
  47.6 42.6 all-gather.1

commit v3 on v2

--- a/solution.py
+++ b/solution.py
@@ -65,19 +65,11 @@
         copy.wait()
 
 
-def input_grad_kernel(grads_ref, down_t_ref, up_ref, dx_ref):
-    proj = dot(grads_ref[...], up_ref[...], NT).astype(jnp.bfloat16)
-    features = down_t_ref.shape[1]
-    step = 1024
-    for at in range(0, features, step):
-        dx = ADAPTER_SCALING * dot(proj, down_t_ref[:, at : at + step], NN)
-        dx_ref[:, at : at + step] = dx.astype(jnp.bfloat16)
-
-
-def weight_grad_kernel(core_ref, recv_ref, down_t_ref, up_ref, keep_ref, send_ref):
+def adapter_kernel(place_ref, recv_ref, down_t_ref, up_ref, dx_ref, keep_ref, send_ref):
     rank, features = down_t_ref.shape
-    blocks = keep_ref.shape[0]
-    first = core_ref[0] == 0
+    n_y, n_zh = keep_ref.shape[:2]
+    blocks = n_y * n_zh
+    first = place_ref[0] == 0
     wide = features // blocks
     half = wide // 2
     quarter = half // 2
@@ -85,24 +77,52 @@
     proj = dot(grads, up_ref[...], NT).astype(jnp.bfloat16)
     total = jnp.zeros((recv_ref.shape[0], rank), jnp.float32)
     step = 1024
+    turn = [lax.rem(y - place_ref[1] + n_y, n_y) for y in range(n_y)]
     for at in range(0, features, step):
         rows = recv_ref[:, at : at + step]
-        total = total + dot(rows, down_t_ref[:, at : at + step], NT)
+        part = down_t_ref[:, at : at + step]
+        dx_ref[:, at : at + step] = (ADAPTER_SCALING * dot(proj, part, NN)).astype(jnp.bfloat16)
+        total = total + dot(rows, part, NT)
         down = ADAPTER_SCALING * dot(rows, proj, TN)
         for b in range(step // wide):
+            zh, y = divmod(at // wide + b, n_y)
             pair = []
             for c in range(2):
                 lo = b * wide + c * half
                 pair.append(jnp.concatenate([down[lo : lo + quarter], down[lo + quarter : lo + half]], axis=1))
-            keep_ref[at // wide + b, :quarter, :] = jnp.where(first, pair[0], pair[1])
-            send_ref[at // wide + b, :quarter, :] = jnp.where(first, pair[1], pair[0])
+            keep_ref[turn[y], zh, :quarter, :] = jnp.where(first, pair[0], pair[1])
+            send_ref[turn[y], zh, :quarter, :] = jnp.where(first, pair[1], pair[0])
     up_t = ADAPTER_SCALING * dot(grads, total.astype(jnp.bfloat16), TN)
     up_t = jnp.concatenate([up_t, jnp.zeros_like(up_t)], axis=1)
     few = grads.shape[1] // (2 * blocks)
     for b in range(blocks):
+        zh, y = divmod(b, n_y)
         low, high = up_t[2 * b * few : (2 * b + 1) * few], up_t[(2 * b + 1) * few : (2 * b + 2) * few]
-        keep_ref[b, quarter:, :] = jnp.where(first, low, high)
-        send_ref[b, quarter:, :] = jnp.where(first, high, low)
+        keep_ref[turn[y], zh, quarter:, :] = jnp.where(first, low, high)
+        send_ref[turn[y], zh, quarter:, :] = jnp.where(first, high, low)
+
+
+def chip_sum_kernel(keep_ref, other_ref, own_ref, *away_refs):
+    own_ref[...] = keep_ref[0] + other_ref[0]
+    for at, away_ref in enumerate(away_refs):
+        away_ref[...] = (keep_ref[at + 1] + other_ref[at + 1]).astype(away_ref.dtype)
+
+
+def column_sum_kernel(own_ref, *refs):
+    *got_refs, out_ref = refs
+    total = own_ref[...]
+    for got_ref in got_refs:
+        total = total + got_ref[...].astype(jnp.float32)
+    out_ref[...] = total
+
+
+def last_sum_kernel(got_ref, down_ref, up_t_ref):
+    half, rank = down_ref.shape
+    quarter = half // 2
+    total = jnp.sum(got_ref[...], axis=0)
+    down_ref[:quarter, :] = total[:quarter, :rank]
+    down_ref[quarter:, :] = total[:quarter, rank:]
+    up_t_ref[...] = total[quarter:, :rank]
 
 
 def final_kernel(place_ref, counts_ref, packing_ref, grads_ref, own_ref, other_ref, back_ref, out_ref, chosen_ref):
@@ -157,12 +177,11 @@
     up = task_up_adapters[0]
     rank = up.shape[0]
     bf16, f32 = jnp.bfloat16, jnp.float32
-    core = lax.axis_index("c").astype(jnp.int32).reshape(1)
+    place = jnp.stack([lax.axis_index("c"), lax.axis_index("y")]).astype(jnp.int32)
 
     with jax.named_scope("frozen_gather"):
-        along_z = [fixed_value_weight]
-        for shift in range(1, n_zh):
-            along_z.append(lax.ppermute(fixed_value_weight, "zh", [(i, (i + shift) % n_zh) for i in range(n_zh)]))
+        spread = jnp.broadcast_to(fixed_value_weight[None], (n_zh, part, kv_width))
+        along_z = lax.all_to_all(spread, "zh", 0, 0, tiled=True).reshape(n_zh * part, kv_width)
 
     with jax.named_scope("pack"):
         packed = pl.pallas_call(
@@ -181,50 +200,64 @@
             ],
             compiler_params=params(WHOLE_VMEM),
         )(live_row_counts, row_packing_order, inputs, output_gradient_rows)
-        packed, *along_z = lax.optimization_barrier((packed, *along_z))
+        packed, along_z = lax.optimization_barrier((packed, along_z))
         recv = lax.all_to_all(packed.reshape(tasks, slot, features + kv_width), DP, 0, 0, tiled=True)
         recv = recv.reshape(per_device, features + kv_width)
-        own = lax.all_gather(jnp.concatenate(along_z, axis=0), "y", axis=0, tiled=True)
-
-    with jax.named_scope("adapter_input_grad"):
-        dx = pl.pallas_call(
-            input_grad_kernel,
-            out_shape=jax.ShapeDtypeStruct((per_device, features), bf16),
+        own = lax.all_gather(along_z, "y", axis=0, tiled=True)
+
+    with jax.named_scope("adapters"):
+        quarter = features // (4 * blocks)
+        few = kv_width // (2 * blocks)
+        deep = quarter + few
+        terms = jax.ShapeDtypeStruct((n_y, n_zh, deep, 2 * rank), f32)
+        dx, keep, send = pl.pallas_call(
+            adapter_kernel,
+            out_shape=(jax.ShapeDtypeStruct((per_device, features), bf16), terms, terms),
             grid=(1,),
-            in_specs=[
-                pl.BlockSpec((per_device, kv_width), lambda i: (0, features // kv_width)),
-                one(rank, features),
-                one(rank, kv_width),
-            ],
-            out_specs=one(per_device, features),
+            in_specs=[scalars(), one(per_device, features + kv_width), one(rank, features), one(rank, kv_width)],
+            out_specs=(one(per_device, features), one(*terms.shape), one(*terms.shape)),
             compiler_params=params(),
-        )(recv, down_t, up)
+        )(place, recv, down_t, up)
         back = lax.all_to_all(dx.reshape(tasks, slot, features), DP, 0, 0, tiled=True)
         back = back.reshape(per_device, features)
 
     with jax.named_scope("weight_grads"):
-        quarter = features // (4 * blocks)
-        few = kv_width // (2 * blocks)
-        terms = jax.ShapeDtypeStruct((blocks, quarter + few, 2 * rank), f32)
-        keep, send = pl.pallas_call(
-            weight_grad_kernel,
-            out_shape=(terms, terms),
+        terms = (n_y, n_zh * deep, 2 * rank)
+        flat = terms[1:]
+        keep, from_core = keep.reshape(terms), lax.ppermute(send.reshape(terms), "c", [(0, 1), (1, 0)])
+        mine, *away = pl.pallas_call(
+            chip_sum_kernel,
+            out_shape=[jax.ShapeDtypeStruct(flat, f32)] + [jax.ShapeDtypeStruct(flat, bf16)] * (n_y - 1),
             grid=(1,),
-            in_specs=[scalars(), one(per_device, features + kv_width), one(rank, features), one(rank, kv_width)],
-            out_specs=(one(*terms.shape), one(*terms.shape)),
+            in_specs=[one(*terms), one(*terms)],
+            out_specs=[one(*flat)] * n_y,
             compiler_params=params(),
-        )(core, recv, down_t, up)
-        chip = (keep + lax.ppermute(send, "c", [(0, 1), (1, 0)])).astype(bf16)
-        chip, own = lax.optimization_barrier((chip, own))
+        )(keep, from_core)
+        own, mine, *away = lax.optimization_barrier((own, mine, *away))
         other = lax.ppermute(own, "c", [(0, 1), (1, 0)])
-        chip, back = lax.optimization_barrier((chip, back))
-        shares = lax.all_to_all(chip, ("zh", "y"), 0, 0, tiled=True)
-        share = jnp.sum(shares.astype(f32), axis=0)
-        down_share = jnp.concatenate([share[:quarter, :rank], share[:quarter, rank:]], axis=0)
-        up_share = share[quarter:, :rank].T
+        got = [lax.ppermute(a, "y", [(i, (i + at + 1) % n_y) for i in range(n_y)]) for at, a in enumerate(away)]
+        column = pl.pallas_call(
+            column_sum_kernel,
+            out_shape=jax.ShapeDtypeStruct(flat, f32),
+            grid=(1,),
+            in_specs=[one(*flat)] * n_y,
+            out_specs=one(*flat),
+            compiler_params=params(),
+        )(mine, *got)
+        column, back = lax.optimization_barrier((column, back))
+        shares = lax.all_to_all(column.reshape(n_zh, deep, 2 * rank), "zh", 0, 0, tiled=True)
+        down_share, up_t_share = pl.pallas_call(
+            last_sum_kernel,
+            out_shape=(jax.ShapeDtypeStruct((2 * quarter, rank), f32), jax.ShapeDtypeStruct((few, rank), f32)),
+            grid=(1,),
+            in_specs=[one(n_zh, deep, 2 * rank)],
+            out_specs=(one(2 * quarter, rank), one(few, rank)),
+            compiler_params=params(),
+        )(shares)
+        up_share = up_t_share.T
 
     with jax.named_scope("input_grad"):
-        halves = 2
+        halves = 1
         several = n_y // halves
         wide = several * 2 * part
         order = (n_y, n_zh, part, kv_width)
@@ -232,12 +265,8 @@
         def block(*shape):
             return pl.BlockSpec(shape, lambda i, place: (0,) * len(shape))
 
-        def weight_at(i, place):
-            return i % halves, lax.rem(place[1] - i // halves + n_zh, n_zh), 0, 0
-
-        weight_spec = pl.BlockSpec((several, 1, part, kv_width), weight_at)
+        weight_spec = pl.BlockSpec((several, 1, part, kv_width), lambda i, place: (i % halves, i // halves, 0, 0))
         rows_spec = pl.BlockSpec((per_device, wide), lambda i, place: (0, i))
-        place = jnp.stack([core[0], lax.axis_index("zh").astype(jnp.int32)])
         input_grad = pl.pallas_call(
             final_kernel,
             out_shape=jax.ShapeDtypeStruct((per_device, features), bf16),
@@ -255,7 +284,7 @@
                 out_specs=rows_spec,
                 scratch_shapes=[pltpu.VMEM((per_device, per_device), bf16)],
             ),
-            compiler_params=params(),
+            compiler_params=params(WHOLE_VMEM),
         )(
             place,
             live_row_counts,

time: 146 us -> 155 us (1.062)
  starting transfers between devices: 55.6 us -> 68.6 us
  other arithmetic: 2.27 us -> 0.08 us
  waiting for transfers between devices: 53.9 us -> 52.2 us
    all_to_all x1, waiting for transfers between devices: 12 us -> 0.01 us  [on_device(): lax.all_to_all(dx.reshape(tasks, slot, features), DP, 0, 0, tiled=True)]
    all_to_all x1 -> x2, starting transfers between devices: 13.7 us -> 24.6 us  [the longest x1 14.5 us: on_device(): lax.all_to_all(spread, 'zh', 0, 0, tiled=True)]
    all_to_all x1 -> x2, waiting for transfers between devices: 8.84 us -> 15 us  [the longest x1 12 us: on_device(): lax.all_to_all(spread, 'zh', 0, 0, tiled=True)]
    ppermute x4 -> x8, starting transfers between devices: 25.9 us -> 29.5 us  [the longest x7 27.6 us: on_device(): lax.ppermute(a, 'y', [(i, (i + at + 1) % n_y) for i in range(n_y)])]
    pallas_call x2 -> x4, Pallas kernels: 2.35 us -> 4.97 us  [the longest x1 3.53 us: on_device(): pl.pallas_call(adapter_kernel, out_shape=(jax.ShapeDtypeStruct((per_devic...]
    all_to_all x1, starting transfers between devices: 8.65 us -> 6.34 us  [on_device(): lax.all_to_all(packed.reshape(tasks, slot, features + kv_width), DP, 0, 0...]
    unnamed x20 -> x14, local copies, waits for them, and re-layouts: 4.63 us -> 2.85 us
    ppermute x4 -> x8, waiting for transfers between devices: 3.38 us -> 5.06 us  [the longest x7 3 us: on_device(): lax.ppermute(a, 'y', [(i, (i + at + 1) % n_y) for i in range(n_y)])]
  transfers between devices with their start and end apart: 9 -> 14, of which waited for: 6 -> 6; matrix products, arithmetic and copies ran while one was open for 1% -> 0% of each run, Pallas kernels for 9% -> 9%
where the time goes in v3:
time: 155 us; the launch traced here: 154 us
  starting transfers between devices  68.6 us (44%)
  waiting for transfers between devices  52.2 us (34%)
  Pallas kernels  14.5 us (9%)
  between operations  14.2 us (9%)
  local copies, waits for them, and re-layouts  4.42 us (3%)
    ppermute x7, starting transfers between devices, on_device(): lax.ppermute(a, 'y', [(i, (i + at + 1) % n_y) for i in range(n_y)])  27.6 us
    all_to_all x1, waiting for transfers between devices, on_device(): lax.all_to_all(packed.reshape(tasks, slot, features + kv_width), DP, 0, 0...  27.2 us
    all_to_all x1, starting transfers between devices, on_device(): lax.all_to_all(spread, 'zh', 0, 0, tiled=True)  14.5 us
    all_to_all x1, waiting for transfers between devices, on_device(): lax.all_to_all(spread, 'zh', 0, 0, tiled=True)  12 us
    all_to_all x1, starting transfers between devices, on_device(): lax.all_to_all(column.reshape(n_zh, deep, 2 * rank), 'zh', 0, 0, tiled=True)  10.1 us
    all_to_all x1, starting transfers between devices, on_device(): lax.all_to_all(packed.reshape(tasks, slot, features + kv_width), DP, 0, 0...  6.34 us
    pallas_call x1, Pallas kernels, on_device(): pl.pallas_call(final_kernel, out_shape=jax.ShapeDtypeStruct((per_device,...  6.32 us
    all_to_all x1, starting transfers between devices, on_device(): lax.all_to_all(dx.reshape(tasks, slot, features), DP, 0, 0, tiled=True)  6.16 us
  transfers between devices with their start and end apart: 14, of which 6 were waited for; matrix products, arithmetic and copies ran while one was open for 0% of the time, Pallas kernels for 9%

profile of v3, /device:TPU:6, one launch (start us, length us, event | category | flops | bytes accessed | tf_op | source)
XLA Modules:
  0.0 153.9 jit_solution(13018007062656601575)
XLA Ops:
  7.2 1.6 %broadcast_in_dim.12 = bf16[4,64,512]{2,1,0:T(8,128)(2,1)} broadcast(bf16[64,512]{1,0:T(8,128)(2,1)} %param.9), dimensions={1,2} | broadcast | bytes 327680 | tf_op jit(solution)/shard_map/frozen_gather/broadcast_in_dim | solution.py:183
  8.7 14.5 %all-to-all-start = ((bf16[4,64,512]{2,1,0:T(8,128)(2,1)}), bf16[4,64,512]{2,1,0:T(8,128)(2,1)S(1)}, u32[]{:S(2)}, u32[]{:S(2)}) async-start(bf16[4,64,512]{2,1,0:T(8,128)(2,1)} %broadcast_in_dim.12), calls=%async_computation | async-start | bytes 524288 | tf_op jit(solution)/shard_map/frozen_gather/all_to_all | solution.py:184
  23.2 3.3 %pack.1 = bf16[192,4608]{1,0:T(8,128)(2,1)} custom-call(s32[1,12]{1,0:T(1,128)} %counts_ref.1, s32[1,192]{1,0:T(1,128)} %packing_ref.1, bf16[192,4096]{1,0:T(8,128)(2,1)} %rows_hbm.1, bf16[192,512]{1,0:T(8,128)(2,1)} %grads_ref.1), custom_call_target="tpu_custom_call" | custom-call | tf_op jit(solution)/shard_map/pack/pallas_call | solution.py:187
  26.5 12.0 %all-to-all-done = bf16[4,64,512]{2,1,0:T(8,128)(2,1)S(1)} async-done(((bf16[4,64,512]{2,1,0:T(8,128)(2,1)}), bf16[4,64,512]{2,1,0:T(8,128)(2,1)S(1)}, u32[]{:S(2)}, u32[]{:S(2)}) %all-to-all-start) | async-done | bytes 262176 | tf_op jit(solution)/shard_map/frozen_gather/all_to_all | solution.py:184
  38.5 0.0 copy-start.6
  38.5 0.0 copy-start
  38.5 0.0 copy-start.1
  38.5 0.7 copy-done.6
  39.2 6.3 %all-to-all-start.1 = ((bf16[12,16,4608]{2,1,0:T(8,128)(2,1)}), bf16[12,16,4608]{2,1,0:T(8,128)(2,1)S(1)}, u32[]{:S(2)}, u32[]{:S(2)}) async-start(bf16[12,16,4608]{2,1,0:T(8,128)(2,1)} %bitcast.25), calls=%async_computation.1 | async-start | bytes 3538944 | tf_op jit(solution)/shard_map/pack/all_to_all | solution.py:204
  45.6 0.0 all-gather.2.cloned.1.call-start
  45.6 0.7 all-gather.2.cloned.1.call-update
  46.3 0.1 pad_add_fusion.place_ref
  46.4 0.0 copy-start.2
  46.4 27.2 %all-to-all-done.1 = bf16[12,16,4608]{2,1,0:T(8,128)(2,1)S(1)} async-done(((bf16[12,16,4608]{2,1,0:T(8,128)(2,1)}), bf16[12,16,4608]{2,1,0:T(8,128)(2,1)S(1)}, u32[]{:S(2)}, u32[]{:S(2)}) %all-to-all-start.1) | async-done | bytes 1769504 | tf_op jit(solution)/shard_map/pack/all_to_all | solution.py:204
  73.6 0.0 copy-done
  73.6 0.0 copy-done.1
  73.6 3.5 %adapters.1 = (bf16[192,4096]{1,0:T(8,128)(2,1)}, f32[8,4,40,128]{3,2,1,0:T(8,128)S(1)}, f32[8,4,40,128]{3,2,1,0:T(8,128)S(1)}) custom-call(s32[2]{0:T(128)S(1)} %pad_add_fusion.place_ref, bf16[192,4608]{1,0:T(8,128)(2,1)S(1)} %bitcast.20, bf16[64,4096]{1,0:T(8,128)(2,1)S(1)} %bitcast.22, bf16[64,512]{1,0:T(8,128)(2,1)S(1)} %bitcast.23), custom_call_target="tpu_custom_call" | custom-call | tf_op jit(solution)/shard_map/adapters/pallas_call | solution.py:213
  77.2 0.0 copy-start.3
  77.2 0.8 copy-done.3
  78.0 0.0 copy-start.4
  78.0 0.0 copy-done.2
  78.0 6.2 %all-to-all-start.2 = ((bf16[12,16,4096]{2,1,0:T(8,128)(2,1)}), bf16[12,16,4096]{2,1,0:T(8,128)(2,1)}, u32[]{:S(2)}, u32[]{:S(2)}) async-start(bf16[12,16,4096]{2,1,0:T(8,128)(2,1)} %bitcast.12), calls=%async_computation.2 | async-start | bytes 3145728 | tf_op jit(solution)/shard_map/adapters/all_to_all | solution.py:221
  84.2 0.0 copy-done.4
  84.2 1.9 %collective-permute-start = (f32[8,160,128]{2,1,0:T(8,128)S(1)}, f32[8,160,128]{2,1,0:T(8,128)S(1)}, u32[]{:S(2)}, u32[]{:S(2)}) collective-permute-start(f32[8,160,128]{2,1,0:T(8,128)S(1)} %bitcast.24), channel_id=1, source_target_pairs={{0,12},{12,0},{1,13},{13,1},{2,14},{14,2},{3,15},{15,3},{4,16},{16... | collective-permute-start | bytes 1966088 | tf_op jit(solution)/shard_map/weight_grads/ppermute | solution.py:227
  86.1 2.1 %collective-permute-done.other_ref = f32[8,160,128]{2,1,0:T(8,128)S(1)} collective-permute-done((f32[8,160,128]{2,1,0:T(8,128)S(1)}, f32[8,160,128]{2,1,0:T(8,128)S(1)}, u32[]{:S(2)}, u32[]{:S(2)}) %collective-permute-start) | collective-permute-done | bytes 655392 | tf_op jit(solution)/shard_map/weight_grads/ppermute | solution.py:227
  88.2 0.1 weight_grads.3
  88.2 4.1 %all-gather.2.cloned.1.call-done = bf16[2048,512]{1,0:T(8,128)(2,1)} async-done(((bf16[256,512]{1,0:T(8,128)(2,1)}), bf16[2048,512]{1,0:T(8,128)(2,1)}) %all-gather.2.cloned.1.call-update) | async-done | bytes 2097168 | tf_op jit(solution)/shard_map/pack/all_gather | solution.py:206
  92.3 1.9 %collective-permute-start.1 = (bf16[2048,512]{1,0:T(8,128)(2,1)}, bf16[2048,512]{1,0:T(8,128)(2,1)S(1)}, u32[]{:S(2)}, u32[]{:S(2)}) collective-permute-start(bf16[2048,512]{1,0:T(8,128)(2,1)} %all-gather.2.cloned.1.call-done), channel_id=1, source_target_pairs={{0,12},{12,0},{1,13},{13,1},{2,14},{14,2},{3,15},{15,3},{4,16},{16... | collective-permute-start | bytes 6291464 | tf_op jit(solution)/shard_map/weight_grads/ppermute | solution.py:237
  94.2 3.1 %collective-permute-start.2 = (bf16[160,128]{1,0:T(8,128)(2,1)S(1)}, bf16[160,128]{1,0:T(8,128)(2,1)S(1)}, u32[]{:S(2)}, u32[]{:S(2)}) collective-permute-start(bf16[160,128]{1,0:T(8,128)(2,1)S(1)} %get-tuple-element.43), channel_id=1, source_target_pairs={{0,24},{24,48},{48,72},{72,96},{96,120},{120,144},{144,168},{168,0... | collective-permute-start | bytes 122888 | tf_op jit(solution)/shard_map/weight_grads/ppermute | solution.py:238
  97.3 4.0 %collective-permute-start.3 = (bf16[160,128]{1,0:T(8,128)(2,1)S(1)}, bf16[160,128]{1,0:T(8,128)(2,1)S(1)}, u32[]{:S(2)}, u32[]{:S(2)}) collective-permute-start(bf16[160,128]{1,0:T(8,128)(2,1)S(1)} %get-tuple-element.44), channel_id=1, source_target_pairs={{0,48},{24,72},{48,96},{72,120},{96,144},{120,168},{144,0},{168,24... | collective-permute-start | bytes 122888 | tf_op jit(solution)/shard_map/weight_grads/ppermute | solution.py:238
  101.3 3.5 %collective-permute-start.4 = (bf16[160,128]{1,0:T(8,128)(2,1)S(1)}, bf16[160,128]{1,0:T(8,128)(2,1)S(1)}, u32[]{:S(2)}, u32[]{:S(2)}) collective-permute-start(bf16[160,128]{1,0:T(8,128)(2,1)S(1)} %get-tuple-element.45), channel_id=1, source_target_pairs={{0,72},{24,96},{48,120},{72,144},{96,168},{120,0},{144,24},{168,48... | collective-permute-start | bytes 122888 | tf_op jit(solution)/shard_map/weight_grads/ppermute | solution.py:238
  104.7 5.0 %collective-permute-start.5 = (bf16[160,128]{1,0:T(8,128)(2,1)S(1)}, bf16[160,128]{1,0:T(8,128)(2,1)S(1)}, u32[]{:S(2)}, u32[]{:S(2)}) collective-permute-start(bf16[160,128]{1,0:T(8,128)(2,1)S(1)} %get-tuple-element.46), channel_id=1, source_target_pairs={{0,96},{24,120},{48,144},{72,168},{96,0},{120,24},{144,48},{168,72... | collective-permute-start | bytes 122888 | tf_op jit(solution)/shard_map/weight_grads/ppermute | solution.py:238
  109.7 0.0 collective-permute-done.2.refs_0_
  109.8 4.9 %collective-permute-start.6 = (bf16[160,128]{1,0:T(8,128)(2,1)S(1)}, bf16[160,128]{1,0:T(8,128)(2,1)S(1)}, u32[]{:S(2)}, u32[]{:S(2)}) collective-permute-start(bf16[160,128]{1,0:T(8,128)(2,1)S(1)} %get-tuple-element.47), channel_id=1, source_target_pairs={{0,120},{24,144},{48,168},{72,0},{96,24},{120,48},{144,72},{168,96... | collective-permute-start | bytes 122888 | tf_op jit(solution)/shard_map/weight_grads/ppermute | solution.py:238
  114.6 0.0 collective-permute-done.3.refs_1_
  114.6 4.4 %collective-permute-start.7 = (bf16[160,128]{1,0:T(8,128)(2,1)S(1)}, bf16[160,128]{1,0:T(8,128)(2,1)S(1)}, u32[]{:S(2)}, u32[]{:S(2)}) collective-permute-start(bf16[160,128]{1,0:T(8,128)(2,1)S(1)} %get-tuple-element.48), channel_id=1, source_target_pairs={{0,144},{24,168},{48,0},{72,24},{96,48},{120,72},{144,96},{168,120... | collective-permute-start | bytes 122888 | tf_op jit(solution)/shard_map/weight_grads/ppermute | solution.py:238
  119.0 0.0 collective-permute-done.4.refs_2_
  119.0 2.9 %collective-permute-start.8 = (bf16[160,128]{1,0:T(8,128)(2,1)S(1)}, bf16[160,128]{1,0:T(8,128)(2,1)S(1)}, u32[]{:S(2)}, u32[]{:S(2)}) collective-permute-start(bf16[160,128]{1,0:T(8,128)(2,1)S(1)} %get-tuple-element.49), channel_id=1, source_target_pairs={{0,168},{24,0},{48,24},{72,48},{96,72},{120,96},{144,120},{168,144... | collective-permute-start | bytes 122888 | tf_op jit(solution)/shard_map/weight_grads/ppermute | solution.py:238
  121.9 0.0 collective-permute-done.5.refs_3_
  121.9 0.0 collective-permute-done.6.refs_4_
  121.9 0.0 collective-permute-done.7.refs_5_
  121.9 3.0 %collective-permute-done.8.refs_6_ = bf16[160,128]{1,0:T(8,128)(2,1)S(1)} collective-permute-done((bf16[160,128]{1,0:T(8,128)(2,1)S(1)}, bf16[160,128]{1,0:T(8,128)(2,1)S(1)}, u32[]{:S(2)}, u32[]{:S(2)}) %collective-permute-start.8) | collective-permute-done | bytes 40992 | tf_op jit(solution)/shard_map/weight_grads/ppermute | solution.py:238
  124.9 0.7 weight_grads.4
  125.6 0.0 all-to-all-done.2
  125.6 10.1 %all-to-all-start.3 = ((f32[4,40,128]{2,1,0:T(8,128)}), f32[4,40,128]{2,1,0:T(8,128)S(1)}, u32[]{:S(2)}, u32[]{:S(2)}) async-start(f32[4,40,128]{2,1,0:T(8,128)} %bitcast.14), calls=%async_computation.3 | async-start | bytes 163840 | tf_op jit(solution)/shard_map/weight_grads/all_to_all | solution.py:248
  135.8 0.0 collective-permute-done.1
  135.8 0.0 copy-start.5
  135.8 1.3 copy-done.5
  137.1 6.3 %input_grad.1 = bf16[192,4096]{1,0:T(8,128)(2,1)} custom-call(s32[2]{0:T(128)} %copy-done.2, s32[1,12]{1,0:T(1,128)} %counts_ref.1, s32[1,192]{1,0:T(1,128)} %packing_ref.1, bf16[192,512]{1,0:T(8,128)(2,1)} %grads_ref.1, bf16[8,4,64,512]{3,2,1,0:T(8,128)(2,1)} %bitcast.26, bf16[8,4,64,512]{3,2,1,0:T(8,128)(2,1)} %bitcast.27, bf16[192,4096]{1,0:T(8,128)(2,1)} %bitcast.13.back_ref), custom_call_target="tpu_custom_call" | custom-call | tf_op jit(solution)/shard_map/input_grad/pallas_call | solution.py:270
  143.4 3.0 %all-to-all-done.3.got_ref = f32[4,40,128]{2,1,0:T(8,128)S(1)} async-done(((f32[4,40,128]{2,1,0:T(8,128)}), f32[4,40,128]{2,1,0:T(8,128)S(1)}, u32[]{:S(2)}, u32[]{:S(2)}) %all-to-all-start.3) | async-done | bytes 81952 | tf_op jit(solution)/shard_map/weight_grads/all_to_all | solution.py:248
  146.4 0.7 weight_grads.5
Async XLA Ops:
  8.7 29.8 %all-to-all-start = ((bf16[4,64,512]{2,1,0:T(8,128)(2,1)}), bf16[4,64,512]{2,1,0:T(8,128)(2,1)S(1)}, u32[]{:S(2)}, u32[]{:S(2)}) async-start(bf16[4,64,512]{2,1,0:T(8,128)(2,1)} %broadcast_in_dim.12), calls=%async_computation | async-start | bytes 524288 | tf_op jit(solution)/shard_map/frozen_gather/all_to_all | solution.py:184
  38.5 0.7 copy-start.6
  38.5 35.1 %copy-start = (bf16[1,4096,64]{1,2,0:T(8,128)(2,1)S(1)}, bf16[1,4096,64]{1,2,0:T(8,128)(2,1)}, u32[]{:S(2)}) copy-start(bf16[1,4096,64]{1,2,0:T(8,128)(2,1)} %param.10) | copy-start | bytes 1572868
  38.5 35.1 %copy-start.1 = (bf16[1,64,512]{2,1,0:T(8,128)(2,1)S(1)}, bf16[1,64,512]{2,1,0:T(8,128)(2,1)}, u32[]{:S(2)}) copy-start(bf16[1,64,512]{2,1,0:T(8,128)(2,1)} %param.11) | copy-start | bytes 196612
  39.2 34.4 %all-to-all-start.1 = ((bf16[12,16,4608]{2,1,0:T(8,128)(2,1)}), bf16[12,16,4608]{2,1,0:T(8,128)(2,1)S(1)}, u32[]{:S(2)}, u32[]{:S(2)}) async-start(bf16[12,16,4608]{2,1,0:T(8,128)(2,1)} %bitcast.25), calls=%async_computation.1 | async-start | bytes 3538944 | tf_op jit(solution)/shard_map/pack/all_to_all | solution.py:204
  45.6 46.8 %all-gather.2.cloned.1.call-start = ((), (), s32[]{:S(2)}) async-start(), calls=%async_computation.4 | async-start | bytes 2359296 | tf_op jit(solution)/shard_map/pack/all_gather | solution.py:206
  46.4 31.6 %copy-start.2 = (s32[2]{0:T(128)}, s32[2]{0:T(128)S(1)}, u32[]{:S(2)}) copy-start(s32[2]{0:T(128)S(1)} %pad_add_fusion.place_ref) | copy-start | bytes 28
  77.2 0.8 copy-start.3
  78.0 6.2 %copy-start.4 = (f32[8,4,40,128]{3,2,1,0:T(8,128)S(1)}, f32[8,4,40,128]{3,2,1,0:T(8,128)}, u32[]{:S(2)}) copy-start(f32[8,4,40,128]{3,2,1,0:T(8,128)} %copy-done.3) | copy-start | bytes 1966084
  78.0 47.6 %all-to-all-start.2 = ((bf16[12,16,4096]{2,1,0:T(8,128)(2,1)}), bf16[12,16,4096]{2,1,0:T(8,128)(2,1)}, u32[]{:S(2)}, u32[]{:S(2)}) async-start(bf16[12,16,4096]{2,1,0:T(8,128)(2,1)} %bitcast.12), calls=%async_computation.2 | async-start | bytes 3145728 | tf_op jit(solution)/shard_map/adapters/all_to_all | solution.py:221
  84.2 4.0 %collective-permute-start = (f32[8,160,128]{2,1,0:T(8,128)S(1)}, f32[8,160,128]{2,1,0:T(8,128)S(1)}, u32[]{:S(2)}, u32[]{:S(2)}) collective-permute-start(f32[8,160,128]{2,1,0:T(8,128)S(1)} %bitcast.24), channel_id=1, source_target_pairs={{0,12},{12,0},{1,13},{13,1},{2,14},{14,2},{3,15},{15,3},{4,16},{16... | collective-permute-start | bytes 1966088 | tf_op jit(solution)/shard_map/weight_grads/ppermute | solution.py:227
  92.3 43.4 %collective-permute-start.1 = (bf16[2048,512]{1,0:T(8,128)(2,1)}, bf16[2048,512]{1,0:T(8,128)(2,1)S(1)}, u32[]{:S(2)}, u32[]{:S(2)}) collective-permute-start(bf16[2048,512]{1,0:T(8,128)(2,1)} %all-gather.2.cloned.1.call-done), channel_id=1, source_target_pairs={{0,12},{12,0},{1,13},{13,1},{2,14},{14,2},{3,15},{15,3},{4,16},{16... | collective-permute-start | bytes 6291464 | tf_op jit(solution)/shard_map/weight_grads/ppermute | solution.py:237
  94.2 15.5 %collective-permute-start.2 = (bf16[160,128]{1,0:T(8,128)(2,1)S(1)}, bf16[160,128]{1,0:T(8,128)(2,1)S(1)}, u32[]{:S(2)}, u32[]{:S(2)}) collective-permute-start(bf16[160,128]{1,0:T(8,128)(2,1)S(1)} %get-tuple-element.43), channel_id=1, source_target_pairs={{0,24},{24,48},{48,72},{72,96},{96,120},{120,144},{144,168},{168,0... | collective-permute-start | bytes 122888 | tf_op jit(solution)/shard_map/weight_grads/ppermute | solution.py:238
  97.3 17.3 %collective-permute-start.3 = (bf16[160,128]{1,0:T(8,128)(2,1)S(1)}, bf16[160,128]{1,0:T(8,128)(2,1)S(1)}, u32[]{:S(2)}, u32[]{:S(2)}) collective-permute-start(bf16[160,128]{1,0:T(8,128)(2,1)S(1)} %get-tuple-element.44), channel_id=1, source_target_pairs={{0,48},{24,72},{48,96},{72,120},{96,144},{120,168},{144,0},{168,24... | collective-permute-start | bytes 122888 | tf_op jit(solution)/shard_map/weight_grads/ppermute | solution.py:238
  101.3 17.8 %collective-permute-start.4 = (bf16[160,128]{1,0:T(8,128)(2,1)S(1)}, bf16[160,128]{1,0:T(8,128)(2,1)S(1)}, u32[]{:S(2)}, u32[]{:S(2)}) collective-permute-start(bf16[160,128]{1,0:T(8,128)(2,1)S(1)} %get-tuple-element.45), channel_id=1, source_target_pairs={{0,72},{24,96},{48,120},{72,144},{96,168},{120,0},{144,24},{168,48... | collective-permute-start | bytes 122888 | tf_op jit(solution)/shard_map/weight_grads/ppermute | solution.py:238
  104.7 17.2 %collective-permute-start.5 = (bf16[160,128]{1,0:T(8,128)(2,1)S(1)}, bf16[160,128]{1,0:T(8,128)(2,1)S(1)}, u32[]{:S(2)}, u32[]{:S(2)}) collective-permute-start(bf16[160,128]{1,0:T(8,128)(2,1)S(1)} %get-tuple-element.46), channel_id=1, source_target_pairs={{0,96},{24,120},{48,144},{72,168},{96,0},{120,24},{144,48},{168,72... | collective-permute-start | bytes 122888 | tf_op jit(solution)/shard_map/weight_grads/ppermute | solution.py:238
  109.8 12.2 %collective-permute-start.6 = (bf16[160,128]{1,0:T(8,128)(2,1)S(1)}, bf16[160,128]{1,0:T(8,128)(2,1)S(1)}, u32[]{:S(2)}, u32[]{:S(2)}) collective-permute-start(bf16[160,128]{1,0:T(8,128)(2,1)S(1)} %get-tuple-element.47), channel_id=1, source_target_pairs={{0,120},{24,144},{48,168},{72,0},{96,24},{120,48},{144,72},{168,96... | collective-permute-start | bytes 122888 | tf_op jit(solution)/shard_map/weight_grads/ppermute | solution.py:238
  114.6 7.3 %collective-permute-start.7 = (bf16[160,128]{1,0:T(8,128)(2,1)S(1)}, bf16[160,128]{1,0:T(8,128)(2,1)S(1)}, u32[]{:S(2)}, u32[]{:S(2)}) collective-permute-start(bf16[160,128]{1,0:T(8,128)(2,1)S(1)} %get-tuple-element.48), channel_id=1, source_target_pairs={{0,144},{24,168},{48,0},{72,24},{96,48},{120,72},{144,96},{168,120... | collective-permute-start | bytes 122888 | tf_op jit(solution)/shard_map/weight_grads/ppermute | solution.py:238
  119.0 5.9 %collective-permute-start.8 = (bf16[160,128]{1,0:T(8,128)(2,1)S(1)}, bf16[160,128]{1,0:T(8,128)(2,1)S(1)}, u32[]{:S(2)}, u32[]{:S(2)}) collective-permute-start(bf16[160,128]{1,0:T(8,128)(2,1)S(1)} %get-tuple-element.49), channel_id=1, source_target_pairs={{0,168},{24,0},{48,24},{72,48},{96,72},{120,96},{144,120},{168,144... | collective-permute-start | bytes 122888 | tf_op jit(solution)/shard_map/weight_grads/ppermute | solution.py:238
  125.6 20.8 %all-to-all-start.3 = ((f32[4,40,128]{2,1,0:T(8,128)}), f32[4,40,128]{2,1,0:T(8,128)S(1)}, u32[]{:S(2)}, u32[]{:S(2)}) async-start(f32[4,40,128]{2,1,0:T(8,128)} %bitcast.14), calls=%async_computation.3 | async-start | bytes 163840 | tf_op jit(solution)/shard_map/weight_grads/all_to_all | solution.py:248
  135.8 1.3 copy-start.5
Sparse Core Ops, SparseCore 0:
  48.8 43.5 all-gather.1

commit v4 on v3

--- a/solution.py
+++ b/solution.py
@@ -77,7 +77,6 @@
     proj = dot(grads, up_ref[...], NT).astype(jnp.bfloat16)
     total = jnp.zeros((recv_ref.shape[0], rank), jnp.float32)
     step = 1024
-    turn = [lax.rem(y - place_ref[1] + n_y, n_y) for y in range(n_y)]
     for at in range(0, features, step):
         rows = recv_ref[:, at : at + step]
         part = down_t_ref[:, at : at + step]
@@ -90,30 +89,20 @@
             for c in range(2):
                 lo = b * wide + c * half
                 pair.append(jnp.concatenate([down[lo : lo + quarter], down[lo + quarter : lo + half]], axis=1))
-            keep_ref[turn[y], zh, :quarter, :] = jnp.where(first, pair[0], pair[1])
-            send_ref[turn[y], zh, :quarter, :] = jnp.where(first, pair[1], pair[0])
+            keep_ref[y, zh, :quarter, :] = jnp.where(first, pair[0], pair[1])
+            send_ref[y, zh, :quarter, :] = jnp.where(first, pair[1], pair[0])
     up_t = ADAPTER_SCALING * dot(grads, total.astype(jnp.bfloat16), TN)
     up_t = jnp.concatenate([up_t, jnp.zeros_like(up_t)], axis=1)
     few = grads.shape[1] // (2 * blocks)
     for b in range(blocks):
         zh, y = divmod(b, n_y)
         low, high = up_t[2 * b * few : (2 * b + 1) * few], up_t[(2 * b + 1) * few : (2 * b + 2) * few]
-        keep_ref[turn[y], zh, quarter:, :] = jnp.where(first, low, high)
-        send_ref[turn[y], zh, quarter:, :] = jnp.where(first, high, low)
-
-
-def chip_sum_kernel(keep_ref, other_ref, own_ref, *away_refs):
-    own_ref[...] = keep_ref[0] + other_ref[0]
-    for at, away_ref in enumerate(away_refs):
-        away_ref[...] = (keep_ref[at + 1] + other_ref[at + 1]).astype(away_ref.dtype)
-
-
-def column_sum_kernel(own_ref, *refs):
-    *got_refs, out_ref = refs
-    total = own_ref[...]
-    for got_ref in got_refs:
-        total = total + got_ref[...].astype(jnp.float32)
-    out_ref[...] = total
+        keep_ref[y, zh, quarter:, :] = jnp.where(first, low, high)
+        send_ref[y, zh, quarter:, :] = jnp.where(first, high, low)
+
+
+def chip_sum_kernel(keep_ref, other_ref, out_ref):
+    out_ref[...] = keep_ref[...] + other_ref[...]
 
 
 def last_sum_kernel(got_ref, down_ref, up_t_ref):
@@ -177,7 +166,7 @@
     up = task_up_adapters[0]
     rank = up.shape[0]
     bf16, f32 = jnp.bfloat16, jnp.float32
-    place = jnp.stack([lax.axis_index("c"), lax.axis_index("y")]).astype(jnp.int32)
+    place = lax.axis_index("c").astype(jnp.int32).reshape(1)
 
     with jax.named_scope("frozen_gather"):
         spread = jnp.broadcast_to(fixed_value_weight[None], (n_zh, part, kv_width))
@@ -222,28 +211,19 @@
         back = back.reshape(per_device, features)
 
     with jax.named_scope("weight_grads"):
-        terms = (n_y, n_zh * deep, 2 * rank)
-        flat = terms[1:]
+        terms = (blocks * deep, 2 * rank)
         keep, from_core = keep.reshape(terms), lax.ppermute(send.reshape(terms), "c", [(0, 1), (1, 0)])
-        mine, *away = pl.pallas_call(
+        chip = pl.pallas_call(
             chip_sum_kernel,
-            out_shape=[jax.ShapeDtypeStruct(flat, f32)] + [jax.ShapeDtypeStruct(flat, bf16)] * (n_y - 1),
+            out_shape=jax.ShapeDtypeStruct(terms, f32),
             grid=(1,),
             in_specs=[one(*terms), one(*terms)],
-            out_specs=[one(*flat)] * n_y,
+            out_specs=one(*terms),
             compiler_params=params(),
         )(keep, from_core)
-        own, mine, *away = lax.optimization_barrier((own, mine, *away))
+        chip, own = lax.optimization_barrier((chip, own))
         other = lax.ppermute(own, "c", [(0, 1), (1, 0)])
-        got = [lax.ppermute(a, "y", [(i, (i + at + 1) % n_y) for i in range(n_y)]) for at, a in enumerate(away)]
-        column = pl.pallas_call(
-            column_sum_kernel,
-            out_shape=jax.ShapeDtypeStruct(flat, f32),
-            grid=(1,),
-            in_specs=[one(*flat)] * n_y,
-            out_specs=one(*flat),
-            compiler_params=params(),
-        )(mine, *got)
+        column = lax.psum_scatter(chip, "y", scatter_dimension=0, tiled=True)
         column, back = lax.optimization_barrier((column, back))
         shares = lax.all_to_all(column.reshape(n_zh, deep, 2 * rank), "zh", 0, 0, tiled=True)
         down_share, up_t_share = pl.pallas_call(

time: 155 us -> 166 us (1.071)
  waiting for transfers between devices: 52.2 us -> 92.5 us
  starting transfers between devices: 68.6 us -> 41 us
    reduce_scatter x0 -> x1, waiting for transfers between devices: none -> 42.9 us  [on_device(): column = lax.psum_scatter(chip, 'y', scatter_dimension=0, tiled=True)]
    ppermute x7 -> x0, starting transfers between devices: 27.6 us -> none  [on_device(): lax.ppermute(a, 'y', [(i, (i + at + 1) % n_y) for i in range(n_y)])]
    ppermute x7 -> x0, waiting for transfers between devices: 3 us -> none  [on_device(): lax.ppermute(a, 'y', [(i, (i + at + 1) % n_y) for i in range(n_y)])]
  transfers between devices with their start and end apart: 14 -> 8, of which waited for: 6 -> 6; matrix products, arithmetic and copies ran while one was open for 0% -> 0% of each run, Pallas kernels for 9% -> 8%
where the time goes in v4:
time: 166 us; the launch traced here: 165 us
  waiting for transfers between devices  92.5 us (56%)
  starting transfers between devices  41 us (25%)
  between operations  14.1 us (8%)
  Pallas kernels  13.5 us (8%)
  local copies, waits for them, and re-layouts  4.42 us (3%)
    reduce_scatter x1, waiting for transfers between devices, on_device(): column = lax.psum_scatter(chip, 'y', scatter_dimension=0, tiled=True)  42.9 us
    all_to_all x1, waiting for transfers between devices, on_device(): lax.all_to_all(packed.reshape(tasks, slot, features + kv_width), DP, 0, 0...  27.3 us
    all_to_all x1, starting transfers between devices, on_device(): lax.all_to_all(spread, 'zh', 0, 0, tiled=True)  14.5 us
    all_to_all x1, waiting for transfers between devices, on_device(): lax.all_to_all(spread, 'zh', 0, 0, tiled=True)  12 us
    all_to_all x1, starting transfers between devices, on_device(): lax.all_to_all(column.reshape(n_zh, deep, 2 * rank), 'zh', 0, 0, tiled=True)  10.1 us
    all_to_all x1, starting transfers between devices, on_device(): lax.all_to_all(packed.reshape(tasks, slot, features + kv_width), DP, 0, 0...  6.34 us
    all_to_all x1, starting transfers between devices, on_device(): lax.all_to_all(dx.reshape(tasks, slot, features), DP, 0, 0, tiled=True)  6.15 us
    pallas_call x1, Pallas kernels, on_device(): pl.pallas_call(final_kernel, out_shape=jax.ShapeDtypeStruct((per_device,...  5.62 us
  transfers between devices with their start and end apart: 8, of which 6 were waited for; matrix products, arithmetic and copies ran while one was open for 0% of the time, Pallas kernels for 8%

profile of v4, /device:TPU:6, one launch (start us, length us, event | category | flops | bytes accessed | tf_op | source)
XLA Modules:
  0.0 165.5 jit_solution(14886708506925131862)
XLA Ops:
  7.2 1.6 broadcast_in_dim.12
  8.7 14.5 %all-to-all-start = ((bf16[4,64,512]{2,1,0:T(8,128)(2,1)}), bf16[4,64,512]{2,1,0:T(8,128)(2,1)S(1)}, u32[]{:S(2)}, u32[]{:S(2)}) async-start(bf16[4,64,512]{2,1,0:T(8,128)(2,1)} %broadcast_in_dim.12), calls=%async_computation | async-start | bytes 524288 | tf_op jit(solution)/shard_map/frozen_gather/all_to_all | solution.py:173
  23.2 3.3 %pack.1 = bf16[192,4608]{1,0:T(8,128)(2,1)} custom-call(s32[1,12]{1,0:T(1,128)} %counts_ref.1, s32[1,192]{1,0:T(1,128)} %packing_ref.1, bf16[192,4096]{1,0:T(8,128)(2,1)} %rows_hbm.1, bf16[192,512]{1,0:T(8,128)(2,1)} %grads_ref.1), custom_call_target="tpu_custom_call" | custom-call | tf_op jit(solution)/shard_map/pack/pallas_call | solution.py:176
  26.5 12.0 %all-to-all-done = bf16[4,64,512]{2,1,0:T(8,128)(2,1)S(1)} async-done(((bf16[4,64,512]{2,1,0:T(8,128)(2,1)}), bf16[4,64,512]{2,1,0:T(8,128)(2,1)S(1)}, u32[]{:S(2)}, u32[]{:S(2)}) %all-to-all-start) | async-done | bytes 262176 | tf_op jit(solution)/shard_map/frozen_gather/all_to_all | solution.py:173
  38.5 0.0 copy-start.5
  38.5 0.0 copy-start
  38.5 0.0 copy-start.1
  38.5 0.7 copy-done.5
  39.2 6.3 %all-to-all-start.1 = ((bf16[12,16,4608]{2,1,0:T(8,128)(2,1)}), bf16[12,16,4608]{2,1,0:T(8,128)(2,1)S(1)}, u32[]{:S(2)}, u32[]{:S(2)}) async-start(bf16[12,16,4608]{2,1,0:T(8,128)(2,1)} %bitcast.24), calls=%async_computation.1 | async-start | bytes 3538944 | tf_op jit(solution)/shard_map/pack/all_to_all | solution.py:193
  45.6 0.0 all-gather.2.cloned.1.call-start
  45.6 0.7 all-gather.2.cloned.1.call-update
  46.3 27.3 %all-to-all-done.1 = bf16[12,16,4608]{2,1,0:T(8,128)(2,1)S(1)} async-done(((bf16[12,16,4608]{2,1,0:T(8,128)(2,1)}), bf16[12,16,4608]{2,1,0:T(8,128)(2,1)S(1)}, u32[]{:S(2)}, u32[]{:S(2)}) %all-to-all-start.1) | async-done | bytes 1769504 | tf_op jit(solution)/shard_map/pack/all_to_all | solution.py:193
  73.6 0.0 copy-done
  73.6 0.0 copy-done.1
  73.6 3.0 %adapters.1 = (bf16[192,4096]{1,0:T(8,128)(2,1)}, f32[8,4,40,128]{3,2,1,0:T(8,128)S(1)}, f32[8,4,40,128]{3,2,1,0:T(8,128)S(1)}) custom-call(s32[1]{0:T(128)} %bitcast.place_ref, bf16[192,4608]{1,0:T(8,128)(2,1)S(1)} %bitcast.19, bf16[64,4096]{1,0:T(8,128)(2,1)S(1)} %bitcast.21, bf16[64,512]{1,0:T(8,128)(2,1)S(1)} %bitcast.22), custom_call_target="tpu_custom_call" | custom-call | tf_op jit(solution)/shard_map/adapters/pallas_call | solution.py:202
  76.6 0.0 copy-start.2
  76.6 0.8 copy-done.2
  77.5 0.0 copy-start.3
  77.5 6.1 %all-to-all-start.2 = ((bf16[12,16,4096]{2,1,0:T(8,128)(2,1)}), bf16[12,16,4096]{2,1,0:T(8,128)(2,1)}, u32[]{:S(2)}, u32[]{:S(2)}) async-start(bf16[12,16,4096]{2,1,0:T(8,128)(2,1)} %bitcast.11), calls=%async_computation.3 | async-start | bytes 3145728 | tf_op jit(solution)/shard_map/adapters/all_to_all | solution.py:210
  83.6 0.0 reduce-scatter.2.cloned.1.call-start
  83.6 0.0 copy-done.3
  83.6 1.9 %collective-permute-start = (f32[1280,128]{1,0:T(8,128)S(1)}, f32[1280,128]{1,0:T(8,128)S(1)}, u32[]{:S(2)}, u32[]{:S(2)}) collective-permute-start(f32[1280,128]{1,0:T(8,128)S(1)} %bitcast.23), channel_id=1, source_target_pairs={{0,12},{12,0},{1,13},{13,1},{2,14},{14,2},{3,15},{15,3},{4,16},{16... | collective-permute-start | bytes 1966088 | tf_op jit(solution)/shard_map/weight_grads/ppermute | solution.py:215
  85.6 2.1 %collective-permute-done.other_ref = f32[1280,128]{1,0:T(8,128)S(1)} collective-permute-done((f32[1280,128]{1,0:T(8,128)S(1)}, f32[1280,128]{1,0:T(8,128)S(1)}, u32[]{:S(2)}, u32[]{:S(2)}) %collective-permute-start) | collective-permute-done | bytes 655392 | tf_op jit(solution)/shard_map/weight_grads/ppermute | solution.py:215
  87.6 0.9 weight_grads.2
  88.5 3.8 %all-gather.2.cloned.1.call-done = bf16[2048,512]{1,0:T(8,128)(2,1)} async-done(((bf16[256,512]{1,0:T(8,128)(2,1)}), bf16[2048,512]{1,0:T(8,128)(2,1)}) %all-gather.2.cloned.1.call-update) | async-done | bytes 2097168 | tf_op jit(solution)/shard_map/pack/all_gather | solution.py:195
  92.3 1.9 %collective-permute-start.1 = (bf16[2048,512]{1,0:T(8,128)(2,1)}, bf16[2048,512]{1,0:T(8,128)(2,1)S(1)}, u32[]{:S(2)}, u32[]{:S(2)}) collective-permute-start(bf16[2048,512]{1,0:T(8,128)(2,1)} %all-gather.2.cloned.1.call-done), channel_id=1, source_target_pairs={{0,12},{12,0},{1,13},{13,1},{2,14},{14,2},{3,15},{15,3},{4,16},{16... | collective-permute-start | bytes 6291464 | tf_op jit(solution)/shard_map/weight_grads/ppermute | solution.py:225
  94.2 0.0 reduce-scatter.2.cloned.1.call-update
  94.3 42.9 %reduce-scatter.2.cloned.1.call-done = f32[160,128]{1,0:T(8,128)} async-done(((f32[1280,128]{1,0:T(8,128)}), f32[160,128]{1,0:T(8,128)}) %reduce-scatter.2.cloned.1.call-update) | async-done | bytes 81936 | tf_op jit(solution)/shard_map/weight_grads/reduce_scatter | solution.py:226
  137.2 0.0 all-to-all-done.2
  137.2 10.1 %all-to-all-start.3 = ((f32[4,40,128]{2,1,0:T(8,128)}), f32[4,40,128]{2,1,0:T(8,128)S(1)}, u32[]{:S(2)}, u32[]{:S(2)}) async-start(f32[4,40,128]{2,1,0:T(8,128)} %bitcast.28), calls=%async_computation.4 | async-start | bytes 163840 | tf_op jit(solution)/shard_map/weight_grads/all_to_all | solution.py:228
  147.3 0.0 collective-permute-done.1
  147.3 0.0 copy-start.4
  147.3 1.3 copy-done.4
  148.6 5.6 %input_grad.1 = bf16[192,4096]{1,0:T(8,128)(2,1)} custom-call(s32[1]{0:T(128)} %bitcast.place_ref, s32[1,12]{1,0:T(1,128)} %counts_ref.1, s32[1,192]{1,0:T(1,128)} %packing_ref.1, bf16[192,512]{1,0:T(8,128)(2,1)} %grads_ref.1, bf16[8,4,64,512]{3,2,1,0:T(8,128)(2,1)} %bitcast.25, bf16[8,4,64,512]{3,2,1,0:T(8,128)(2,1)} %bitcast.26, ...), custom_call_target="tpu_custom_call" | custom-call | tf_op jit(solution)/shard_map/input_grad/pallas_call | solution.py:250
  154.2 3.7 %all-to-all-done.3.got_ref = f32[4,40,128]{2,1,0:T(8,128)S(1)} async-done(((f32[4,40,128]{2,1,0:T(8,128)}), f32[4,40,128]{2,1,0:T(8,128)S(1)}, u32[]{:S(2)}, u32[]{:S(2)}) %all-to-all-start.3) | async-done | bytes 81952 | tf_op jit(solution)/shard_map/weight_grads/all_to_all | solution.py:228
  157.9 0.7 weight_grads.3
Async XLA Ops:
  8.7 29.8 %all-to-all-start = ((bf16[4,64,512]{2,1,0:T(8,128)(2,1)}), bf16[4,64,512]{2,1,0:T(8,128)(2,1)S(1)}, u32[]{:S(2)}, u32[]{:S(2)}) async-start(bf16[4,64,512]{2,1,0:T(8,128)(2,1)} %broadcast_in_dim.12), calls=%async_computation | async-start | bytes 524288 | tf_op jit(solution)/shard_map/frozen_gather/all_to_all | solution.py:173
  38.5 0.7 copy-start.5
  38.5 35.1 %copy-start = (bf16[1,4096,64]{1,2,0:T(8,128)(2,1)S(1)}, bf16[1,4096,64]{1,2,0:T(8,128)(2,1)}, u32[]{:S(2)}) copy-start(bf16[1,4096,64]{1,2,0:T(8,128)(2,1)} %param.10) | copy-start | bytes 1572868
  38.5 35.1 %copy-start.1 = (bf16[1,64,512]{2,1,0:T(8,128)(2,1)S(1)}, bf16[1,64,512]{2,1,0:T(8,128)(2,1)}, u32[]{:S(2)}) copy-start(bf16[1,64,512]{2,1,0:T(8,128)(2,1)} %param.11) | copy-start | bytes 196612
  39.2 34.4 %all-to-all-start.1 = ((bf16[12,16,4608]{2,1,0:T(8,128)(2,1)}), bf16[12,16,4608]{2,1,0:T(8,128)(2,1)S(1)}, u32[]{:S(2)}, u32[]{:S(2)}) async-start(bf16[12,16,4608]{2,1,0:T(8,128)(2,1)} %bitcast.24), calls=%async_computation.1 | async-start | bytes 3538944 | tf_op jit(solution)/shard_map/pack/all_to_all | solution.py:193
  45.6 46.8 %all-gather.2.cloned.1.call-start = ((), (), s32[]{:S(2)}) async-start(), calls=%async_computation.5 | async-start | bytes 2359296 | tf_op jit(solution)/shard_map/pack/all_gather | solution.py:195
  76.6 0.8 copy-start.2
  77.5 6.2 %copy-start.3 = (f32[8,4,40,128]{3,2,1,0:T(8,128)S(1)}, f32[8,4,40,128]{3,2,1,0:T(8,128)}, u32[]{:S(2)}) copy-start(f32[8,4,40,128]{3,2,1,0:T(8,128)} %copy-done.2) | copy-start | bytes 1966084
  77.5 59.7 %all-to-all-start.2 = ((bf16[12,16,4096]{2,1,0:T(8,128)(2,1)}), bf16[12,16,4096]{2,1,0:T(8,128)(2,1)}, u32[]{:S(2)}, u32[]{:S(2)}) async-start(bf16[12,16,4096]{2,1,0:T(8,128)(2,1)} %bitcast.11), calls=%async_computation.3 | async-start | bytes 3145728 | tf_op jit(solution)/shard_map/adapters/all_to_all | solution.py:210
  83.6 53.5 %reduce-scatter.2.cloned.1.call-start = ((), (), s32[]{:S(2)}) async-start(), calls=%async_computation.6 | async-start | bytes 737280 | tf_op jit(solution)/shard_map/weight_grads/reduce_scatter | solution.py:226
  83.6 4.0 %collective-permute-start = (f32[1280,128]{1,0:T(8,128)S(1)}, f32[1280,128]{1,0:T(8,128)S(1)}, u32[]{:S(2)}, u32[]{:S(2)}) collective-permute-start(f32[1280,128]{1,0:T(8,128)S(1)} %bitcast.23), channel_id=1, source_target_pairs={{0,12},{12,0},{1,13},{13,1},{2,14},{14,2},{3,15},{15,3},{4,16},{16... | collective-permute-start | bytes 1966088 | tf_op jit(solution)/shard_map/weight_grads/ppermute | solution.py:215
  92.3 55.0 %collective-permute-start.1 = (bf16[2048,512]{1,0:T(8,128)(2,1)}, bf16[2048,512]{1,0:T(8,128)(2,1)S(1)}, u32[]{:S(2)}, u32[]{:S(2)}) collective-permute-start(bf16[2048,512]{1,0:T(8,128)(2,1)} %all-gather.2.cloned.1.call-done), channel_id=1, source_target_pairs={{0,12},{12,0},{1,13},{13,1},{2,14},{14,2},{3,15},{15,3},{4,16},{16... | collective-permute-start | bytes 6291464 | tf_op jit(solution)/shard_map/weight_grads/ppermute | solution.py:225
  137.2 20.8 %all-to-all-start.3 = ((f32[4,40,128]{2,1,0:T(8,128)}), f32[4,40,128]{2,1,0:T(8,128)S(1)}, u32[]{:S(2)}, u32[]{:S(2)}) async-start(f32[4,40,128]{2,1,0:T(8,128)} %bitcast.28), calls=%async_computation.4 | async-start | bytes 163840 | tf_op jit(solution)/shard_map/weight_grads/all_to_all | solution.py:228
  147.3 1.3 copy-start.4
Sparse Core Ops, SparseCore 0:
  48.8 43.5 all-gather.1
  95.4 41.6 reduce-scatter.1

commit v5 on v4

--- a/solution.py
+++ b/solution.py
@@ -77,6 +77,13 @@
     proj = dot(grads, up_ref[...], NT).astype(jnp.bfloat16)
     total = jnp.zeros((recv_ref.shape[0], rank), jnp.float32)
     step = 1024
+    turn = []
+    for y in range(n_y):
+        apart, at, bit = lax.bitwise_xor(place_ref[1], y), 0, n_y // 2
+        while bit:
+            at = at + (apart % 2) * bit
+            apart, bit = apart // 2, bit // 2
+        turn.append(at)
     for at in range(0, features, step):
         rows = recv_ref[:, at : at + step]
         part = down_t_ref[:, at : at + step]
@@ -89,20 +96,26 @@
             for c in range(2):
                 lo = b * wide + c * half
                 pair.append(jnp.concatenate([down[lo : lo + quarter], down[lo + quarter : lo + half]], axis=1))
-            keep_ref[y, zh, :quarter, :] = jnp.where(first, pair[0], pair[1])
-            send_ref[y, zh, :quarter, :] = jnp.where(first, pair[1], pair[0])
+            keep_ref[turn[y], zh, :quarter, :] = jnp.where(first, pair[0], pair[1])
+            send_ref[turn[y], zh, :quarter, :] = jnp.where(first, pair[1], pair[0])
     up_t = ADAPTER_SCALING * dot(grads, total.astype(jnp.bfloat16), TN)
     up_t = jnp.concatenate([up_t, jnp.zeros_like(up_t)], axis=1)
     few = grads.shape[1] // (2 * blocks)
     for b in range(blocks):
         zh, y = divmod(b, n_y)
         low, high = up_t[2 * b * few : (2 * b + 1) * few], up_t[(2 * b + 1) * few : (2 * b + 2) * few]
-        keep_ref[y, zh, quarter:, :] = jnp.where(first, low, high)
-        send_ref[y, zh, quarter:, :] = jnp.where(first, high, low)
-
-
-def chip_sum_kernel(keep_ref, other_ref, out_ref):
-    out_ref[...] = keep_ref[...] + other_ref[...]
+        keep_ref[turn[y], zh, quarter:, :] = jnp.where(first, low, high)
+        send_ref[turn[y], zh, quarter:, :] = jnp.where(first, high, low)
+
+
+def half_kernel(held_ref, got_ref, keep_ref, send_ref):
+    half = keep_ref.shape[0]
+    keep_ref[...] = held_ref[:half] + got_ref[:half].astype(jnp.float32)
+    send_ref[...] = (held_ref[half:] + got_ref[half:].astype(jnp.float32)).astype(send_ref.dtype)
+
+
+def add_kernel(held_ref, got_ref, out_ref):
+    out_ref[...] = held_ref[...] + got_ref[...].astype(jnp.float32)
 
 
 def last_sum_kernel(got_ref, down_ref, up_t_ref):
@@ -166,11 +179,13 @@
     up = task_up_adapters[0]
     rank = up.shape[0]
     bf16, f32 = jnp.bfloat16, jnp.float32
-    place = lax.axis_index("c").astype(jnp.int32).reshape(1)
+    place = jnp.stack([lax.axis_index("c"), lax.axis_index("y"), lax.axis_index("zh")]).astype(jnp.int32)
 
     with jax.named_scope("frozen_gather"):
-        spread = jnp.broadcast_to(fixed_value_weight[None], (n_zh, part, kv_width))
-        along_z = lax.all_to_all(spread, "zh", 0, 0, tiled=True).reshape(n_zh * part, kv_width)
+        along_z = [fixed_value_weight]
+        for shift in range(1, n_zh):
+            along_z.append(lax.ppermute(fixed_value_weight, "zh", [(i, (i + shift) % n_zh) for i in range(n_zh)]))
+        own = lax.all_gather(jnp.concatenate(along_z, axis=0), "y", axis=0, tiled=True)
 
     with jax.named_scope("pack"):
         packed = pl.pallas_call(
@@ -189,10 +204,9 @@
             ],
             compiler_params=params(WHOLE_VMEM),
         )(live_row_counts, row_packing_order, inputs, output_gradient_rows)
-        packed, along_z = lax.optimization_barrier((packed, along_z))
         recv = lax.all_to_all(packed.reshape(tasks, slot, features + kv_width), DP, 0, 0, tiled=True)
         recv = recv.reshape(per_device, features + kv_width)
-        own = lax.all_gather(along_z, "y", axis=0, tiled=True)
+        recv, *along_z = lax.optimization_barrier((recv, *along_z))
 
     with jax.named_scope("adapters"):
         quarter = features // (4 * blocks)
@@ -211,19 +225,31 @@
         back = back.reshape(per_device, features)
 
     with jax.named_scope("weight_grads"):
-        terms = (blocks * deep, 2 * rank)
-        keep, from_core = keep.reshape(terms), lax.ppermute(send.reshape(terms), "c", [(0, 1), (1, 0)])
-        chip = pl.pallas_call(
-            chip_sum_kernel,
-            out_shape=jax.ShapeDtypeStruct(terms, f32),
+        flat = (n_zh * deep, 2 * rank)
+        held, got = keep.reshape(n_y, *flat), lax.ppermute(send.reshape(n_y, *flat), "c", [(0, 1), (1, 0)])
+        count, apart = n_y, 1
+        while count > 1:
+            count //= 2
+            held, away = pl.pallas_call(
+                half_kernel,
+                out_shape=(jax.ShapeDtypeStruct((count, *flat), f32), jax.ShapeDtypeStruct((count, *flat), bf16)),
+                grid=(1,),
+                in_specs=[one(2 * count, *flat), one(2 * count, *flat)],
+                out_specs=(one(count, *flat), one(count, *flat)),
+                compiler_params=params(),
+            )(held, got)
+            got = lax.ppermute(away, "y", [(i, i ^ apart) for i in range(n_y)])
+            apart *= 2
+        column = pl.pallas_call(
+            add_kernel,
+            out_shape=jax.ShapeDtypeStruct((1, *flat), f32),
             grid=(1,),
-            in_specs=[one(*terms), one(*terms)],
-            out_specs=one(*terms),
+            in_specs=[one(1, *flat), one(1, *flat)],
+            out_specs=one(1, *flat),
             compiler_params=params(),
-        )(keep, from_core)
-        chip, own = lax.optimization_barrier((chip, own))
+        )(held, got)
+        column, own = lax.optimization_barrier((column, own))
         other = lax.ppermute(own, "c", [(0, 1), (1, 0)])
-        column = lax.psum_scatter(chip, "y", scatter_dimension=0, tiled=True)
         column, back = lax.optimization_barrier((column, back))
         shares = lax.all_to_all(column.reshape(n_zh, deep, 2 * rank), "zh", 0, 0, tiled=True)
         down_share, up_t_share = pl.pallas_call(
@@ -245,7 +271,11 @@
         def block(*shape):
             return pl.BlockSpec(shape, lambda i, place: (0,) * len(shape))
 
-        weight_spec = pl.BlockSpec((several, 1, part, kv_width), lambda i, place: (i % halves, i // halves, 0, 0))
+
+        def weight_at(i, place):
+            return i % halves, lax.rem(place[2] - i // halves + n_zh, n_zh), 0, 0
+
+        weight_spec = pl.BlockSpec((several, 1, part, kv_width), weight_at)
         rows_spec = pl.BlockSpec((per_device, wide), lambda i, place: (0, i))
         input_grad = pl.pallas_call(
             final_kernel,

time: 166 us -> 147 us (0.89)
  waiting for transfers between devices: 92.5 us -> 50.3 us
  starting transfers between devices: 41 us -> 63.5 us
  local copies, waits for them, and re-layouts: 4.42 us -> 2.18 us
    reduce_scatter x1 -> x0, waiting for transfers between devices: 42.9 us -> none  [on_device(): column = lax.psum_scatter(chip, 'y', scatter_dimension=0, tiled=True)]
    ppermute x1 -> x7, waiting for transfers between devices: 2.06 us -> 42.8 us  [the longest x3 22.8 us: on_device(): lax.ppermute(fixed_value_weight, 'zh', [(i, (i + shift) % n_zh) for i in...]
    ppermute x1 -> x7, starting transfers between devices: 1.92 us -> 34.4 us  [the longest x3 17.5 us: on_device(): lax.ppermute(fixed_value_weight, 'zh', [(i, (i + shift) % n_zh) for i in...]
    all_to_all x1, waiting for transfers between devices: 27.3 us -> 0.01 us  [on_device(): lax.all_to_all(packed.reshape(tasks, slot, features + kv_width), DP, 0, 0...]
    all_to_all x1 -> x0, starting transfers between devices: 14.5 us -> none  [on_device(): lax.all_to_all(spread, 'zh', 0, 0, tiled=True)]
    all_to_all x1 -> x0, waiting for transfers between devices: 12 us -> none  [on_device(): lax.all_to_all(spread, 'zh', 0, 0, tiled=True)]
    all_to_all x1, starting transfers between devices: 6.34 us -> 13.2 us  [on_device(): lax.all_to_all(packed.reshape(tasks, slot, features + kv_width), DP, 0, 0...]
    all_to_all x1, starting transfers between devices: 10.1 us -> 8.34 us  [on_device(): lax.all_to_all(column.reshape(n_zh, deep, 2 * rank), 'zh', 0, 0, tiled=True)]
  transfers between devices with their start and end apart: 8 -> 12, of which waited for: 6 -> 7; matrix products, arithmetic and copies ran while one was open for 0% -> 1% of each run, Pallas kernels for 8% -> 7%
where the time goes in v5:
time: 147 us; the launch traced here: 146 us
  starting transfers between devices  63.5 us (43%)
  waiting for transfers between devices  50.3 us (34%)
  Pallas kernels  14.6 us (10%)
  between operations  14.2 us (10%)
  local copies, waits for them, and re-layouts  2.18 us (1%)
    ppermute x3, waiting for transfers between devices, on_device(): lax.ppermute(fixed_value_weight, 'zh', [(i, (i + shift) % n_zh) for i in...  22.8 us
    ppermute x3, waiting for transfers between devices, on_device(): got = lax.ppermute(away, 'y', [(i, i ^ apart) for i in range(n_y)])  17.9 us
    ppermute x3, starting transfers between devices, on_device(): lax.ppermute(fixed_value_weight, 'zh', [(i, (i + shift) % n_zh) for i in...  17.5 us
    ppermute x3, starting transfers between devices, on_device(): got = lax.ppermute(away, 'y', [(i, i ^ apart) for i in range(n_y)])  14.9 us
    all_to_all x1, starting transfers between devices, on_device(): lax.all_to_all(packed.reshape(tasks, slot, features + kv_width), DP, 0, 0...  13.2 us
    all_to_all x1, starting transfers between devices, on_device(): lax.all_to_all(column.reshape(n_zh, deep, 2 * rank), 'zh', 0, 0, tiled=True)  8.34 us
    pallas_call x1, Pallas kernels, on_device(): pl.pallas_call(final_kernel, out_shape=jax.ShapeDtypeStruct((per_device,...  6.37 us
    all_to_all x1, starting transfers between devices, on_device(): lax.all_to_all(dx.reshape(tasks, slot, features), DP, 0, 0, tiled=True)  5.73 us
  transfers between devices with their start and end apart: 12, of which 7 were waited for; matrix products, arithmetic and copies ran while one was open for 1% of the time, Pallas kernels for 7%

profile of v5, /device:TPU:6, one launch (start us, length us, event | category | flops | bytes accessed | tf_op | source)
XLA Modules:
  0.0 145.6 jit_solution(15771179519260636263)
XLA Ops:
  7.2 3.3 %pack.1 = bf16[192,4608]{1,0:T(8,128)(2,1)} custom-call(s32[1,12]{1,0:T(1,128)} %counts_ref.1, s32[1,192]{1,0:T(1,128)} %packing_ref.1, bf16[192,4096]{1,0:T(8,128)(2,1)} %rows_hbm.1, bf16[192,512]{1,0:T(8,128)(2,1)} %grads_ref.1), custom_call_target="tpu_custom_call" | custom-call | tf_op jit(solution)/shard_map/pack/pallas_call | solution.py:191
  10.4 0.0 copy-start.6
  10.5 0.0 copy-start
  10.5 0.0 copy-start.1
  10.5 13.2 %all-to-all-start = ((bf16[12,16,4608]{2,1,0:T(8,128)(2,1)}), bf16[12,16,4608]{2,1,0:T(8,128)(2,1)S(1)}, u32[]{:S(2)}, u32[]{:S(2)}) async-start(bf16[12,16,4608]{2,1,0:T(8,128)(2,1)} %bitcast.25), calls=%async_computation | async-start | bytes 3538944 | tf_op jit(solution)/shard_map/pack/all_to_all | solution.py:207
  23.7 0.0 all-gather.2.cloned.1.call-start
  23.7 0.0 copy-done.6
  23.7 8.1 %collective-permute-start.2 = (bf16[64,512]{1,0:T(8,128)(2,1)S(1)}, bf16[64,512]{1,0:T(8,128)(2,1)S(1)}, u32[]{:S(2)}, u32[]{:S(2)}) collective-permute-start(bf16[64,512]{1,0:T(8,128)(2,1)S(1)} %copy-done.6), channel_id=1, source_target_pairs={{0,576},{192,0},{384,192},{576,384},{1,577},{193,1},{385,193},{577... | collective-permute-start | bytes 196616 | tf_op jit(solution)/shard_map/frozen_gather/ppermute | solution.py:187
  31.8 3.3 %collective-permute-start.1 = (bf16[64,512]{1,0:T(8,128)(2,1)S(1)}, bf16[64,512]{1,0:T(8,128)(2,1)S(1)}, u32[]{:S(2)}, u32[]{:S(2)}) collective-permute-start(bf16[64,512]{1,0:T(8,128)(2,1)S(1)} %copy-done.6), channel_id=1, source_target_pairs={{0,384},{192,576},{384,0},{576,192},{1,385},{193,577},{385,1},{577... | collective-permute-start | bytes 196616 | tf_op jit(solution)/shard_map/frozen_gather/ppermute | solution.py:187
  35.1 6.1 %collective-permute-start = (bf16[64,512]{1,0:T(8,128)(2,1)S(1)}, bf16[64,512]{1,0:T(8,128)(2,1)S(1)}, u32[]{:S(2)}, u32[]{:S(2)}) collective-permute-start(bf16[64,512]{1,0:T(8,128)(2,1)S(1)} %copy-done.6), channel_id=1, source_target_pairs={{0,192},{192,384},{384,576},{576,0},{1,193},{193,385},{385,577},{5... | collective-permute-start | bytes 196616 | tf_op jit(solution)/shard_map/frozen_gather/ppermute | solution.py:187
  41.2 0.0 collective-permute-done.2
  41.3 22.8 %collective-permute-done.1 = bf16[64,512]{1,0:T(8,128)(2,1)S(1)} collective-permute-done((bf16[64,512]{1,0:T(8,128)(2,1)S(1)}, bf16[64,512]{1,0:T(8,128)(2,1)S(1)}, u32[]{:S(2)}, u32[]{:S(2)}) %collective-permute-start.1) | collective-permute-done | bytes 65568 | tf_op jit(solution)/shard_map/frozen_gather/ppermute | solution.py:187
  64.1 0.0 collective-permute-done
  64.1 0.7 pad_maximum_fusion
  64.8 0.0 all-gather.2.cloned.1.call-update
  64.8 0.1 pad_add_fusion.place_ref
  64.9 0.0 copy-start.2
  64.9 0.0 all-to-all-done
  64.9 0.0 copy-done
  64.9 0.0 copy-done.1
  64.9 3.5 %adapters.1 = (bf16[192,4096]{1,0:T(8,128)(2,1)}, f32[8,4,40,128]{3,2,1,0:T(8,128)S(1)}, f32[8,4,40,128]{3,2,1,0:T(8,128)S(1)}) custom-call(s32[3]{0:T(128)S(1)} %pad_add_fusion.place_ref, bf16[192,4608]{1,0:T(8,128)(2,1)S(1)} %bitcast.20, bf16[64,4096]{1,0:T(8,128)(2,1)S(1)} %bitcast.22, bf16[64,512]{1,0:T(8,128)(2,1)S(1)} %bitcast.23), custom_call_target="tpu_custom_call" | custom-call | tf_op jit(solution)/shard_map/adapters/pallas_call | solution.py:216
  68.5 0.0 copy-start.3
  68.5 0.8 copy-done.3
  69.3 0.0 copy-start.4
  69.3 0.0 copy-done.2
  69.3 5.7 %all-to-all-start.1 = ((bf16[12,16,4096]{2,1,0:T(8,128)(2,1)}), bf16[12,16,4096]{2,1,0:T(8,128)(2,1)}, u32[]{:S(2)}, u32[]{:S(2)}) async-start(bf16[12,16,4096]{2,1,0:T(8,128)(2,1)} %bitcast.12), calls=%async_computation.1 | async-start | bytes 3145728 | tf_op jit(solution)/shard_map/adapters/all_to_all | solution.py:224
  75.0 0.0 copy-done.4
  75.0 1.9 %collective-permute-start.3 = (f32[8,160,128]{2,1,0:T(8,128)S(1)}, f32[8,160,128]{2,1,0:T(8,128)S(1)}, u32[]{:S(2)}, u32[]{:S(2)}) collective-permute-start(f32[8,160,128]{2,1,0:T(8,128)S(1)} %bitcast.24), channel_id=1, source_target_pairs={{0,12},{12,0},{1,13},{13,1},{2,14},{14,2},{3,15},{15,3},{4,16},{16... | collective-permute-start | bytes 1966088 | tf_op jit(solution)/shard_map/weight_grads/ppermute | solution.py:229
  77.0 2.1 %collective-permute-done.3.got_ref = f32[8,160,128]{2,1,0:T(8,128)S(1)} collective-permute-done((f32[8,160,128]{2,1,0:T(8,128)S(1)}, f32[8,160,128]{2,1,0:T(8,128)S(1)}, u32[]{:S(2)}, u32[]{:S(2)}) %collective-permute-start.3) | collective-permute-done | bytes 655392 | tf_op jit(solution)/shard_map/weight_grads/ppermute | solution.py:229
  79.0 0.1 weight_grads.5
  79.1 3.5 %collective-permute-start.4 = (bf16[4,160,128]{2,1,0:T(8,128)(2,1)S(1)}, bf16[4,160,128]{2,1,0:T(8,128)(2,1)S(1)}, u32[]{:S(2)}, u32[]{:S(2)}) collective-permute-start(bf16[4,160,128]{2,1,0:T(8,128)(2,1)S(1)} %get-tuple-element.23), channel_id=1, source_target_pairs={{0,24},{24,0},{48,72},{72,48},{96,120},{120,96},{144,168},{168,144... | collective-permute-start | bytes 491528 | tf_op jit(solution)/shard_map/weight_grads/ppermute | solution.py:241
  82.6 8.5 %collective-permute-done.4.got_ref = bf16[4,160,128]{2,1,0:T(8,128)(2,1)S(1)} collective-permute-done((bf16[4,160,128]{2,1,0:T(8,128)(2,1)S(1)}, bf16[4,160,128]{2,1,0:T(8,128)(2,1)S(1)}, u32[]{:S(2)}, u32[]{:S(2)}) %collective-permute-start.4) | collective-permute-done | bytes 163872 | tf_op jit(solution)/shard_map/weight_grads/ppermute | solution.py:241
  91.2 4.2 %collective-permute-start.5 = (bf16[2,160,128]{2,1,0:T(8,128)(2,1)S(1)}, bf16[2,160,128]{2,1,0:T(8,128)(2,1)S(1)}, u32[]{:S(2)}, u32[]{:S(2)}) collective-permute-start(bf16[2,160,128]{2,1,0:T(8,128)(2,1)S(1)} %get-tuple-element.25), channel_id=1, source_target_pairs={{0,48},{24,72},{48,0},{72,24},{96,144},{120,168},{144,96},{168,120... | collective-permute-start | bytes 245768 | tf_op jit(solution)/shard_map/weight_grads/ppermute | solution.py:241
  95.3 6.6 %collective-permute-done.5.got_ref = bf16[2,160,128]{2,1,0:T(8,128)(2,1)S(1)} collective-permute-done((bf16[2,160,128]{2,1,0:T(8,128)(2,1)S(1)}, bf16[2,160,128]{2,1,0:T(8,128)(2,1)S(1)}, u32[]{:S(2)}, u32[]{:S(2)}) %collective-permute-start.5) | collective-permute-done | bytes 81952 | tf_op jit(solution)/shard_map/weight_grads/ppermute | solution.py:241
  101.9 7.3 %collective-permute-start.6 = (bf16[1,160,128]{2,1,0:T(8,128)(2,1)S(1)}, bf16[1,160,128]{2,1,0:T(8,128)(2,1)S(1)}, u32[]{:S(2)}, u32[]{:S(2)}) collective-permute-start(bf16[1,160,128]{2,1,0:T(8,128)(2,1)S(1)} %get-tuple-element.27), channel_id=1, source_target_pairs={{0,96},{24,120},{48,144},{72,168},{96,0},{120,24},{144,48},{168,72... | collective-permute-start | bytes 122888 | tf_op jit(solution)/shard_map/weight_grads/ppermute | solution.py:241
  109.2 2.8 %collective-permute-done.6.got_ref = bf16[1,160,128]{2,1,0:T(8,128)(2,1)S(1)} collective-permute-done((bf16[1,160,128]{2,1,0:T(8,128)(2,1)S(1)}, bf16[1,160,128]{2,1,0:T(8,128)(2,1)S(1)}, u32[]{:S(2)}, u32[]{:S(2)}) %collective-permute-start.6) | collective-permute-done | bytes 40992 | tf_op jit(solution)/shard_map/weight_grads/ppermute | solution.py:241
  112.0 0.6 weight_grads.8
  112.7 3.5 %all-gather.2.cloned.1.call-done = bf16[2048,512]{1,0:T(8,128)(2,1)} async-done(((bf16[256,512]{1,0:T(8,128)(2,1)}), bf16[2048,512]{1,0:T(8,128)(2,1)}) %all-gather.2.cloned.1.call-update) | async-done | bytes 2097168 | tf_op jit(solution)/shard_map/frozen_gather/all_gather | solution.py:188
  116.2 1.9 %collective-permute-start.7 = (bf16[2048,512]{1,0:T(8,128)(2,1)}, bf16[2048,512]{1,0:T(8,128)(2,1)S(1)}, u32[]{:S(2)}, u32[]{:S(2)}) collective-permute-start(bf16[2048,512]{1,0:T(8,128)(2,1)} %all-gather.2.cloned.1.call-done), channel_id=1, source_target_pairs={{0,12},{12,0},{1,13},{13,1},{2,14},{14,2},{3,15},{15,3},{4,16},{16... | collective-permute-start | bytes 6291464 | tf_op jit(solution)/shard_map/weight_grads/ppermute | solution.py:252
  118.1 0.0 all-to-all-done.1
  118.1 8.3 %all-to-all-start.2 = ((f32[4,40,128]{2,1,0:T(8,128)}), f32[4,40,128]{2,1,0:T(8,128)S(1)}, u32[]{:S(2)}, u32[]{:S(2)}) async-start(f32[4,40,128]{2,1,0:T(8,128)} %bitcast.14), calls=%async_computation.2 | async-start | bytes 163840 | tf_op jit(solution)/shard_map/weight_grads/all_to_all | solution.py:254
  126.5 0.0 collective-permute-done.7
  126.5 0.0 copy-start.5
  126.5 1.3 copy-done.5
  127.8 6.4 %input_grad.1 = bf16[192,4096]{1,0:T(8,128)(2,1)} custom-call(s32[3]{0:T(128)} %copy-done.2, s32[1,12]{1,0:T(1,128)} %counts_ref.1, s32[1,192]{1,0:T(1,128)} %packing_ref.1, bf16[192,512]{1,0:T(8,128)(2,1)} %grads_ref.1, bf16[8,4,64,512]{3,2,1,0:T(8,128)(2,1)} %bitcast.26, bf16[8,4,64,512]{3,2,1,0:T(8,128)(2,1)} %bitcast.27, bf16[192,4096]{1,0:T(8,128)(2,1)} %bitcast.13.back_ref), custom_call_target="tpu_custom_call" | custom-call | tf_op jit(solution)/shard_map/input_grad/pallas_call | solution.py:280
  134.2 3.9 %all-to-all-done.2.got_ref = f32[4,40,128]{2,1,0:T(8,128)S(1)} async-done(((f32[4,40,128]{2,1,0:T(8,128)}), f32[4,40,128]{2,1,0:T(8,128)S(1)}, u32[]{:S(2)}, u32[]{:S(2)}) %all-to-all-start.2) | async-done | bytes 81952 | tf_op jit(solution)/shard_map/weight_grads/all_to_all | solution.py:254
  138.1 0.7 weight_grads.9
  (2 shorter events, 0.0 us)
Async XLA Ops:
  10.4 13.2 %copy-start.6 = (bf16[64,512]{1,0:T(8,128)(2,1)S(1)}, bf16[64,512]{1,0:T(8,128)(2,1)}, u32[]{:S(2)}) copy-start(bf16[64,512]{1,0:T(8,128)(2,1)} %param.9) | copy-start | bytes 196612
  10.5 54.5 %copy-start = (bf16[1,4096,64]{1,2,0:T(8,128)(2,1)S(1)}, bf16[1,4096,64]{1,2,0:T(8,128)(2,1)}, u32[]{:S(2)}) copy-start(bf16[1,4096,64]{1,2,0:T(8,128)(2,1)} %param.10) | copy-start | bytes 1572868
  10.5 54.4 %copy-start.1 = (bf16[1,64,512]{2,1,0:T(8,128)(2,1)S(1)}, bf16[1,64,512]{2,1,0:T(8,128)(2,1)}, u32[]{:S(2)}) copy-start(bf16[1,64,512]{2,1,0:T(8,128)(2,1)} %param.11) | copy-start | bytes 196612
  10.5 54.4 %all-to-all-start = ((bf16[12,16,4608]{2,1,0:T(8,128)(2,1)}), bf16[12,16,4608]{2,1,0:T(8,128)(2,1)S(1)}, u32[]{:S(2)}, u32[]{:S(2)}) async-start(bf16[12,16,4608]{2,1,0:T(8,128)(2,1)} %bitcast.25), calls=%async_computation | async-start | bytes 3538944 | tf_op jit(solution)/shard_map/pack/all_to_all | solution.py:207
  23.7 92.5 %all-gather.2.cloned.1.call-start = ((), (), s32[]{:S(2)}) async-start(), calls=%async_computation.3 | async-start | bytes 2359296 | tf_op jit(solution)/shard_map/frozen_gather/all_gather | solution.py:188
  23.7 17.6 %collective-permute-start.2 = (bf16[64,512]{1,0:T(8,128)(2,1)S(1)}, bf16[64,512]{1,0:T(8,128)(2,1)S(1)}, u32[]{:S(2)}, u32[]{:S(2)}) collective-permute-start(bf16[64,512]{1,0:T(8,128)(2,1)S(1)} %copy-done.6), channel_id=1, source_target_pairs={{0,576},{192,0},{384,192},{576,384},{1,577},{193,1},{385,193},{577... | collective-permute-start | bytes 196616 | tf_op jit(solution)/shard_map/frozen_gather/ppermute | solution.py:187
  31.8 32.3 %collective-permute-start.1 = (bf16[64,512]{1,0:T(8,128)(2,1)S(1)}, bf16[64,512]{1,0:T(8,128)(2,1)S(1)}, u32[]{:S(2)}, u32[]{:S(2)}) collective-permute-start(bf16[64,512]{1,0:T(8,128)(2,1)S(1)} %copy-done.6), channel_id=1, source_target_pairs={{0,384},{192,576},{384,0},{576,192},{1,385},{193,577},{385,1},{577... | collective-permute-start | bytes 196616 | tf_op jit(solution)/shard_map/frozen_gather/ppermute | solution.py:187
  35.1 28.9 %collective-permute-start = (bf16[64,512]{1,0:T(8,128)(2,1)S(1)}, bf16[64,512]{1,0:T(8,128)(2,1)S(1)}, u32[]{:S(2)}, u32[]{:S(2)}) collective-permute-start(bf16[64,512]{1,0:T(8,128)(2,1)S(1)} %copy-done.6), channel_id=1, source_target_pairs={{0,192},{192,384},{384,576},{576,0},{1,193},{193,385},{385,577},{5... | collective-permute-start | bytes 196616 | tf_op jit(solution)/shard_map/frozen_gather/ppermute | solution.py:187
  64.9 4.4 %copy-start.2 = (s32[3]{0:T(128)}, s32[3]{0:T(128)S(1)}, u32[]{:S(2)}) copy-start(s32[3]{0:T(128)S(1)} %pad_add_fusion.place_ref) | copy-start | bytes 40
  68.5 0.8 copy-start.3
  69.3 5.7 %copy-start.4 = (f32[8,4,40,128]{3,2,1,0:T(8,128)S(1)}, f32[8,4,40,128]{3,2,1,0:T(8,128)}, u32[]{:S(2)}) copy-start(f32[8,4,40,128]{3,2,1,0:T(8,128)} %copy-done.3) | copy-start | bytes 1966084
  69.3 48.8 %all-to-all-start.1 = ((bf16[12,16,4096]{2,1,0:T(8,128)(2,1)}), bf16[12,16,4096]{2,1,0:T(8,128)(2,1)}, u32[]{:S(2)}, u32[]{:S(2)}) async-start(bf16[12,16,4096]{2,1,0:T(8,128)(2,1)} %bitcast.12), calls=%async_computation.1 | async-start | bytes 3145728 | tf_op jit(solution)/shard_map/adapters/all_to_all | solution.py:224
  75.0 4.0 %collective-permute-start.3 = (f32[8,160,128]{2,1,0:T(8,128)S(1)}, f32[8,160,128]{2,1,0:T(8,128)S(1)}, u32[]{:S(2)}, u32[]{:S(2)}) collective-permute-start(f32[8,160,128]{2,1,0:T(8,128)S(1)} %bitcast.24), channel_id=1, source_target_pairs={{0,12},{12,0},{1,13},{13,1},{2,14},{14,2},{3,15},{15,3},{4,16},{16... | collective-permute-start | bytes 1966088 | tf_op jit(solution)/shard_map/weight_grads/ppermute | solution.py:229
  79.1 12.0 %collective-permute-start.4 = (bf16[4,160,128]{2,1,0:T(8,128)(2,1)S(1)}, bf16[4,160,128]{2,1,0:T(8,128)(2,1)S(1)}, u32[]{:S(2)}, u32[]{:S(2)}) collective-permute-start(bf16[4,160,128]{2,1,0:T(8,128)(2,1)S(1)} %get-tuple-element.23), channel_id=1, source_target_pairs={{0,24},{24,0},{48,72},{72,48},{96,120},{120,96},{144,168},{168,144... | collective-permute-start | bytes 491528 | tf_op jit(solution)/shard_map/weight_grads/ppermute | solution.py:241
  91.2 10.8 %collective-permute-start.5 = (bf16[2,160,128]{2,1,0:T(8,128)(2,1)S(1)}, bf16[2,160,128]{2,1,0:T(8,128)(2,1)S(1)}, u32[]{:S(2)}, u32[]{:S(2)}) collective-permute-start(bf16[2,160,128]{2,1,0:T(8,128)(2,1)S(1)} %get-tuple-element.25), channel_id=1, source_target_pairs={{0,48},{24,72},{48,0},{72,24},{96,144},{120,168},{144,96},{168,120... | collective-permute-start | bytes 245768 | tf_op jit(solution)/shard_map/weight_grads/ppermute | solution.py:241
  101.9 10.1 %collective-permute-start.6 = (bf16[1,160,128]{2,1,0:T(8,128)(2,1)S(1)}, bf16[1,160,128]{2,1,0:T(8,128)(2,1)S(1)}, u32[]{:S(2)}, u32[]{:S(2)}) collective-permute-start(bf16[1,160,128]{2,1,0:T(8,128)(2,1)S(1)} %get-tuple-element.27), channel_id=1, source_target_pairs={{0,96},{24,120},{48,144},{72,168},{96,0},{120,24},{144,48},{168,72... | collective-permute-start | bytes 122888 | tf_op jit(solution)/shard_map/weight_grads/ppermute | solution.py:241
  116.2 10.3 %collective-permute-start.7 = (bf16[2048,512]{1,0:T(8,128)(2,1)}, bf16[2048,512]{1,0:T(8,128)(2,1)S(1)}, u32[]{:S(2)}, u32[]{:S(2)}) collective-permute-start(bf16[2048,512]{1,0:T(8,128)(2,1)} %all-gather.2.cloned.1.call-done), channel_id=1, source_target_pairs={{0,12},{12,0},{1,13},{13,1},{2,14},{14,2},{3,15},{15,3},{4,16},{16... | collective-permute-start | bytes 6291464 | tf_op jit(solution)/shard_map/weight_grads/ppermute | solution.py:252
  118.1 19.9 %all-to-all-start.2 = ((f32[4,40,128]{2,1,0:T(8,128)}), f32[4,40,128]{2,1,0:T(8,128)S(1)}, u32[]{:S(2)}, u32[]{:S(2)}) async-start(f32[4,40,128]{2,1,0:T(8,128)} %bitcast.14), calls=%async_computation.2 | async-start | bytes 163840 | tf_op jit(solution)/shard_map/weight_grads/all_to_all | solution.py:254
  126.5 1.3 copy-start.5
Sparse Core Ops, SparseCore 0:
  64.9 51.2 all-gather.1

commit v6 on v4

--- a/solution.py
+++ b/solution.py
@@ -9,7 +9,7 @@
 from jax.sharding import Mesh, PartitionSpec as P
 
 ADAPTER_SCALING = 2.0
-FSDP = ("zh", "y", "c")
+FSDP = ("zh", "yh", "yl", "c")
 DP = ("zl", "x")
 VMEM_LIMIT = 16 * 1024 * 1024
 WHOLE_VMEM = 60 * 1024 * 1024
@@ -67,8 +67,7 @@
 
 def adapter_kernel(place_ref, recv_ref, down_t_ref, up_ref, dx_ref, keep_ref, send_ref):
     rank, features = down_t_ref.shape
-    n_y, n_zh = keep_ref.shape[:2]
-    blocks = n_y * n_zh
+    blocks = 2 * keep_ref.shape[1]
     first = place_ref[0] == 0
     wide = features // blocks
     half = wide // 2
@@ -77,6 +76,7 @@
     proj = dot(grads, up_ref[...], NT).astype(jnp.bfloat16)
     total = jnp.zeros((recv_ref.shape[0], rank), jnp.float32)
     step = 1024
+    turn = [lax.bitwise_xor(place_ref[1], yl) for yl in range(2)]
     for at in range(0, features, step):
         rows = recv_ref[:, at : at + step]
         part = down_t_ref[:, at : at + step]
@@ -84,48 +84,47 @@
         total = total + dot(rows, part, NT)
         down = ADAPTER_SCALING * dot(rows, proj, TN)
         for b in range(step // wide):
-            zh, y = divmod(at // wide + b, n_y)
+            pair_at, yl = divmod(at // wide + b, 2)
             pair = []
             for c in range(2):
                 lo = b * wide + c * half
                 pair.append(jnp.concatenate([down[lo : lo + quarter], down[lo + quarter : lo + half]], axis=1))
-            keep_ref[y, zh, :quarter, :] = jnp.where(first, pair[0], pair[1])
-            send_ref[y, zh, :quarter, :] = jnp.where(first, pair[1], pair[0])
+            keep_ref[turn[yl], pair_at, :quarter, :] = jnp.where(first, pair[0], pair[1])
+            send_ref[turn[yl], pair_at, :quarter, :] = jnp.where(first, pair[1], pair[0])
     up_t = ADAPTER_SCALING * dot(grads, total.astype(jnp.bfloat16), TN)
     up_t = jnp.concatenate([up_t, jnp.zeros_like(up_t)], axis=1)
     few = grads.shape[1] // (2 * blocks)
     for b in range(blocks):
-        zh, y = divmod(b, n_y)
+        pair_at, yl = divmod(b, 2)
         low, high = up_t[2 * b * few : (2 * b + 1) * few], up_t[(2 * b + 1) * few : (2 * b + 2) * few]
-        keep_ref[y, zh, quarter:, :] = jnp.where(first, low, high)
-        send_ref[y, zh, quarter:, :] = jnp.where(first, high, low)
-
-
-def chip_sum_kernel(keep_ref, other_ref, out_ref):
-    out_ref[...] = keep_ref[...] + other_ref[...]
+        keep_ref[turn[yl], pair_at, quarter:, :] = jnp.where(first, low, high)
+        send_ref[turn[yl], pair_at, quarter:, :] = jnp.where(first, high, low)
+
+
+def half_kernel(held_ref, got_ref, keep_ref, send_ref):
+    keep_ref[...] = held_ref[0] + got_ref[0]
+    send_ref[...] = (held_ref[1] + got_ref[1]).astype(send_ref.dtype)
+
+
+def add_kernel(held_ref, got_ref, out_ref):
+    out_ref[...] = (held_ref[...] + got_ref[...].astype(jnp.float32)).astype(out_ref.dtype)
 
 
 def last_sum_kernel(got_ref, down_ref, up_t_ref):
     half, rank = down_ref.shape
     quarter = half // 2
-    total = jnp.sum(got_ref[...], axis=0)
+    total = jnp.sum(got_ref[...].astype(jnp.float32), axis=0)
     down_ref[:quarter, :] = total[:quarter, :rank]
     down_ref[quarter:, :] = total[:quarter, rank:]
     up_t_ref[...] = total[quarter:, :rank]
 
 
-def final_kernel(place_ref, counts_ref, packing_ref, grads_ref, own_ref, other_ref, back_ref, out_ref, chosen_ref):
+def final_kernel(counts_ref, packing_ref, grads_ref, weight_ref, back_ref, out_ref, chosen_ref):
     @pl.when(pl.program_id(0) == 0)
     def _():
         chosen_ref[...] = live_one_hot(counts_ref, packing_ref)
 
-    first = place_ref[0] == 0
-    several, _, part, depth = own_ref.shape
-    own, other = own_ref[:, 0], other_ref[:, 0]
-    low = jnp.where(first, own, other)
-    high = jnp.where(first, other, own)
-    weight = jnp.concatenate([low, high], axis=1).reshape(several * 2 * part, depth)
-    frozen = dot(grads_ref[...], weight, NT).astype(jnp.bfloat16)
+    frozen = dot(grads_ref[...], weight_ref[...], NT).astype(jnp.bfloat16)
     placed = dot(chosen_ref[...], back_ref[...], NN)
     out_ref[...] = (frozen.astype(jnp.float32) + placed).astype(jnp.bfloat16)
 
@@ -159,18 +158,17 @@
     kv_width = output_gradient_rows.shape[1]
     tasks = lax.axis_size("zl") * lax.axis_size("x")
     slot = per_device // tasks
-    n_zh, n_y = lax.axis_size("zh"), lax.axis_size("y")
-    blocks = n_zh * n_y
-    part = fixed_value_weight.shape[0]
+    n_zh, n_yh = lax.axis_size("zh"), lax.axis_size("yh")
+    pairs = n_zh * n_yh
+    blocks = 2 * pairs
     down_t = task_down_adapters[0].T
     up = task_up_adapters[0]
     rank = up.shape[0]
     bf16, f32 = jnp.bfloat16, jnp.float32
-    place = lax.axis_index("c").astype(jnp.int32).reshape(1)
+    place = jnp.stack([lax.axis_index("c"), lax.axis_index("yl")]).astype(jnp.int32)
 
     with jax.named_scope("frozen_gather"):
-        spread = jnp.broadcast_to(fixed_value_weight[None], (n_zh, part, kv_width))
-        along_z = lax.all_to_all(spread, "zh", 0, 0, tiled=True).reshape(n_zh * part, kv_width)
+        weight = lax.all_gather(fixed_value_weight, FSDP, axis=0, tiled=True)
 
     with jax.named_scope("pack"):
         packed = pl.pallas_call(
@@ -189,16 +187,14 @@
             ],
             compiler_params=params(WHOLE_VMEM),
         )(live_row_counts, row_packing_order, inputs, output_gradient_rows)
-        packed, along_z = lax.optimization_barrier((packed, along_z))
         recv = lax.all_to_all(packed.reshape(tasks, slot, features + kv_width), DP, 0, 0, tiled=True)
         recv = recv.reshape(per_device, features + kv_width)
-        own = lax.all_gather(along_z, "y", axis=0, tiled=True)
 
     with jax.named_scope("adapters"):
         quarter = features // (4 * blocks)
         few = kv_width // (2 * blocks)
         deep = quarter + few
-        terms = jax.ShapeDtypeStruct((n_y, n_zh, deep, 2 * rank), f32)
+        terms = jax.ShapeDtypeStruct((2, pairs, deep, 2 * rank), f32)
         dx, keep, send = pl.pallas_call(
             adapter_kernel,
             out_shape=(jax.ShapeDtypeStruct((per_device, features), bf16), terms, terms),
@@ -211,73 +207,58 @@
         back = back.reshape(per_device, features)
 
     with jax.named_scope("weight_grads"):
-        terms = (blocks * deep, 2 * rank)
-        keep, from_core = keep.reshape(terms), lax.ppermute(send.reshape(terms), "c", [(0, 1), (1, 0)])
-        chip = pl.pallas_call(
-            chip_sum_kernel,
-            out_shape=jax.ShapeDtypeStruct(terms, f32),
-            grid=(1,),
-            in_specs=[one(*terms), one(*terms)],
-            out_specs=one(*terms),
-            compiler_params=params(),
-        )(keep, from_core)
-        chip, own = lax.optimization_barrier((chip, own))
-        other = lax.ppermute(own, "c", [(0, 1), (1, 0)])
-        column = lax.psum_scatter(chip, "y", scatter_dimension=0, tiled=True)
+        flat = (pairs * deep, 2 * rank)
+        held, got = keep.reshape(2, *flat), lax.ppermute(send.reshape(2, *flat), "c", [(0, 1), (1, 0)])
+        held, away = pl.pallas_call(
+            half_kernel,
+            out_shape=(jax.ShapeDtypeStruct(flat, f32), jax.ShapeDtypeStruct(flat, bf16)),
+            grid=(1,),
+            in_specs=[one(2, *flat), one(2, *flat)],
+            out_specs=(one(*flat), one(*flat)),
+            compiler_params=params(),
+        )(held, got)
+        column = pl.pallas_call(
+            add_kernel,
+            out_shape=jax.ShapeDtypeStruct(flat, bf16),
+            grid=(1,),
+            in_specs=[one(*flat), one(*flat)],
+            out_specs=one(*flat),
+            compiler_params=params(),
+        )(held, lax.ppermute(away, "yl", [(0, 1), (1, 0)]))
         column, back = lax.optimization_barrier((column, back))
-        shares = lax.all_to_all(column.reshape(n_zh, deep, 2 * rank), "zh", 0, 0, tiled=True)
+        shares = lax.all_to_all(column.reshape(pairs, deep, 2 * rank), ("zh", "yh"), 0, 0, tiled=True)
         down_share, up_t_share = pl.pallas_call(
             last_sum_kernel,
             out_shape=(jax.ShapeDtypeStruct((2 * quarter, rank), f32), jax.ShapeDtypeStruct((few, rank), f32)),
             grid=(1,),
-            in_specs=[one(n_zh, deep, 2 * rank)],
+            in_specs=[one(pairs, deep, 2 * rank)],
             out_specs=(one(2 * quarter, rank), one(few, rank)),
             compiler_params=params(),
         )(shares)
         up_share = up_t_share.T
 
     with jax.named_scope("input_grad"):
-        halves = 1
-        several = n_y // halves
-        wide = several * 2 * part
-        order = (n_y, n_zh, part, kv_width)
-
-        def block(*shape):
-            return pl.BlockSpec(shape, lambda i, place: (0,) * len(shape))
-
-        weight_spec = pl.BlockSpec((several, 1, part, kv_width), lambda i, place: (i % halves, i // halves, 0, 0))
-        rows_spec = pl.BlockSpec((per_device, wide), lambda i, place: (0, i))
+        wide = features // 4
+        rows_spec = pl.BlockSpec((per_device, wide), lambda i: (0, i))
         input_grad = pl.pallas_call(
             final_kernel,
             out_shape=jax.ShapeDtypeStruct((per_device, features), bf16),
-            grid_spec=pltpu.PrefetchScalarGridSpec(
-                num_scalar_prefetch=1,
-                grid=(features // wide,),
-                in_specs=[
-                    scalars(),
-                    block(1, per_device),
-                    block(per_device, kv_width),
-                    weight_spec,
-                    weight_spec,
-                    rows_spec,
-                ],
-                out_specs=rows_spec,
-                scratch_shapes=[pltpu.VMEM((per_device, per_device), bf16)],
-            ),
+            grid=(features // wide,),
+            in_specs=[
+                scalars(),
+                one(1, per_device),
+                one(per_device, kv_width),
+                pl.BlockSpec((wide, kv_width), lambda i: (i, 0)),
+                rows_spec,
+            ],
+            out_specs=rows_spec,
+            scratch_shapes=[pltpu.VMEM((per_device, per_device), bf16)],
             compiler_params=params(WHOLE_VMEM),
-        )(
-            place,
-            live_row_counts,
-            row_packing_order,
-            output_gradient_rows,
-            own.reshape(order),
-            other.reshape(order),
-            back,
-        )
+        )(live_row_counts, row_packing_order, output_gradient_rows, weight, back)
     return (input_grad, down_share[None], up_share[None])
 
 
-def solution(mesh, parts=(4, 8, 2, 3, 4)):
+def solution(mesh, parts=(4, 4, 2, 2, 3, 4)):
     fine = Mesh(np.asarray(mesh.devices).reshape(parts), FSDP + DP)
     rows = P(FSDP + DP, None)
     in_specs = (

time: 166 us -> 158 us (0.952)
  waiting for transfers between devices: 92.5 us -> 82.4 us
  starting transfers between devices: 41 us -> 45.2 us
  local copies, waits for them, and re-layouts: 4.42 us -> 0.86 us
    reduce_scatter x1 -> x0, waiting for transfers between devices: 42.9 us -> none  [on_device(): column = lax.psum_scatter(chip, 'y', scatter_dimension=0, tiled=True)]
    all_gather x1, waiting for transfers between devices: 3.78 us -> 38.2 us  [on_device(): weight = lax.all_gather(fixed_value_weight, FSDP, axis=0, tiled=True)]
    all_to_all x2 -> x1, waiting for transfers between devices: 15.7 us -> 0.01 us  [on_device(): lax.all_to_all(column.reshape(pairs, deep, 2 * rank), ('zh', 'yh'), 0, 0,...]
    all_to_all x1, waiting for transfers between devices: 0.01 us -> 13 us  [on_device(): lax.all_to_all(dx.reshape(tasks, slot, features), DP, 0, 0, tiled=True)]
    all_to_all x1, starting transfers between devices: 6.34 us -> 13.2 us  [on_device(): lax.all_to_all(packed.reshape(tasks, slot, features + kv_width), DP, 0, 0...]
    ppermute x2, waiting for transfers between devices: 2.07 us -> 7.05 us  [the longest x1 4.98 us: on_device(): lax.ppermute(away, 'yl', [(0, 1), (1, 0)])]
    all_to_all x2 -> x1, starting transfers between devices: 24.6 us -> 20.4 us  [on_device(): lax.all_to_all(column.reshape(pairs, deep, 2 * rank), ('zh', 'yh'), 0, 0,...]
    all_to_all x1, waiting for transfers between devices: 27.3 us -> 23.4 us  [on_device(): lax.all_to_all(packed.reshape(tasks, slot, features + kv_width), DP, 0, 0...]
  transfers between devices with their start and end apart: 8 -> 6, of which waited for: 6 -> 5; matrix products, arithmetic and copies ran while one was open for 0% -> 0% of each run, Pallas kernels for 8% -> 6%
where the time goes in v6:
time: 158 us; the launch traced here: 157 us
  waiting for transfers between devices  82.4 us (52%)
  starting transfers between devices  45.2 us (29%)
  between operations  14.1 us (9%)
  Pallas kernels  13.9 us (9%)
    all_gather x1, waiting for transfers between devices, on_device(): weight = lax.all_gather(fixed_value_weight, FSDP, axis=0, tiled=True)  38.2 us
    all_to_all x1, waiting for transfers between devices, on_device(): lax.all_to_all(packed.reshape(tasks, slot, features + kv_width), DP, 0, 0...  23.4 us
    all_to_all x1, starting transfers between devices, on_device(): lax.all_to_all(column.reshape(pairs, deep, 2 * rank), ('zh', 'yh'), 0, 0,...  20.4 us
    all_to_all x1, starting transfers between devices, on_device(): lax.all_to_all(packed.reshape(tasks, slot, features + kv_width), DP, 0, 0...  13.2 us
    all_to_all x1, waiting for transfers between devices, on_device(): lax.all_to_all(dx.reshape(tasks, slot, features), DP, 0, 0, tiled=True)  13 us
    all_to_all x1, starting transfers between devices, on_device(): lax.all_to_all(dx.reshape(tasks, slot, features), DP, 0, 0, tiled=True)  6.14 us
    pallas_call x1, Pallas kernels, on_device(): pl.pallas_call(final_kernel, out_shape=jax.ShapeDtypeStruct((per_device,...  5.62 us
    ppermute x1, waiting for transfers between devices, on_device(): lax.ppermute(away, 'yl', [(0, 1), (1, 0)])  4.98 us
  transfers between devices with their start and end apart: 6, of which 5 were waited for; matrix products, arithmetic and copies ran while one was open for 0% of the time, Pallas kernels for 6%

profile of v6, /device:TPU:6, one launch (start us, length us, event | category | flops | bytes accessed | tf_op | source)
XLA Modules:
  0.0 156.5 jit_solution(12973341378431169596)
XLA Ops:
  7.2 3.3 %pack.1 = bf16[192,4608]{1,0:T(8,128)(2,1)} custom-call(s32[1,12]{1,0:T(1,128)} %counts_ref.1, s32[1,192]{1,0:T(1,128)} %packing_ref.1, bf16[192,4096]{1,0:T(8,128)(2,1)} %rows_hbm.1, bf16[192,512]{1,0:T(8,128)(2,1)} %grads_ref.1), custom_call_target="tpu_custom_call" | custom-call | tf_op jit(solution)/shard_map/pack/pallas_call | solution.py:174
  10.4 0.0 copy-start
  10.4 0.0 copy-start.1
  10.4 13.2 %all-to-all-start = ((bf16[12,16,4608]{2,1,0:T(8,128)(2,1)}), bf16[12,16,4608]{2,1,0:T(8,128)(2,1)S(1)}, u32[]{:S(2)}, u32[]{:S(2)}) async-start(bf16[12,16,4608]{2,1,0:T(8,128)(2,1)} %bitcast.22), calls=%async_computation | async-start | bytes 3538944 | tf_op jit(solution)/shard_map/pack/all_to_all | solution.py:190
  23.7 0.0 all-gather.2.cloned.1.call-start
  23.7 0.7 all-gather.2.cloned.1.call-update
  24.4 0.1 pad_add_fusion.place_ref
  24.5 23.4 %all-to-all-done = bf16[12,16,4608]{2,1,0:T(8,128)(2,1)S(1)} async-done(((bf16[12,16,4608]{2,1,0:T(8,128)(2,1)}), bf16[12,16,4608]{2,1,0:T(8,128)(2,1)S(1)}, u32[]{:S(2)}, u32[]{:S(2)}) %all-to-all-start) | async-done | bytes 1769504 | tf_op jit(solution)/shard_map/pack/all_to_all | solution.py:190
  47.9 0.0 copy-done
  47.9 0.0 copy-done.1
  47.9 3.5 %adapters.1 = (bf16[192,4096]{1,0:T(8,128)(2,1)}, f32[2,16,40,128]{3,2,1,0:T(8,128)S(1)}, f32[2,16,40,128]{3,2,1,0:T(8,128)S(1)}) custom-call(s32[2]{0:T(128)S(1)} %pad_add_fusion.place_ref, bf16[192,4608]{1,0:T(8,128)(2,1)S(1)} %bitcast.17, bf16[64,4096]{1,0:T(8,128)(2,1)S(1)} %bitcast.19, bf16[64,512]{1,0:T(8,128)(2,1)S(1)} %bitcast.20), custom_call_target="tpu_custom_call" | custom-call | tf_op jit(solution)/shard_map/adapters/pallas_call | solution.py:198
  51.4 0.0 copy-start.2
  51.4 0.8 copy-done.2
  52.3 0.0 copy-start.3
  52.3 6.1 %all-to-all-start.1 = ((bf16[12,16,4096]{2,1,0:T(8,128)(2,1)}), bf16[12,16,4096]{2,1,0:T(8,128)(2,1)}, u32[]{:S(2)}, u32[]{:S(2)}) async-start(bf16[12,16,4096]{2,1,0:T(8,128)(2,1)} %bitcast.9), calls=%async_computation.1 | async-start | bytes 3145728 | tf_op jit(solution)/shard_map/adapters/all_to_all | solution.py:206
  58.4 0.0 copy-done.3
  58.4 1.9 %collective-permute-start = (f32[2,640,128]{2,1,0:T(8,128)S(1)}, f32[2,640,128]{2,1,0:T(8,128)S(1)}, u32[]{:S(2)}, u32[]{:S(2)}) collective-permute-start(f32[2,640,128]{2,1,0:T(8,128)S(1)} %bitcast.21), channel_id=1, source_target_pairs={{0,12},{12,0},{1,13},{13,1},{2,14},{14,2},{3,15},{15,3},{4,16},{16... | collective-permute-start | bytes 1966088 | tf_op jit(solution)/shard_map/weight_grads/ppermute | solution.py:211
  60.4 2.1 %collective-permute-done.got_ref = f32[2,640,128]{2,1,0:T(8,128)S(1)} collective-permute-done((f32[2,640,128]{2,1,0:T(8,128)S(1)}, f32[2,640,128]{2,1,0:T(8,128)S(1)}, u32[]{:S(2)}, u32[]{:S(2)}) %collective-permute-start) | collective-permute-done | bytes 655392 | tf_op jit(solution)/shard_map/weight_grads/ppermute | solution.py:211
  62.4 0.1 weight_grads.3
  62.5 3.6 %collective-permute-start.1 = (bf16[640,128]{1,0:T(8,128)(2,1)S(1)}, bf16[640,128]{1,0:T(8,128)(2,1)S(1)}, u32[]{:S(2)}, u32[]{:S(2)}) collective-permute-start(bf16[640,128]{1,0:T(8,128)(2,1)S(1)} %get-tuple-element.15), channel_id=1, source_target_pairs={{0,24},{24,0},{1,25},{25,1},{2,26},{26,2},{3,27},{27,3},{4,28},{28... | collective-permute-start | bytes 491528 | tf_op jit(solution)/shard_map/weight_grads/ppermute | solution.py:227
  66.1 5.0 %collective-permute-done.1.got_ref = bf16[640,128]{1,0:T(8,128)(2,1)S(1)} collective-permute-done((bf16[640,128]{1,0:T(8,128)(2,1)S(1)}, bf16[640,128]{1,0:T(8,128)(2,1)S(1)}, u32[]{:S(2)}, u32[]{:S(2)}) %collective-permute-start.1) | collective-permute-done | bytes 163872 | tf_op jit(solution)/shard_map/weight_grads/ppermute | solution.py:227
  71.1 0.7 weight_grads.4
  71.8 13.0 %all-to-all-done.1 = bf16[12,16,4096]{2,1,0:T(8,128)(2,1)} async-done(((bf16[12,16,4096]{2,1,0:T(8,128)(2,1)}), bf16[12,16,4096]{2,1,0:T(8,128)(2,1)}, u32[]{:S(2)}, u32[]{:S(2)}) %all-to-all-start.1) | async-done | bytes 1572896 | tf_op jit(solution)/shard_map/adapters/all_to_all | solution.py:206
  84.8 20.4 %all-to-all-start.2 = ((bf16[16,40,128]{2,1,0:T(8,128)(2,1)}), bf16[16,40,128]{2,1,0:T(8,128)(2,1)S(1)}, u32[]{:S(2)}, u32[]{:S(2)}) async-start(bf16[16,40,128]{2,1,0:T(8,128)(2,1)} %bitcast.11), calls=%async_computation.2 | async-start | bytes 327680 | tf_op jit(solution)/shard_map/weight_grads/all_to_all | solution.py:229
  105.2 38.2 %all-gather.2.cloned.1.call-done.weight_ref = bf16[4096,512]{1,0:T(8,128)(2,1)} async-done(((bf16[64,512]{1,0:T(8,128)(2,1)}), bf16[4096,512]{1,0:T(8,128)(2,1)}) %all-gather.2.cloned.1.call-update) | async-done | bytes 4194320 | tf_op jit(solution)/shard_map/frozen_gather/all_gather | solution.py:171
  143.4 5.6 %input_grad.1 = bf16[192,4096]{1,0:T(8,128)(2,1)} custom-call(s32[1,12]{1,0:T(1,128)} %counts_ref.1, s32[1,192]{1,0:T(1,128)} %packing_ref.1, bf16[192,512]{1,0:T(8,128)(2,1)} %grads_ref.1, bf16[4096,512]{1,0:T(8,128)(2,1)} %all-gather.2.cloned.1.call-done.weight_ref, bf16[192,4096]{1,0:T(8,128)(2,1)} %bitcast.10.back_ref), custom_call_target="tpu_custom_call" | custom-call | tf_op jit(solution)/shard_map/input_grad/pallas_call | solution.py:243
  149.0 0.0 all-to-all-done.2.got_ref
  149.0 0.7 weight_grads.5
Async XLA Ops:
  10.4 37.5 %copy-start = (bf16[1,4096,64]{1,2,0:T(8,128)(2,1)S(1)}, bf16[1,4096,64]{1,2,0:T(8,128)(2,1)}, u32[]{:S(2)}) copy-start(bf16[1,4096,64]{1,2,0:T(8,128)(2,1)} %param.10) | copy-start | bytes 1572868
  10.4 37.5 %copy-start.1 = (bf16[1,64,512]{2,1,0:T(8,128)(2,1)S(1)}, bf16[1,64,512]{2,1,0:T(8,128)(2,1)}, u32[]{:S(2)}) copy-start(bf16[1,64,512]{2,1,0:T(8,128)(2,1)} %param.11) | copy-start | bytes 196612
  10.4 37.5 %all-to-all-start = ((bf16[12,16,4608]{2,1,0:T(8,128)(2,1)}), bf16[12,16,4608]{2,1,0:T(8,128)(2,1)S(1)}, u32[]{:S(2)}, u32[]{:S(2)}) async-start(bf16[12,16,4608]{2,1,0:T(8,128)(2,1)} %bitcast.22), calls=%async_computation | async-start | bytes 3538944 | tf_op jit(solution)/shard_map/pack/all_to_all | solution.py:190
  23.7 119.7 %all-gather.2.cloned.1.call-start = ((), (), s32[]{:S(2)}) async-start(), calls=%async_computation.3 | async-start | bytes 4259840 | tf_op jit(solution)/shard_map/frozen_gather/all_gather | solution.py:171
  51.4 0.8 copy-start.2
  52.3 6.1 %copy-start.3 = (f32[2,16,40,128]{3,2,1,0:T(8,128)S(1)}, f32[2,16,40,128]{3,2,1,0:T(8,128)}, u32[]{:S(2)}) copy-start(f32[2,16,40,128]{3,2,1,0:T(8,128)} %copy-done.2) | copy-start | bytes 1966084
  52.3 32.5 %all-to-all-start.1 = ((bf16[12,16,4096]{2,1,0:T(8,128)(2,1)}), bf16[12,16,4096]{2,1,0:T(8,128)(2,1)}, u32[]{:S(2)}, u32[]{:S(2)}) async-start(bf16[12,16,4096]{2,1,0:T(8,128)(2,1)} %bitcast.9), calls=%async_computation.1 | async-start | bytes 3145728 | tf_op jit(solution)/shard_map/adapters/all_to_all | solution.py:206
  58.4 4.0 %collective-permute-start = (f32[2,640,128]{2,1,0:T(8,128)S(1)}, f32[2,640,128]{2,1,0:T(8,128)S(1)}, u32[]{:S(2)}, u32[]{:S(2)}) collective-permute-start(f32[2,640,128]{2,1,0:T(8,128)S(1)} %bitcast.21), channel_id=1, source_target_pairs={{0,12},{12,0},{1,13},{13,1},{2,14},{14,2},{3,15},{15,3},{4,16},{16... | collective-permute-start | bytes 1966088 | tf_op jit(solution)/shard_map/weight_grads/ppermute | solution.py:211
  62.5 8.6 %collective-permute-start.1 = (bf16[640,128]{1,0:T(8,128)(2,1)S(1)}, bf16[640,128]{1,0:T(8,128)(2,1)S(1)}, u32[]{:S(2)}, u32[]{:S(2)}) collective-permute-start(bf16[640,128]{1,0:T(8,128)(2,1)S(1)} %get-tuple-element.15), channel_id=1, source_target_pairs={{0,24},{24,0},{1,25},{25,1},{2,26},{26,2},{3,27},{27,3},{4,28},{28... | collective-permute-start | bytes 491528 | tf_op jit(solution)/shard_map/weight_grads/ppermute | solution.py:227
  84.8 64.2 %all-to-all-start.2 = ((bf16[16,40,128]{2,1,0:T(8,128)(2,1)}), bf16[16,40,128]{2,1,0:T(8,128)(2,1)S(1)}, u32[]{:S(2)}, u32[]{:S(2)}) async-start(bf16[16,40,128]{2,1,0:T(8,128)(2,1)} %bitcast.11), calls=%async_computation.2 | async-start | bytes 327680 | tf_op jit(solution)/shard_map/weight_grads/all_to_all | solution.py:229
Sparse Core Ops, SparseCore 0:
  28.4 114.8 all-gather.1

commit v7 on v6

--- a/solution.py
+++ b/solution.py
@@ -119,12 +119,18 @@
     up_t_ref[...] = total[quarter:, :rank]
 
 
-def final_kernel(counts_ref, packing_ref, grads_ref, weight_ref, back_ref, out_ref, chosen_ref):
+def final_kernel(place_ref, counts_ref, packing_ref, grads_ref, own_ref, other_ref, back_ref, out_ref, chosen_ref):
     @pl.when(pl.program_id(0) == 0)
     def _():
         chosen_ref[...] = live_one_hot(counts_ref, packing_ref)
 
-    frozen = dot(grads_ref[...], weight_ref[...], NT).astype(jnp.bfloat16)
+    first = place_ref[0] == 0
+    several, _, part, depth = own_ref.shape
+    own, other = own_ref[:, 0], other_ref[:, 0]
+    low = jnp.where(first, own, other)
+    high = jnp.where(first, other, own)
+    weight = jnp.concatenate([low, high], axis=1).reshape(several * 2 * part, depth)
+    frozen = dot(grads_ref[...], weight, NT).astype(jnp.bfloat16)
     placed = dot(chosen_ref[...], back_ref[...], NN)
     out_ref[...] = (frozen.astype(jnp.float32) + placed).astype(jnp.bfloat16)
 
@@ -161,6 +167,7 @@
     n_zh, n_yh = lax.axis_size("zh"), lax.axis_size("yh")
     pairs = n_zh * n_yh
     blocks = 2 * pairs
+    part = fixed_value_weight.shape[0]
     down_t = task_down_adapters[0].T
     up = task_up_adapters[0]
     rank = up.shape[0]
@@ -168,7 +175,8 @@
     place = jnp.stack([lax.axis_index("c"), lax.axis_index("yl")]).astype(jnp.int32)
 
     with jax.named_scope("frozen_gather"):
-        weight = lax.all_gather(fixed_value_weight, FSDP, axis=0, tiled=True)
+        spread = jnp.broadcast_to(fixed_value_weight[None], (n_zh, part, kv_width))
+        along_z = lax.all_to_all(spread, "zh", 0, 0, tiled=True).reshape(n_zh * part, kv_width)
 
     with jax.named_scope("pack"):
         packed = pl.pallas_call(
@@ -187,6 +195,8 @@
             ],
             compiler_params=params(WHOLE_VMEM),
         )(live_row_counts, row_packing_order, inputs, output_gradient_rows)
+        packed, along_z = lax.optimization_barrier((packed, along_z))
+        own = lax.all_gather(along_z, ("yh", "yl"), axis=0, tiled=True)
         recv = lax.all_to_all(packed.reshape(tasks, slot, features + kv_width), DP, 0, 0, tiled=True)
         recv = recv.reshape(per_device, features + kv_width)
 
@@ -225,6 +235,8 @@
             out_specs=one(*flat),
             compiler_params=params(),
         )(held, lax.ppermute(away, "yl", [(0, 1), (1, 0)]))
+        column, own = lax.optimization_barrier((column, own))
+        other = lax.ppermute(own, "c", [(0, 1), (1, 0)])
         column, back = lax.optimization_barrier((column, back))
         shares = lax.all_to_all(column.reshape(pairs, deep, 2 * rank), ("zh", "yh"), 0, 0, tiled=True)
         down_share, up_t_share = pl.pallas_call(
@@ -238,23 +250,42 @@
         up_share = up_t_share.T
 
     with jax.named_scope("input_grad"):
-        wide = features // 4
-        rows_spec = pl.BlockSpec((per_device, wide), lambda i: (0, i))
+        n_y = 2 * n_yh
+        wide = n_y * 2 * part
+        order = (n_y, n_zh, part, kv_width)
+
+        def block(*shape):
+            return pl.BlockSpec(shape, lambda i, place: (0,) * len(shape))
+
+        weight_spec = pl.BlockSpec((n_y, 1, part, kv_width), lambda i, place: (0, i, 0, 0))
+        rows_spec = pl.BlockSpec((per_device, wide), lambda i, place: (0, i))
         input_grad = pl.pallas_call(
             final_kernel,
             out_shape=jax.ShapeDtypeStruct((per_device, features), bf16),
-            grid=(features // wide,),
-            in_specs=[
-                scalars(),
-                one(1, per_device),
-                one(per_device, kv_width),
-                pl.BlockSpec((wide, kv_width), lambda i: (i, 0)),
-                rows_spec,
-            ],
-            out_specs=rows_spec,
-            scratch_shapes=[pltpu.VMEM((per_device, per_device), bf16)],
+            grid_spec=pltpu.PrefetchScalarGridSpec(
+                num_scalar_prefetch=1,
+                grid=(features // wide,),
+                in_specs=[
+                    scalars(),
+                    block(1, per_device),
+                    block(per_device, kv_width),
+                    weight_spec,
+                    weight_spec,
+                    rows_spec,
+                ],
+                out_specs=rows_spec,
+                scratch_shapes=[pltpu.VMEM((per_device, per_device), bf16)],
+            ),
             compiler_params=params(WHOLE_VMEM),
-        )(live_row_counts, row_packing_order, output_gradient_rows, weight, back)
+        )(
+            place,
+            live_row_counts,
+            row_packing_order,
+            output_gradient_rows,
+            own.reshape(order),
+            other.reshape(order),
+            back,
+        )
     return (input_grad, down_share[None], up_share[None])
 
 

time: 158 us -> 143 us (0.905)
  waiting for transfers between devices: 82.4 us -> 64.2 us
  local copies, waits for them, and re-layouts: 0.86 us -> 4.41 us
    all_gather x1, waiting for transfers between devices: 38.2 us -> 0.01 us  [on_device(): own = lax.all_gather(along_z, ('yh', 'yl'), axis=0, tiled=True)]
    all_to_all x0 -> x1, starting transfers between devices: none -> 14.5 us  [on_device(): lax.all_to_all(spread, 'zh', 0, 0, tiled=True)]
    all_to_all x0 -> x1, waiting for transfers between devices: none -> 12 us  [on_device(): lax.all_to_all(spread, 'zh', 0, 0, tiled=True)]
    all_to_all x1, starting transfers between devices: 20.4 us -> 11 us  [on_device(): lax.all_to_all(column.reshape(pairs, deep, 2 * rank), ('zh', 'yh'), 0, 0,...]
    all_to_all x1, waiting for transfers between devices: 0.01 us -> 7.37 us  [on_device(): lax.all_to_all(column.reshape(pairs, deep, 2 * rank), ('zh', 'yh'), 0, 0,...]
    all_to_all x1, starting transfers between devices: 13.2 us -> 6.34 us  [on_device(): lax.all_to_all(packed.reshape(tasks, slot, features + kv_width), DP, 0, 0...]
    all_to_all x1, waiting for transfers between devices: 23.4 us -> 27.2 us  [on_device(): lax.all_to_all(packed.reshape(tasks, slot, features + kv_width), DP, 0, 0...]
    all_to_all x1, waiting for transfers between devices: 13 us -> 10.1 us  [on_device(): lax.all_to_all(dx.reshape(tasks, slot, features), DP, 0, 0, tiled=True)]
  transfers between devices with their start and end apart: 6 -> 8, of which waited for: 5 -> 6; matrix products, arithmetic and copies ran while one was open for 0% -> 0% of each run, Pallas kernels for 6% -> 10%
where the time goes in v7:
time: 143 us
  waiting for transfers between devices  64.2 us (45%)
  starting transfers between devices  45.3 us (32%)
  Pallas kernels  14.6 us (10%)
  between operations  14.1 us (10%)
  local copies, waits for them, and re-layouts  4.41 us (3%)
    all_to_all x1, waiting for transfers between devices, on_device(): lax.all_to_all(packed.reshape(tasks, slot, features + kv_width), DP, 0, 0...  27.2 us
    all_to_all x1, starting transfers between devices, on_device(): lax.all_to_all(spread, 'zh', 0, 0, tiled=True)  14.5 us
    all_to_all x1, waiting for transfers between devices, on_device(): lax.all_to_all(spread, 'zh', 0, 0, tiled=True)  12 us
    all_to_all x1, starting transfers between devices, on_device(): lax.all_to_all(column.reshape(pairs, deep, 2 * rank), ('zh', 'yh'), 0, 0,...  11 us
    all_to_all x1, waiting for transfers between devices, on_device(): lax.all_to_all(dx.reshape(tasks, slot, features), DP, 0, 0, tiled=True)  10.1 us
    all_to_all x1, waiting for transfers between devices, on_device(): lax.all_to_all(column.reshape(pairs, deep, 2 * rank), ('zh', 'yh'), 0, 0,...  7.37 us
    all_to_all x1, starting transfers between devices, on_device(): lax.all_to_all(packed.reshape(tasks, slot, features + kv_width), DP, 0, 0...  6.34 us
    pallas_call x1, Pallas kernels, on_device(): pl.pallas_call(final_kernel, out_shape=jax.ShapeDtypeStruct((per_device,...  6.33 us
  transfers between devices with their start and end apart: 8, of which 6 were waited for; matrix products, arithmetic and copies ran while one was open for 0% of the time, Pallas kernels for 10%

profile of v7, /device:TPU:6, one launch (start us, length us, event | category | flops | bytes accessed | tf_op | source)
XLA Modules:
  0.0 142.7 jit_solution(11681542222165045723)
XLA Ops:
  7.2 1.6 %broadcast_in_dim.12 = bf16[4,64,512]{2,1,0:T(8,128)(2,1)} broadcast(bf16[64,512]{1,0:T(8,128)(2,1)} %param.9), dimensions={1,2} | broadcast | bytes 327680 | tf_op jit(solution)/shard_map/frozen_gather/broadcast_in_dim | solution.py:178
  8.7 14.5 %all-to-all-start = ((bf16[4,64,512]{2,1,0:T(8,128)(2,1)}), bf16[4,64,512]{2,1,0:T(8,128)(2,1)S(1)}, u32[]{:S(2)}, u32[]{:S(2)}) async-start(bf16[4,64,512]{2,1,0:T(8,128)(2,1)} %broadcast_in_dim.12), calls=%async_computation | async-start | bytes 524288 | tf_op jit(solution)/shard_map/frozen_gather/all_to_all | solution.py:179
  23.2 3.3 %pack.1 = bf16[192,4608]{1,0:T(8,128)(2,1)} custom-call(s32[1,12]{1,0:T(1,128)} %counts_ref.1, s32[1,192]{1,0:T(1,128)} %packing_ref.1, bf16[192,4096]{1,0:T(8,128)(2,1)} %rows_hbm.1, bf16[192,512]{1,0:T(8,128)(2,1)} %grads_ref.1), custom_call_target="tpu_custom_call" | custom-call | tf_op jit(solution)/shard_map/pack/pallas_call | solution.py:182
  26.5 12.0 %all-to-all-done = bf16[4,64,512]{2,1,0:T(8,128)(2,1)S(1)} async-done(((bf16[4,64,512]{2,1,0:T(8,128)(2,1)}), bf16[4,64,512]{2,1,0:T(8,128)(2,1)S(1)}, u32[]{:S(2)}, u32[]{:S(2)}) %all-to-all-start) | async-done | bytes 262176 | tf_op jit(solution)/shard_map/frozen_gather/all_to_all | solution.py:179
  38.5 0.0 copy-start.6
  38.5 0.0 copy-start
  38.5 0.0 copy-start.1
  38.5 0.7 copy-done.6
  39.2 6.3 %all-to-all-start.1 = ((bf16[12,16,4608]{2,1,0:T(8,128)(2,1)}), bf16[12,16,4608]{2,1,0:T(8,128)(2,1)S(1)}, u32[]{:S(2)}, u32[]{:S(2)}) async-start(bf16[12,16,4608]{2,1,0:T(8,128)(2,1)} %bitcast.25), calls=%async_computation.1 | async-start | bytes 3538944 | tf_op jit(solution)/shard_map/pack/all_to_all | solution.py:200
  45.6 0.0 all-gather.2.cloned.1.call-start
  45.6 0.7 all-gather.2.cloned.1.call-update
  46.3 0.1 pad_add_fusion.place_ref
  46.4 0.0 copy-start.2
  46.4 27.2 %all-to-all-done.1 = bf16[12,16,4608]{2,1,0:T(8,128)(2,1)S(1)} async-done(((bf16[12,16,4608]{2,1,0:T(8,128)(2,1)}), bf16[12,16,4608]{2,1,0:T(8,128)(2,1)S(1)}, u32[]{:S(2)}, u32[]{:S(2)}) %all-to-all-start.1) | async-done | bytes 1769504 | tf_op jit(solution)/shard_map/pack/all_to_all | solution.py:200
  73.6 0.0 copy-done
  73.6 0.0 copy-done.1
  73.6 3.5 %adapters.1 = (bf16[192,4096]{1,0:T(8,128)(2,1)}, f32[2,16,40,128]{3,2,1,0:T(8,128)S(1)}, f32[2,16,40,128]{3,2,1,0:T(8,128)S(1)}) custom-call(s32[2]{0:T(128)S(1)} %pad_add_fusion.place_ref, bf16[192,4608]{1,0:T(8,128)(2,1)S(1)} %bitcast.20, bf16[64,4096]{1,0:T(8,128)(2,1)S(1)} %bitcast.22, bf16[64,512]{1,0:T(8,128)(2,1)S(1)} %bitcast.23), custom_call_target="tpu_custom_call" | custom-call | tf_op jit(solution)/shard_map/adapters/pallas_call | solution.py:208
  77.2 0.0 copy-start.3
  77.2 0.9 copy-done.3
  78.0 0.0 copy-start.4
  78.0 0.0 copy-done.2
  78.0 6.2 %all-to-all-start.2 = ((bf16[12,16,4096]{2,1,0:T(8,128)(2,1)}), bf16[12,16,4096]{2,1,0:T(8,128)(2,1)}, u32[]{:S(2)}, u32[]{:S(2)}) async-start(bf16[12,16,4096]{2,1,0:T(8,128)(2,1)} %bitcast.12), calls=%async_computation.2 | async-start | bytes 3145728 | tf_op jit(solution)/shard_map/adapters/all_to_all | solution.py:216
  84.2 0.0 copy-done.4
  84.2 1.9 %collective-permute-start = (f32[2,640,128]{2,1,0:T(8,128)S(1)}, f32[2,640,128]{2,1,0:T(8,128)S(1)}, u32[]{:S(2)}, u32[]{:S(2)}) collective-permute-start(f32[2,640,128]{2,1,0:T(8,128)S(1)} %bitcast.24), channel_id=1, source_target_pairs={{0,12},{12,0},{1,13},{13,1},{2,14},{14,2},{3,15},{15,3},{4,16},{16... | collective-permute-start | bytes 1966088 | tf_op jit(solution)/shard_map/weight_grads/ppermute | solution.py:221
  86.1 2.1 %collective-permute-done.got_ref = f32[2,640,128]{2,1,0:T(8,128)S(1)} collective-permute-done((f32[2,640,128]{2,1,0:T(8,128)S(1)}, f32[2,640,128]{2,1,0:T(8,128)S(1)}, u32[]{:S(2)}, u32[]{:S(2)}) %collective-permute-start) | collective-permute-done | bytes 655392 | tf_op jit(solution)/shard_map/weight_grads/ppermute | solution.py:221
  88.2 0.1 weight_grads.3
  88.2 3.5 %collective-permute-start.1 = (bf16[640,128]{1,0:T(8,128)(2,1)S(1)}, bf16[640,128]{1,0:T(8,128)(2,1)S(1)}, u32[]{:S(2)}, u32[]{:S(2)}) collective-permute-start(bf16[640,128]{1,0:T(8,128)(2,1)S(1)} %get-tuple-element.20), channel_id=1, source_target_pairs={{0,24},{24,0},{1,25},{25,1},{2,26},{26,2},{3,27},{27,3},{4,28},{28... | collective-permute-start | bytes 491528 | tf_op jit(solution)/shard_map/weight_grads/ppermute | solution.py:237
  91.7 4.6 %collective-permute-done.1.got_ref = bf16[640,128]{1,0:T(8,128)(2,1)S(1)} collective-permute-done((bf16[640,128]{1,0:T(8,128)(2,1)S(1)}, bf16[640,128]{1,0:T(8,128)(2,1)S(1)}, u32[]{:S(2)}, u32[]{:S(2)}) %collective-permute-start.1) | collective-permute-done | bytes 163872 | tf_op jit(solution)/shard_map/weight_grads/ppermute | solution.py:237
  96.4 0.7 weight_grads.4
  97.1 0.0 all-gather.2.cloned.1.call-done
  97.1 1.9 %collective-permute-start.2 = (bf16[2048,512]{1,0:T(8,128)(2,1)}, bf16[2048,512]{1,0:T(8,128)(2,1)S(1)}, u32[]{:S(2)}, u32[]{:S(2)}) collective-permute-start(bf16[2048,512]{1,0:T(8,128)(2,1)} %all-gather.2.cloned.1.call-done), channel_id=1, source_target_pairs={{0,12},{12,0},{1,13},{13,1},{2,14},{14,2},{3,15},{15,3},{4,16},{16... | collective-permute-start | bytes 6291464 | tf_op jit(solution)/shard_map/weight_grads/ppermute | solution.py:239
  99.0 10.1 %all-to-all-done.2 = bf16[12,16,4096]{2,1,0:T(8,128)(2,1)} async-done(((bf16[12,16,4096]{2,1,0:T(8,128)(2,1)}), bf16[12,16,4096]{2,1,0:T(8,128)(2,1)}, u32[]{:S(2)}, u32[]{:S(2)}) %all-to-all-start.2) | async-done | bytes 1572896 | tf_op jit(solution)/shard_map/adapters/all_to_all | solution.py:216
  109.1 11.0 %all-to-all-start.3 = ((bf16[16,40,128]{2,1,0:T(8,128)(2,1)}), bf16[16,40,128]{2,1,0:T(8,128)(2,1)S(1)}, u32[]{:S(2)}, u32[]{:S(2)}) async-start(bf16[16,40,128]{2,1,0:T(8,128)(2,1)} %bitcast.14), calls=%async_computation.3 | async-start | bytes 327680 | tf_op jit(solution)/shard_map/weight_grads/all_to_all | solution.py:241
  120.1 0.0 collective-permute-done.2
  120.1 0.0 copy-start.5
  120.1 1.3 copy-done.5
  121.4 6.3 %input_grad.1 = bf16[192,4096]{1,0:T(8,128)(2,1)} custom-call(s32[2]{0:T(128)} %copy-done.2, s32[1,12]{1,0:T(1,128)} %counts_ref.1, s32[1,192]{1,0:T(1,128)} %packing_ref.1, bf16[192,512]{1,0:T(8,128)(2,1)} %grads_ref.1, bf16[8,4,64,512]{3,2,1,0:T(8,128)(2,1)} %bitcast.26, bf16[8,4,64,512]{3,2,1,0:T(8,128)(2,1)} %bitcast.27, bf16[192,4096]{1,0:T(8,128)(2,1)} %bitcast.13.back_ref), custom_call_target="tpu_custom_call" | custom-call | tf_op jit(solution)/shard_map/input_grad/pallas_call | solution.py:262
  127.7 7.4 %all-to-all-done.3.got_ref = bf16[16,40,128]{2,1,0:T(8,128)(2,1)S(1)} async-done(((bf16[16,40,128]{2,1,0:T(8,128)(2,1)}), bf16[16,40,128]{2,1,0:T(8,128)(2,1)S(1)}, u32[]{:S(2)}, u32[]{:S(2)}) %all-to-all-start.3) | async-done | bytes 163872 | tf_op jit(solution)/shard_map/weight_grads/all_to_all | solution.py:241
  135.1 0.7 weight_grads.5
Async XLA Ops:
  8.7 29.8 %all-to-all-start = ((bf16[4,64,512]{2,1,0:T(8,128)(2,1)}), bf16[4,64,512]{2,1,0:T(8,128)(2,1)S(1)}, u32[]{:S(2)}, u32[]{:S(2)}) async-start(bf16[4,64,512]{2,1,0:T(8,128)(2,1)} %broadcast_in_dim.12), calls=%async_computation | async-start | bytes 524288 | tf_op jit(solution)/shard_map/frozen_gather/all_to_all | solution.py:179
  38.5 0.7 copy-start.6
  38.5 35.1 %copy-start = (bf16[1,4096,64]{1,2,0:T(8,128)(2,1)S(1)}, bf16[1,4096,64]{1,2,0:T(8,128)(2,1)}, u32[]{:S(2)}) copy-start(bf16[1,4096,64]{1,2,0:T(8,128)(2,1)} %param.10) | copy-start | bytes 1572868
  38.5 35.1 %copy-start.1 = (bf16[1,64,512]{2,1,0:T(8,128)(2,1)S(1)}, bf16[1,64,512]{2,1,0:T(8,128)(2,1)}, u32[]{:S(2)}) copy-start(bf16[1,64,512]{2,1,0:T(8,128)(2,1)} %param.11) | copy-start | bytes 196612
  39.2 34.4 %all-to-all-start.1 = ((bf16[12,16,4608]{2,1,0:T(8,128)(2,1)}), bf16[12,16,4608]{2,1,0:T(8,128)(2,1)S(1)}, u32[]{:S(2)}, u32[]{:S(2)}) async-start(bf16[12,16,4608]{2,1,0:T(8,128)(2,1)} %bitcast.25), calls=%async_computation.1 | async-start | bytes 3538944 | tf_op jit(solution)/shard_map/pack/all_to_all | solution.py:200
  45.6 51.5 %all-gather.2.cloned.1.call-start = ((), (), s32[]{:S(2)}) async-start(), calls=%async_computation.4 | async-start | bytes 2359296 | tf_op jit(solution)/shard_map/pack/all_gather | solution.py:199
  46.4 31.7 %copy-start.2 = (s32[2]{0:T(128)}, s32[2]{0:T(128)S(1)}, u32[]{:S(2)}) copy-start(s32[2]{0:T(128)S(1)} %pad_add_fusion.place_ref) | copy-start | bytes 28
  77.2 0.9 copy-start.3
  78.0 6.2 %copy-start.4 = (f32[2,16,40,128]{3,2,1,0:T(8,128)S(1)}, f32[2,16,40,128]{3,2,1,0:T(8,128)}, u32[]{:S(2)}) copy-start(f32[2,16,40,128]{3,2,1,0:T(8,128)} %copy-done.3) | copy-start | bytes 1966084
  78.0 31.0 %all-to-all-start.2 = ((bf16[12,16,4096]{2,1,0:T(8,128)(2,1)}), bf16[12,16,4096]{2,1,0:T(8,128)(2,1)}, u32[]{:S(2)}, u32[]{:S(2)}) async-start(bf16[12,16,4096]{2,1,0:T(8,128)(2,1)} %bitcast.12), calls=%async_computation.2 | async-start | bytes 3145728 | tf_op jit(solution)/shard_map/adapters/all_to_all | solution.py:216
  84.2 4.0 %collective-permute-start = (f32[2,640,128]{2,1,0:T(8,128)S(1)}, f32[2,640,128]{2,1,0:T(8,128)S(1)}, u32[]{:S(2)}, u32[]{:S(2)}) collective-permute-start(f32[2,640,128]{2,1,0:T(8,128)S(1)} %bitcast.24), channel_id=1, source_target_pairs={{0,12},{12,0},{1,13},{13,1},{2,14},{14,2},{3,15},{15,3},{4,16},{16... | collective-permute-start | bytes 1966088 | tf_op jit(solution)/shard_map/weight_grads/ppermute | solution.py:221
  88.2 8.1 %collective-permute-start.1 = (bf16[640,128]{1,0:T(8,128)(2,1)S(1)}, bf16[640,128]{1,0:T(8,128)(2,1)S(1)}, u32[]{:S(2)}, u32[]{:S(2)}) collective-permute-start(bf16[640,128]{1,0:T(8,128)(2,1)S(1)} %get-tuple-element.20), channel_id=1, source_target_pairs={{0,24},{24,0},{1,25},{25,1},{2,26},{26,2},{3,27},{27,3},{4,28},{28... | collective-permute-start | bytes 491528 | tf_op jit(solution)/shard_map/weight_grads/ppermute | solution.py:237
  97.1 23.0 %collective-permute-start.2 = (bf16[2048,512]{1,0:T(8,128)(2,1)}, bf16[2048,512]{1,0:T(8,128)(2,1)S(1)}, u32[]{:S(2)}, u32[]{:S(2)}) collective-permute-start(bf16[2048,512]{1,0:T(8,128)(2,1)} %all-gather.2.cloned.1.call-done), channel_id=1, source_target_pairs={{0,12},{12,0},{1,13},{13,1},{2,14},{14,2},{3,15},{15,3},{4,16},{16... | collective-permute-start | bytes 6291464 | tf_op jit(solution)/shard_map/weight_grads/ppermute | solution.py:239
  109.1 26.0 %all-to-all-start.3 = ((bf16[16,40,128]{2,1,0:T(8,128)(2,1)}), bf16[16,40,128]{2,1,0:T(8,128)(2,1)S(1)}, u32[]{:S(2)}, u32[]{:S(2)}) async-start(bf16[16,40,128]{2,1,0:T(8,128)(2,1)} %bitcast.14), calls=%async_computation.3 | async-start | bytes 327680 | tf_op jit(solution)/shard_map/weight_grads/all_to_all | solution.py:241
  120.1 1.3 copy-start.5
Sparse Core Ops, SparseCore 0:
  48.8 43.5 all-gather.1

commit v8 on v7

--- a/solution.py
+++ b/solution.py
@@ -65,7 +65,16 @@
         copy.wait()
 
 
-def adapter_kernel(place_ref, recv_ref, down_t_ref, up_ref, dx_ref, keep_ref, send_ref):
+def input_grad_kernel(grads_ref, down_t_ref, up_ref, dx_ref):
+    proj = dot(grads_ref[...], up_ref[...], NT).astype(jnp.bfloat16)
+    features = down_t_ref.shape[1]
+    step = 1024
+    for at in range(0, features, step):
+        dx = ADAPTER_SCALING * dot(proj, down_t_ref[:, at : at + step], NN)
+        dx_ref[:, at : at + step] = dx.astype(jnp.bfloat16)
+
+
+def weight_grad_kernel(place_ref, recv_ref, down_t_ref, up_ref, keep_ref, send_ref):
     rank, features = down_t_ref.shape
     blocks = 2 * keep_ref.shape[1]
     first = place_ref[0] == 0
@@ -80,7 +89,6 @@
     for at in range(0, features, step):
         rows = recv_ref[:, at : at + step]
         part = down_t_ref[:, at : at + step]
-        dx_ref[:, at : at + step] = (ADAPTER_SCALING * dot(proj, part, NN)).astype(jnp.bfloat16)
         total = total + dot(rows, part, NT)
         down = ADAPTER_SCALING * dot(rows, proj, TN)
         for b in range(step // wide):
@@ -172,11 +180,12 @@
     up = task_up_adapters[0]
     rank = up.shape[0]
     bf16, f32 = jnp.bfloat16, jnp.float32
-    place = jnp.stack([lax.axis_index("c"), lax.axis_index("yl")]).astype(jnp.int32)
+    place = jnp.stack([lax.axis_index("c"), lax.axis_index("yl"), lax.axis_index("zh")]).astype(jnp.int32)
 
     with jax.named_scope("frozen_gather"):
-        spread = jnp.broadcast_to(fixed_value_weight[None], (n_zh, part, kv_width))
-        along_z = lax.all_to_all(spread, "zh", 0, 0, tiled=True).reshape(n_zh * part, kv_width)
+        along_z = [fixed_value_weight]
+        for shift in range(1, n_zh):
+            along_z.append(lax.ppermute(fixed_value_weight, "zh", [(i, (i + shift) % n_zh) for i in range(n_zh)]))
 
     with jax.named_scope("pack"):
         packed = pl.pallas_call(
@@ -195,8 +204,8 @@
             ],
             compiler_params=params(WHOLE_VMEM),
         )(live_row_counts, row_packing_order, inputs, output_gradient_rows)
-        packed, along_z = lax.optimization_barrier((packed, along_z))
-        own = lax.all_gather(along_z, ("yh", "yl"), axis=0, tiled=True)
+        packed, *along_z = lax.optimization_barrier((packed, *along_z))
+        own = lax.all_gather(jnp.concatenate(along_z, axis=0), ("yh", "yl"), axis=0, tiled=True)
         recv = lax.all_to_all(packed.reshape(tasks, slot, features + kv_width), DP, 0, 0, tiled=True)
         recv = recv.reshape(per_device, features + kv_width)
 
@@ -205,12 +214,24 @@
         few = kv_width // (2 * blocks)
         deep = quarter + few
         terms = jax.ShapeDtypeStruct((2, pairs, deep, 2 * rank), f32)
-        dx, keep, send = pl.pallas_call(
-            adapter_kernel,
-            out_shape=(jax.ShapeDtypeStruct((per_device, features), bf16), terms, terms),
+        dx = pl.pallas_call(
+            input_grad_kernel,
+            out_shape=jax.ShapeDtypeStruct((per_device, features), bf16),
+            grid=(1,),
+            in_specs=[
+                pl.BlockSpec((per_device, kv_width), lambda i: (0, features // kv_width)),
+                one(rank, features),
+                one(rank, kv_width),
+            ],
+            out_specs=one(per_device, features),
+            compiler_params=params(),
+        )(recv, down_t, up)
+        keep, send = pl.pallas_call(
+            weight_grad_kernel,
+            out_shape=(terms, terms),
             grid=(1,),
             in_specs=[scalars(), one(per_device, features + kv_width), one(rank, features), one(rank, kv_width)],
-            out_specs=(one(per_device, features), one(*terms.shape), one(*terms.shape)),
+            out_specs=(one(*terms.shape), one(*terms.shape)),
             compiler_params=params(),
         )(place, recv, down_t, up)
         back = lax.all_to_all(dx.reshape(tasks, slot, features), DP, 0, 0, tiled=True)
@@ -257,7 +278,10 @@
         def block(*shape):
             return pl.BlockSpec(shape, lambda i, place: (0,) * len(shape))
 
-        weight_spec = pl.BlockSpec((n_y, 1, part, kv_width), lambda i, place: (0, i, 0, 0))
+        def weight_at(i, place):
+            return 0, lax.rem(place[2] - i + n_zh, n_zh), 0, 0
+
+        weight_spec = pl.BlockSpec((n_y, 1, part, kv_width), weight_at)
         rows_spec = pl.BlockSpec((per_device, wide), lambda i, place: (0, i))
         input_grad = pl.pallas_call(
             final_kernel,

time: 143 us -> 141 us (0.986)
  waiting for transfers between devices: 64.2 us -> 49.6 us
  starting transfers between devices: 45.3 us -> 59.4 us
  local copies, waits for them, and re-layouts: 4.41 us -> 1.31 us
    ppermute x0 -> x3, starting transfers between devices: none -> 24 us  [on_device(): lax.ppermute(fixed_value_weight, 'zh', [(i, (i + shift) % n_zh) for i in...]
    all_to_all x1 -> x0, starting transfers between devices: 14.5 us -> none  [on_device(): lax.all_to_all(spread, 'zh', 0, 0, tiled=True)]
    all_to_all x1 -> x0, waiting for transfers between devices: 12 us -> none  [on_device(): lax.all_to_all(spread, 'zh', 0, 0, tiled=True)]
    all_to_all x1, starting transfers between devices: 11 us -> 13.5 us  [on_device(): lax.all_to_all(column.reshape(pairs, deep, 2 * rank), ('zh', 'yh'), 0, 0,...]
    all_to_all x1, starting transfers between devices: 6.34 us -> 8.65 us  [on_device(): lax.all_to_all(packed.reshape(tasks, slot, features + kv_width), DP, 0, 0...]
    all_to_all x1, waiting for transfers between devices: 10.1 us -> 8.08 us  [on_device(): lax.all_to_all(dx.reshape(tasks, slot, features), DP, 0, 0, tiled=True)]
    broadcast_in_dim x1 -> x0, local copies, waits for them, and re-layouts: 1.56 us -> none  [on_device(): spread = jnp.broadcast_to(fixed_value_weight[None], (n_zh, part, kv_width))]
    unnamed x14 -> x10, local copies, waits for them, and re-layouts: 2.85 us -> 1.31 us
  transfers between devices with their start and end apart: 8 -> 10, of which waited for: 6 -> 6; matrix products, arithmetic and copies ran while one was open for 0% -> 1% of each run, Pallas kernels for 10% -> 10%
where the time goes in v8:
time: 141 us; the launch traced here: 140 us
  starting transfers between devices  59.4 us (42%)
  waiting for transfers between devices  49.6 us (35%)
  Pallas kernels  15.2 us (11%)
  between operations  14.1 us (10%)
    all_to_all x1, waiting for transfers between devices, on_device(): lax.all_to_all(packed.reshape(tasks, slot, features + kv_width), DP, 0, 0...  26.1 us
    ppermute x3, starting transfers between devices, on_device(): lax.ppermute(fixed_value_weight, 'zh', [(i, (i + shift) % n_zh) for i in...  24 us
    all_to_all x1, starting transfers between devices, on_device(): lax.all_to_all(column.reshape(pairs, deep, 2 * rank), ('zh', 'yh'), 0, 0,...  13.5 us
    all_to_all x1, starting transfers between devices, on_device(): lax.all_to_all(packed.reshape(tasks, slot, features + kv_width), DP, 0, 0...  8.65 us
    all_to_all x1, waiting for transfers between devices, on_device(): lax.all_to_all(dx.reshape(tasks, slot, features), DP, 0, 0, tiled=True)  8.08 us
    all_to_all x1, waiting for transfers between devices, on_device(): lax.all_to_all(column.reshape(pairs, deep, 2 * rank), ('zh', 'yh'), 0, 0,...  7.32 us
    pallas_call x1, Pallas kernels, on_device(): pl.pallas_call(final_kernel, out_shape=jax.ShapeDtypeStruct((per_device,...  6.38 us
    all_to_all x1, starting transfers between devices, on_device(): lax.all_to_all(dx.reshape(tasks, slot, features), DP, 0, 0, tiled=True)  6.03 us
  transfers between devices with their start and end apart: 10, of which 6 were waited for; matrix products, arithmetic and copies ran while one was open for 1% of the time, Pallas kernels for 10%

profile of v8, /device:TPU:6, one launch (start us, length us, event | category | flops | bytes accessed | tf_op | source)
XLA Modules:
  0.0 140.4 jit_solution(11959731092600888511)
XLA Ops:
  7.2 15.1 %collective-permute-start.1 = (bf16[64,512]{1,0:T(8,128)(2,1)}, bf16[64,512]{1,0:T(8,128)(2,1)S(1)}, u32[]{:S(2)}, u32[]{:S(2)}) collective-permute-start(bf16[64,512]{1,0:T(8,128)(2,1)} %param.9), channel_id=1, source_target_pairs={{0,384},{192,576},{384,0},{576,192},{1,385},{193,577},{385,1},{577... | collective-permute-start | bytes 196616 | tf_op jit(solution)/shard_map/frozen_gather/ppermute | solution.py:188
  22.3 5.2 %collective-permute-start = (bf16[64,512]{1,0:T(8,128)(2,1)}, bf16[64,512]{1,0:T(8,128)(2,1)S(1)}, u32[]{:S(2)}, u32[]{:S(2)}) collective-permute-start(bf16[64,512]{1,0:T(8,128)(2,1)} %param.9), channel_id=1, source_target_pairs={{0,192},{192,384},{384,576},{576,0},{1,193},{193,385},{385,577},{5... | collective-permute-start | bytes 196616 | tf_op jit(solution)/shard_map/frozen_gather/ppermute | solution.py:188
  27.5 3.7 %collective-permute-start.2 = (bf16[64,512]{1,0:T(8,128)(2,1)}, bf16[64,512]{1,0:T(8,128)(2,1)S(1)}, u32[]{:S(2)}, u32[]{:S(2)}) collective-permute-start(bf16[64,512]{1,0:T(8,128)(2,1)} %param.9), channel_id=1, source_target_pairs={{0,576},{192,0},{384,192},{576,384},{1,577},{193,1},{385,193},{577... | collective-permute-start | bytes 196616 | tf_op jit(solution)/shard_map/frozen_gather/ppermute | solution.py:188
  31.2 3.3 %pack.1 = bf16[192,4608]{1,0:T(8,128)(2,1)} custom-call(s32[1,12]{1,0:T(1,128)} %counts_ref.1, s32[1,192]{1,0:T(1,128)} %packing_ref.1, bf16[192,4096]{1,0:T(8,128)(2,1)} %rows_hbm.1, bf16[192,512]{1,0:T(8,128)(2,1)} %grads_ref.1), custom_call_target="tpu_custom_call" | custom-call | tf_op jit(solution)/shard_map/pack/pallas_call | solution.py:191
  34.5 0.0 collective-permute-done.1
  34.5 0.0 collective-permute-done
  34.5 1.3 collective-permute-done.2
  35.8 0.0 copy-start.4
  35.8 0.0 copy-start
  35.8 0.0 copy-start.1
  35.8 8.6 %all-to-all-start = ((bf16[12,16,4608]{2,1,0:T(8,128)(2,1)}), bf16[12,16,4608]{2,1,0:T(8,128)(2,1)S(1)}, u32[]{:S(2)}, u32[]{:S(2)}) async-start(bf16[12,16,4608]{2,1,0:T(8,128)(2,1)} %bitcast.28), calls=%async_computation | async-start | bytes 3538944 | tf_op jit(solution)/shard_map/pack/all_to_all | solution.py:209
  44.5 0.0 all-gather.2.cloned.1.call-start
  44.5 0.0 copy-done.4
  44.5 0.7 pad_maximum_fusion
  45.2 0.0 all-gather.2.cloned.1.call-update
  45.2 26.1 %all-to-all-done = bf16[12,16,4608]{2,1,0:T(8,128)(2,1)S(1)} async-done(((bf16[12,16,4608]{2,1,0:T(8,128)(2,1)}), bf16[12,16,4608]{2,1,0:T(8,128)(2,1)S(1)}, u32[]{:S(2)}, u32[]{:S(2)}) %all-to-all-start) | async-done | bytes 1769504 | tf_op jit(solution)/shard_map/pack/all_to_all | solution.py:209
  71.3 0.0 copy-done
  71.3 0.0 copy-done.1
  71.3 1.9 %adapters.3 = bf16[192,4096]{1,0:T(8,128)(2,1)} custom-call(bf16[192,4608]{1,0:T(8,128)(2,1)S(1)} %bitcast.20, bf16[64,4096]{1,0:T(8,128)(2,1)S(1)} %bitcast.22, bf16[64,512]{1,0:T(8,128)(2,1)S(1)} %bitcast.25), custom_call_target="tpu_custom_call" | custom-call | tf_op jit(solution)/shard_map/adapters/pallas_call | solution.py:217
  73.3 6.0 %all-to-all-start.1 = ((bf16[12,16,4096]{2,1,0:T(8,128)(2,1)}), bf16[12,16,4096]{2,1,0:T(8,128)(2,1)}, u32[]{:S(2)}, u32[]{:S(2)}) async-start(bf16[12,16,4096]{2,1,0:T(8,128)(2,1)} %bitcast.13), calls=%async_computation.1 | async-start | bytes 3145728 | tf_op jit(solution)/shard_map/adapters/all_to_all | solution.py:237
  79.3 0.1 pad_add_fusion.place_ref
  79.4 0.0 copy-start.2
  79.4 2.1 %adapters.2 = (f32[2,16,40,128]{3,2,1,0:T(8,128)S(1)}, f32[2,16,40,128]{3,2,1,0:T(8,128)S(1)}) custom-call(s32[3]{0:T(128)S(1)} %pad_add_fusion.place_ref, bf16[192,4608]{1,0:T(8,128)(2,1)S(1)} %bitcast.21, bf16[64,4096]{1,0:T(8,128)(2,1)S(1)} %bitcast.23, bf16[64,512]{1,0:T(8,128)(2,1)S(1)} %bitcast.26), custom_call_target="tpu_custom_call" | custom-call | tf_op jit(solution)/shard_map/adapters/pallas_call | solution.py:229
  81.5 1.9 %collective-permute-start.3 = (f32[2,640,128]{2,1,0:T(8,128)S(1)}, f32[2,640,128]{2,1,0:T(8,128)S(1)}, u32[]{:S(2)}, u32[]{:S(2)}) collective-permute-start(f32[2,640,128]{2,1,0:T(8,128)S(1)} %bitcast.27), channel_id=1, source_target_pairs={{0,12},{12,0},{1,13},{13,1},{2,14},{14,2},{3,15},{15,3},{4,16},{16... | collective-permute-start | bytes 1966088 | tf_op jit(solution)/shard_map/weight_grads/ppermute | solution.py:242
  83.4 2.1 %collective-permute-done.3.got_ref = f32[2,640,128]{2,1,0:T(8,128)S(1)} collective-permute-done((f32[2,640,128]{2,1,0:T(8,128)S(1)}, f32[2,640,128]{2,1,0:T(8,128)S(1)}, u32[]{:S(2)}, u32[]{:S(2)}) %collective-permute-start.3) | collective-permute-done | bytes 655392 | tf_op jit(solution)/shard_map/weight_grads/ppermute | solution.py:242
  85.5 0.1 weight_grads.3
  85.6 0.0 copy-done.2
  85.6 3.5 %collective-permute-start.4 = (bf16[640,128]{1,0:T(8,128)(2,1)S(1)}, bf16[640,128]{1,0:T(8,128)(2,1)S(1)}, u32[]{:S(2)}, u32[]{:S(2)}) collective-permute-start(bf16[640,128]{1,0:T(8,128)(2,1)S(1)} %get-tuple-element.22), channel_id=1, source_target_pairs={{0,24},{24,0},{1,25},{25,1},{2,26},{26,2},{3,27},{27,3},{4,28},{28... | collective-permute-start | bytes 491528 | tf_op jit(solution)/shard_map/weight_grads/ppermute | solution.py:258
  89.1 4.6 %collective-permute-done.4.got_ref = bf16[640,128]{1,0:T(8,128)(2,1)S(1)} collective-permute-done((bf16[640,128]{1,0:T(8,128)(2,1)S(1)}, bf16[640,128]{1,0:T(8,128)(2,1)S(1)}, u32[]{:S(2)}, u32[]{:S(2)}) %collective-permute-start.4) | collective-permute-done | bytes 163872 | tf_op jit(solution)/shard_map/weight_grads/ppermute | solution.py:258
  93.7 0.7 weight_grads.4
  94.4 0.0 all-gather.2.cloned.1.call-done
  94.4 1.9 %collective-permute-start.5 = (bf16[2048,512]{1,0:T(8,128)(2,1)}, bf16[2048,512]{1,0:T(8,128)(2,1)S(1)}, u32[]{:S(2)}, u32[]{:S(2)}) collective-permute-start(bf16[2048,512]{1,0:T(8,128)(2,1)} %all-gather.2.cloned.1.call-done), channel_id=1, source_target_pairs={{0,12},{12,0},{1,13},{13,1},{2,14},{14,2},{3,15},{15,3},{4,16},{16... | collective-permute-start | bytes 6291464 | tf_op jit(solution)/shard_map/weight_grads/ppermute | solution.py:260
  96.3 8.1 %all-to-all-done.1 = bf16[12,16,4096]{2,1,0:T(8,128)(2,1)} async-done(((bf16[12,16,4096]{2,1,0:T(8,128)(2,1)}), bf16[12,16,4096]{2,1,0:T(8,128)(2,1)}, u32[]{:S(2)}, u32[]{:S(2)}) %all-to-all-start.1) | async-done | bytes 1572896 | tf_op jit(solution)/shard_map/adapters/all_to_all | solution.py:237
  104.4 13.5 %all-to-all-start.2 = ((bf16[16,40,128]{2,1,0:T(8,128)(2,1)}), bf16[16,40,128]{2,1,0:T(8,128)(2,1)S(1)}, u32[]{:S(2)}, u32[]{:S(2)}) async-start(bf16[16,40,128]{2,1,0:T(8,128)(2,1)} %bitcast.15), calls=%async_computation.2 | async-start | bytes 327680 | tf_op jit(solution)/shard_map/weight_grads/all_to_all | solution.py:262
  117.9 0.0 collective-permute-done.5
  117.9 0.0 copy-start.3
  117.9 1.3 copy-done.3
  119.2 6.4 %input_grad.1 = bf16[192,4096]{1,0:T(8,128)(2,1)} custom-call(s32[3]{0:T(128)} %copy-done.2, s32[1,12]{1,0:T(1,128)} %counts_ref.1, s32[1,192]{1,0:T(1,128)} %packing_ref.1, bf16[192,512]{1,0:T(8,128)(2,1)} %grads_ref.1, bf16[8,4,64,512]{3,2,1,0:T(8,128)(2,1)} %bitcast.29, bf16[8,4,64,512]{3,2,1,0:T(8,128)(2,1)} %bitcast.30, bf16[192,4096]{1,0:T(8,128)(2,1)} %bitcast.14.back_ref), custom_call_target="tpu_custom_call" | custom-call | tf_op jit(solution)/shard_map/input_grad/pallas_call | solution.py:286
  125.5 7.3 %all-to-all-done.2.got_ref = bf16[16,40,128]{2,1,0:T(8,128)(2,1)S(1)} async-done(((bf16[16,40,128]{2,1,0:T(8,128)(2,1)}), bf16[16,40,128]{2,1,0:T(8,128)(2,1)S(1)}, u32[]{:S(2)}, u32[]{:S(2)}) %all-to-all-start.2) | async-done | bytes 163872 | tf_op jit(solution)/shard_map/weight_grads/all_to_all | solution.py:262
  132.9 0.7 weight_grads.5
Async XLA Ops:
  7.2 27.3 %collective-permute-start.1 = (bf16[64,512]{1,0:T(8,128)(2,1)}, bf16[64,512]{1,0:T(8,128)(2,1)S(1)}, u32[]{:S(2)}, u32[]{:S(2)}) collective-permute-start(bf16[64,512]{1,0:T(8,128)(2,1)} %param.9), channel_id=1, source_target_pairs={{0,384},{192,576},{384,0},{576,192},{1,385},{193,577},{385,1},{577... | collective-permute-start | bytes 196616 | tf_op jit(solution)/shard_map/frozen_gather/ppermute | solution.py:188
  22.3 12.2 %collective-permute-start = (bf16[64,512]{1,0:T(8,128)(2,1)}, bf16[64,512]{1,0:T(8,128)(2,1)S(1)}, u32[]{:S(2)}, u32[]{:S(2)}) collective-permute-start(bf16[64,512]{1,0:T(8,128)(2,1)} %param.9), channel_id=1, source_target_pairs={{0,192},{192,384},{384,576},{576,0},{1,193},{193,385},{385,577},{5... | collective-permute-start | bytes 196616 | tf_op jit(solution)/shard_map/frozen_gather/ppermute | solution.py:188
  27.5 8.3 %collective-permute-start.2 = (bf16[64,512]{1,0:T(8,128)(2,1)}, bf16[64,512]{1,0:T(8,128)(2,1)S(1)}, u32[]{:S(2)}, u32[]{:S(2)}) collective-permute-start(bf16[64,512]{1,0:T(8,128)(2,1)} %param.9), channel_id=1, source_target_pairs={{0,576},{192,0},{384,192},{576,384},{1,577},{193,1},{385,193},{577... | collective-permute-start | bytes 196616 | tf_op jit(solution)/shard_map/frozen_gather/ppermute | solution.py:188
  35.8 8.7 %copy-start.4 = (bf16[64,512]{1,0:T(8,128)(2,1)S(1)}, bf16[64,512]{1,0:T(8,128)(2,1)}, u32[]{:S(2)}) copy-start(bf16[64,512]{1,0:T(8,128)(2,1)} %param.9) | copy-start | bytes 196612
  35.8 35.5 %copy-start = (bf16[1,4096,64]{1,2,0:T(8,128)(2,1)S(1)}, bf16[1,4096,64]{1,2,0:T(8,128)(2,1)}, u32[]{:S(2)}) copy-start(bf16[1,4096,64]{1,2,0:T(8,128)(2,1)} %param.10) | copy-start | bytes 1572868
  35.8 35.5 %copy-start.1 = (bf16[1,64,512]{2,1,0:T(8,128)(2,1)S(1)}, bf16[1,64,512]{2,1,0:T(8,128)(2,1)}, u32[]{:S(2)}) copy-start(bf16[1,64,512]{2,1,0:T(8,128)(2,1)} %param.11) | copy-start | bytes 196612
  35.8 35.5 %all-to-all-start = ((bf16[12,16,4608]{2,1,0:T(8,128)(2,1)}), bf16[12,16,4608]{2,1,0:T(8,128)(2,1)S(1)}, u32[]{:S(2)}, u32[]{:S(2)}) async-start(bf16[12,16,4608]{2,1,0:T(8,128)(2,1)} %bitcast.28), calls=%async_computation | async-start | bytes 3538944 | tf_op jit(solution)/shard_map/pack/all_to_all | solution.py:209
  44.5 50.0 %all-gather.2.cloned.1.call-start = ((), (), s32[]{:S(2)}) async-start(), calls=%async_computation.3 | async-start | bytes 2359296 | tf_op jit(solution)/shard_map/pack/all_gather | solution.py:208
  73.3 31.1 %all-to-all-start.1 = ((bf16[12,16,4096]{2,1,0:T(8,128)(2,1)}), bf16[12,16,4096]{2,1,0:T(8,128)(2,1)}, u32[]{:S(2)}, u32[]{:S(2)}) async-start(bf16[12,16,4096]{2,1,0:T(8,128)(2,1)} %bitcast.13), calls=%async_computation.1 | async-start | bytes 3145728 | tf_op jit(solution)/shard_map/adapters/all_to_all | solution.py:237
  79.4 6.2 %copy-start.2 = (s32[3]{0:T(128)}, s32[3]{0:T(128)S(1)}, u32[]{:S(2)}) copy-start(s32[3]{0:T(128)S(1)} %pad_add_fusion.place_ref) | copy-start | bytes 40
  81.5 4.0 %collective-permute-start.3 = (f32[2,640,128]{2,1,0:T(8,128)S(1)}, f32[2,640,128]{2,1,0:T(8,128)S(1)}, u32[]{:S(2)}, u32[]{:S(2)}) collective-permute-start(f32[2,640,128]{2,1,0:T(8,128)S(1)} %bitcast.27), channel_id=1, source_target_pairs={{0,12},{12,0},{1,13},{13,1},{2,14},{14,2},{3,15},{15,3},{4,16},{16... | collective-permute-start | bytes 1966088 | tf_op jit(solution)/shard_map/weight_grads/ppermute | solution.py:242
  85.6 8.1 %collective-permute-start.4 = (bf16[640,128]{1,0:T(8,128)(2,1)S(1)}, bf16[640,128]{1,0:T(8,128)(2,1)S(1)}, u32[]{:S(2)}, u32[]{:S(2)}) collective-permute-start(bf16[640,128]{1,0:T(8,128)(2,1)S(1)} %get-tuple-element.22), channel_id=1, source_target_pairs={{0,24},{24,0},{1,25},{25,1},{2,26},{26,2},{3,27},{27,3},{4,28},{28... | collective-permute-start | bytes 491528 | tf_op jit(solution)/shard_map/weight_grads/ppermute | solution.py:258
  94.4 23.5 %collective-permute-start.5 = (bf16[2048,512]{1,0:T(8,128)(2,1)}, bf16[2048,512]{1,0:T(8,128)(2,1)S(1)}, u32[]{:S(2)}, u32[]{:S(2)}) collective-permute-start(bf16[2048,512]{1,0:T(8,128)(2,1)} %all-gather.2.cloned.1.call-done), channel_id=1, source_target_pairs={{0,12},{12,0},{1,13},{13,1},{2,14},{14,2},{3,15},{15,3},{4,16},{16... | collective-permute-start | bytes 6291464 | tf_op jit(solution)/shard_map/weight_grads/ppermute | solution.py:260
  104.4 28.5 %all-to-all-start.2 = ((bf16[16,40,128]{2,1,0:T(8,128)(2,1)}), bf16[16,40,128]{2,1,0:T(8,128)(2,1)S(1)}, u32[]{:S(2)}, u32[]{:S(2)}) async-start(bf16[16,40,128]{2,1,0:T(8,128)(2,1)} %bitcast.15), calls=%async_computation.2 | async-start | bytes 327680 | tf_op jit(solution)/shard_map/weight_grads/all_to_all | solution.py:262
  117.9 1.3 copy-start.3
Sparse Core Ops, SparseCore 0:
  47.6 42.6 all-gather.1

commit v9 on v8

--- a/solution.py
+++ b/solution.py
@@ -183,9 +183,10 @@
     place = jnp.stack([lax.axis_index("c"), lax.axis_index("yl"), lax.axis_index("zh")]).astype(jnp.int32)
 
     with jax.named_scope("frozen_gather"):
-        along_z = [fixed_value_weight]
-        for shift in range(1, n_zh):
-            along_z.append(lax.ppermute(fixed_value_weight, "zh", [(i, (i + shift) % n_zh) for i in range(n_zh)]))
+        along_z = fixed_value_weight
+        for apart in (1, 3)[: n_zh // 2]:
+            got = lax.ppermute(along_z, "zh", [(i, i ^ apart) for i in range(n_zh)])
+            along_z = jnp.concatenate([along_z, got], axis=0)
 
     with jax.named_scope("pack"):
         packed = pl.pallas_call(
@@ -204,8 +205,8 @@
             ],
             compiler_params=params(WHOLE_VMEM),
         )(live_row_counts, row_packing_order, inputs, output_gradient_rows)
-        packed, *along_z = lax.optimization_barrier((packed, *along_z))
-        own = lax.all_gather(jnp.concatenate(along_z, axis=0), ("yh", "yl"), axis=0, tiled=True)
+        packed, got = lax.optimization_barrier((packed, got))
+        own = lax.all_gather(along_z, ("yh", "yl"), axis=0, tiled=True)
         recv = lax.all_to_all(packed.reshape(tasks, slot, features + kv_width), DP, 0, 0, tiled=True)
         recv = recv.reshape(per_device, features + kv_width)
 
@@ -279,7 +280,8 @@
             return pl.BlockSpec(shape, lambda i, place: (0,) * len(shape))
 
         def weight_at(i, place):
-            return 0, lax.rem(place[2] - i + n_zh, n_zh), 0, 0
+            apart = lax.bitwise_xor(place[2], i)
+            return 0, lax.bitwise_xor(apart, apart // 2), 0, 0
 
         weight_spec = pl.BlockSpec((n_y, 1, part, kv_width), weight_at)
         rows_spec = pl.BlockSpec((per_device, wide), lambda i, place: (0, i))

time: 141 us -> 141 us (level)
  starting transfers between devices: 59.4 us -> 53.2 us
  waiting for transfers between devices: 49.6 us -> 54.6 us
    ppermute x3 -> x2, waiting for transfers between devices: 1.32 us -> 6.45 us  [on_device(): got = lax.ppermute(along_z, 'zh', [(i, i ^ apart) for i in range(n_zh)])]
    ppermute x3 -> x2, starting transfers between devices: 24 us -> 21.6 us  [on_device(): got = lax.ppermute(along_z, 'zh', [(i, i ^ apart) for i in range(n_zh)])]
    all_to_all x1, starting transfers between devices: 8.65 us -> 6.47 us  [on_device(): lax.all_to_all(packed.reshape(tasks, slot, features + kv_width), DP, 0, 0...]
    all_to_all x1, starting transfers between devices: 13.5 us -> 11.9 us  [on_device(): lax.all_to_all(column.reshape(pairs, deep, 2 * rank), ('zh', 'yh'), 0, 0,...]
  transfers between devices with their start and end apart: 10 -> 9, of which waited for: 6 -> 7; matrix products, arithmetic and copies ran while one was open for 1% -> 1% of each run, Pallas kernels for 10% -> 10%
where the time goes in v9:
time: 141 us; the launch traced here: 140 us
  waiting for transfers between devices  54.6 us (39%)
  starting transfers between devices  53.2 us (38%)
  Pallas kernels  15.2 us (11%)
  between operations  14.1 us (10%)
  other arithmetic  1.64 us (1%)
    all_to_all x1, waiting for transfers between devices, on_device(): lax.all_to_all(packed.reshape(tasks, slot, features + kv_width), DP, 0, 0...  26 us
    ppermute x2, starting transfers between devices, on_device(): got = lax.ppermute(along_z, 'zh', [(i, i ^ apart) for i in range(n_zh)])  21.6 us
    all_to_all x1, starting transfers between devices, on_device(): lax.all_to_all(column.reshape(pairs, deep, 2 * rank), ('zh', 'yh'), 0, 0,...  11.9 us
    all_to_all x1, waiting for transfers between devices, on_device(): lax.all_to_all(column.reshape(pairs, deep, 2 * rank), ('zh', 'yh'), 0, 0,...  7.31 us
    all_to_all x1, waiting for transfers between devices, on_device(): lax.all_to_all(dx.reshape(tasks, slot, features), DP, 0, 0, tiled=True)  7.1 us
    all_to_all x1, starting transfers between devices, on_device(): lax.all_to_all(packed.reshape(tasks, slot, features + kv_width), DP, 0, 0...  6.47 us
    ppermute x2, waiting for transfers between devices, on_device(): got = lax.ppermute(along_z, 'zh', [(i, i ^ apart) for i in range(n_zh)])  6.45 us
    pallas_call x1, Pallas kernels, on_device(): pl.pallas_call(final_kernel, out_shape=jax.ShapeDtypeStruct((per_device,...  6.38 us
  transfers between devices with their start and end apart: 9, of which 7 were waited for; matrix products, arithmetic and copies ran while one was open for 1% of the time, Pallas kernels for 10%

profile of v9, /device:TPU:6, one launch (start us, length us, event | category | flops | bytes accessed | tf_op | source)
XLA Modules:
  0.0 140.1 jit_solution(2192851841401612533)
XLA Ops:
  7.2 7.9 %collective-permute-start = (bf16[64,512]{1,0:T(8,128)(2,1)}, bf16[64,512]{1,0:T(8,128)(2,1)S(1)}, u32[]{:S(2)}, u32[]{:S(2)}) collective-permute-start(bf16[64,512]{1,0:T(8,128)(2,1)} %param.9), channel_id=1, source_target_pairs={{0,192},{192,0},{384,576},{576,384},{1,193},{193,1},{385,577},{577... | collective-permute-start | bytes 196616 | tf_op jit(solution)/shard_map/frozen_gather/ppermute | solution.py:188
  15.1 2.4 %collective-permute-done = bf16[64,512]{1,0:T(8,128)(2,1)S(1)} collective-permute-done((bf16[64,512]{1,0:T(8,128)(2,1)}, bf16[64,512]{1,0:T(8,128)(2,1)S(1)}, u32[]{:S(2)}, u32[]{:S(2)}) %collective-permute-start) | collective-permute-done | bytes 65568 | tf_op jit(solution)/shard_map/frozen_gather/ppermute | solution.py:188
  17.5 0.8 pad_maximum_fusion.1
  18.4 13.7 %collective-permute-start.1 = (bf16[128,512]{1,0:T(8,128)(2,1)S(1)}, bf16[128,512]{1,0:T(8,128)(2,1)S(1)}, u32[]{:S(2)}, u32[]{:S(2)}) collective-permute-start(bf16[128,512]{1,0:T(8,128)(2,1)S(1)} %pad_maximum_fusion.1), channel_id=1, source_target_pairs={{0,576},{192,384},{384,192},{576,0},{1,577},{193,385},{385,193},{5... | collective-permute-start | bytes 393224 | tf_op jit(solution)/shard_map/frozen_gather/ppermute | solution.py:188
  32.1 3.3 %pack.1 = bf16[192,4608]{1,0:T(8,128)(2,1)} custom-call(s32[1,12]{1,0:T(1,128)} %counts_ref.1, s32[1,192]{1,0:T(1,128)} %packing_ref.1, bf16[192,4096]{1,0:T(8,128)(2,1)} %rows_hbm.1, bf16[192,512]{1,0:T(8,128)(2,1)} %grads_ref.1), custom_call_target="tpu_custom_call" | custom-call | tf_op jit(solution)/shard_map/pack/pallas_call | solution.py:192
  35.3 4.0 %collective-permute-done.1 = bf16[128,512]{1,0:T(8,128)(2,1)S(1)} collective-permute-done((bf16[128,512]{1,0:T(8,128)(2,1)S(1)}, bf16[128,512]{1,0:T(8,128)(2,1)S(1)}, u32[]{:S(2)}, u32[]{:S(2)}) %collective-permute-start.1) | collective-permute-done | bytes 131104 | tf_op jit(solution)/shard_map/frozen_gather/ppermute | solution.py:188
  39.3 0.0 copy-start.4
  39.3 0.0 copy-start
  39.3 0.0 copy-start.1
  39.3 6.5 %all-to-all-start = ((bf16[12,16,4608]{2,1,0:T(8,128)(2,1)}), bf16[12,16,4608]{2,1,0:T(8,128)(2,1)S(1)}, u32[]{:S(2)}, u32[]{:S(2)}) async-start(bf16[12,16,4608]{2,1,0:T(8,128)(2,1)} %bitcast.28), calls=%async_computation | async-start | bytes 3538944 | tf_op jit(solution)/shard_map/pack/all_to_all | solution.py:210
  45.8 0.0 all-gather.2.cloned.1.call-start
  45.8 0.0 copy-done.4
  45.8 0.7 pad_maximum_fusion
  46.5 0.0 all-gather.2.cloned.1.call-update
  46.6 26.0 %all-to-all-done = bf16[12,16,4608]{2,1,0:T(8,128)(2,1)S(1)} async-done(((bf16[12,16,4608]{2,1,0:T(8,128)(2,1)}), bf16[12,16,4608]{2,1,0:T(8,128)(2,1)S(1)}, u32[]{:S(2)}, u32[]{:S(2)}) %all-to-all-start) | async-done | bytes 1769504 | tf_op jit(solution)/shard_map/pack/all_to_all | solution.py:210
  72.5 0.0 copy-done
  72.5 0.0 copy-done.1
  72.5 1.9 %adapters.3 = bf16[192,4096]{1,0:T(8,128)(2,1)} custom-call(bf16[192,4608]{1,0:T(8,128)(2,1)S(1)} %bitcast.20, bf16[64,4096]{1,0:T(8,128)(2,1)S(1)} %bitcast.22, bf16[64,512]{1,0:T(8,128)(2,1)S(1)} %bitcast.25), custom_call_target="tpu_custom_call" | custom-call | tf_op jit(solution)/shard_map/adapters/pallas_call | solution.py:218
  74.5 6.0 %all-to-all-start.1 = ((bf16[12,16,4096]{2,1,0:T(8,128)(2,1)}), bf16[12,16,4096]{2,1,0:T(8,128)(2,1)}, u32[]{:S(2)}, u32[]{:S(2)}) async-start(bf16[12,16,4096]{2,1,0:T(8,128)(2,1)} %bitcast.13), calls=%async_computation.1 | async-start | bytes 3145728 | tf_op jit(solution)/shard_map/adapters/all_to_all | solution.py:238
  80.5 0.1 pad_add_fusion.place_ref
  80.5 0.0 copy-start.2
  80.5 2.1 %adapters.2 = (f32[2,16,40,128]{3,2,1,0:T(8,128)S(1)}, f32[2,16,40,128]{3,2,1,0:T(8,128)S(1)}) custom-call(s32[3]{0:T(128)S(1)} %pad_add_fusion.place_ref, bf16[192,4608]{1,0:T(8,128)(2,1)S(1)} %bitcast.21, bf16[64,4096]{1,0:T(8,128)(2,1)S(1)} %bitcast.23, bf16[64,512]{1,0:T(8,128)(2,1)S(1)} %bitcast.26), custom_call_target="tpu_custom_call" | custom-call | tf_op jit(solution)/shard_map/adapters/pallas_call | solution.py:230
  82.7 1.9 %collective-permute-start.2 = (f32[2,640,128]{2,1,0:T(8,128)S(1)}, f32[2,640,128]{2,1,0:T(8,128)S(1)}, u32[]{:S(2)}, u32[]{:S(2)}) collective-permute-start(f32[2,640,128]{2,1,0:T(8,128)S(1)} %bitcast.27), channel_id=1, source_target_pairs={{0,12},{12,0},{1,13},{13,1},{2,14},{14,2},{3,15},{15,3},{4,16},{16... | collective-permute-start | bytes 1966088 | tf_op jit(solution)/shard_map/weight_grads/ppermute | solution.py:243
  84.6 2.1 %collective-permute-done.2.got_ref = f32[2,640,128]{2,1,0:T(8,128)S(1)} collective-permute-done((f32[2,640,128]{2,1,0:T(8,128)S(1)}, f32[2,640,128]{2,1,0:T(8,128)S(1)}, u32[]{:S(2)}, u32[]{:S(2)}) %collective-permute-start.2) | collective-permute-done | bytes 655392 | tf_op jit(solution)/shard_map/weight_grads/ppermute | solution.py:243
  86.6 0.1 weight_grads.3
  86.7 0.0 copy-done.2
  86.7 3.5 %collective-permute-start.3 = (bf16[640,128]{1,0:T(8,128)(2,1)S(1)}, bf16[640,128]{1,0:T(8,128)(2,1)S(1)}, u32[]{:S(2)}, u32[]{:S(2)}) collective-permute-start(bf16[640,128]{1,0:T(8,128)(2,1)S(1)} %get-tuple-element.18), channel_id=1, source_target_pairs={{0,24},{24,0},{1,25},{25,1},{2,26},{26,2},{3,27},{27,3},{4,28},{28... | collective-permute-start | bytes 491528 | tf_op jit(solution)/shard_map/weight_grads/ppermute | solution.py:259
  90.2 5.7 %collective-permute-done.3.got_ref = bf16[640,128]{1,0:T(8,128)(2,1)S(1)} collective-permute-done((bf16[640,128]{1,0:T(8,128)(2,1)S(1)}, bf16[640,128]{1,0:T(8,128)(2,1)S(1)}, u32[]{:S(2)}, u32[]{:S(2)}) %collective-permute-start.3) | collective-permute-done | bytes 163872 | tf_op jit(solution)/shard_map/weight_grads/ppermute | solution.py:259
  95.9 0.7 weight_grads.4
  96.6 0.0 all-gather.2.cloned.1.call-done
  96.6 1.9 %collective-permute-start.4 = (bf16[2048,512]{1,0:T(8,128)(2,1)}, bf16[2048,512]{1,0:T(8,128)(2,1)S(1)}, u32[]{:S(2)}, u32[]{:S(2)}) collective-permute-start(bf16[2048,512]{1,0:T(8,128)(2,1)} %all-gather.2.cloned.1.call-done), channel_id=1, source_target_pairs={{0,12},{12,0},{1,13},{13,1},{2,14},{14,2},{3,15},{15,3},{4,16},{16... | collective-permute-start | bytes 6291464 | tf_op jit(solution)/shard_map/weight_grads/ppermute | solution.py:261
  98.5 7.1 %all-to-all-done.1 = bf16[12,16,4096]{2,1,0:T(8,128)(2,1)} async-done(((bf16[12,16,4096]{2,1,0:T(8,128)(2,1)}), bf16[12,16,4096]{2,1,0:T(8,128)(2,1)}, u32[]{:S(2)}, u32[]{:S(2)}) %all-to-all-start.1) | async-done | bytes 1572896 | tf_op jit(solution)/shard_map/adapters/all_to_all | solution.py:238
  105.6 11.9 %all-to-all-start.2 = ((bf16[16,40,128]{2,1,0:T(8,128)(2,1)}), bf16[16,40,128]{2,1,0:T(8,128)(2,1)S(1)}, u32[]{:S(2)}, u32[]{:S(2)}) async-start(bf16[16,40,128]{2,1,0:T(8,128)(2,1)} %bitcast.15), calls=%async_computation.2 | async-start | bytes 327680 | tf_op jit(solution)/shard_map/weight_grads/all_to_all | solution.py:263
  117.5 0.0 collective-permute-done.4
  117.5 0.0 copy-start.3
  117.6 1.3 copy-done.3
  118.9 6.4 %input_grad.1 = bf16[192,4096]{1,0:T(8,128)(2,1)} custom-call(s32[3]{0:T(128)} %copy-done.2, s32[1,12]{1,0:T(1,128)} %counts_ref.1, s32[1,192]{1,0:T(1,128)} %packing_ref.1, bf16[192,512]{1,0:T(8,128)(2,1)} %grads_ref.1, bf16[8,4,64,512]{3,2,1,0:T(8,128)(2,1)} %bitcast.29, bf16[8,4,64,512]{3,2,1,0:T(8,128)(2,1)} %bitcast.30, bf16[192,4096]{1,0:T(8,128)(2,1)} %bitcast.14.back_ref), custom_call_target="tpu_custom_call" | custom-call | tf_op jit(solution)/shard_map/input_grad/pallas_call | solution.py:288
  125.2 7.3 %all-to-all-done.2.got_ref = bf16[16,40,128]{2,1,0:T(8,128)(2,1)S(1)} async-done(((bf16[16,40,128]{2,1,0:T(8,128)(2,1)}), bf16[16,40,128]{2,1,0:T(8,128)(2,1)S(1)}, u32[]{:S(2)}, u32[]{:S(2)}) %all-to-all-start.2) | async-done | bytes 163872 | tf_op jit(solution)/shard_map/weight_grads/all_to_all | solution.py:263
  132.5 0.7 weight_grads.5
Async XLA Ops:
  7.2 10.3 %collective-permute-start = (bf16[64,512]{1,0:T(8,128)(2,1)}, bf16[64,512]{1,0:T(8,128)(2,1)S(1)}, u32[]{:S(2)}, u32[]{:S(2)}) collective-permute-start(bf16[64,512]{1,0:T(8,128)(2,1)} %param.9), channel_id=1, source_target_pairs={{0,192},{192,0},{384,576},{576,384},{1,193},{193,1},{385,577},{577... | collective-permute-start | bytes 196616 | tf_op jit(solution)/shard_map/frozen_gather/ppermute | solution.py:188
  18.4 21.0 %collective-permute-start.1 = (bf16[128,512]{1,0:T(8,128)(2,1)S(1)}, bf16[128,512]{1,0:T(8,128)(2,1)S(1)}, u32[]{:S(2)}, u32[]{:S(2)}) collective-permute-start(bf16[128,512]{1,0:T(8,128)(2,1)S(1)} %pad_maximum_fusion.1), channel_id=1, source_target_pairs={{0,576},{192,384},{384,192},{576,0},{1,577},{193,385},{385,193},{5... | collective-permute-start | bytes 393224 | tf_op jit(solution)/shard_map/frozen_gather/ppermute | solution.py:188
  39.3 6.5 %copy-start.4 = (bf16[64,512]{1,0:T(8,128)(2,1)S(1)}, bf16[64,512]{1,0:T(8,128)(2,1)}, u32[]{:S(2)}) copy-start(bf16[64,512]{1,0:T(8,128)(2,1)} %param.9) | copy-start | bytes 196612
  39.3 33.2 %copy-start = (bf16[1,4096,64]{1,2,0:T(8,128)(2,1)S(1)}, bf16[1,4096,64]{1,2,0:T(8,128)(2,1)}, u32[]{:S(2)}) copy-start(bf16[1,4096,64]{1,2,0:T(8,128)(2,1)} %param.10) | copy-start | bytes 1572868
  39.3 33.2 %copy-start.1 = (bf16[1,64,512]{2,1,0:T(8,128)(2,1)S(1)}, bf16[1,64,512]{2,1,0:T(8,128)(2,1)}, u32[]{:S(2)}) copy-start(bf16[1,64,512]{2,1,0:T(8,128)(2,1)} %param.11) | copy-start | bytes 196612
  39.3 33.2 %all-to-all-start = ((bf16[12,16,4608]{2,1,0:T(8,128)(2,1)}), bf16[12,16,4608]{2,1,0:T(8,128)(2,1)S(1)}, u32[]{:S(2)}, u32[]{:S(2)}) async-start(bf16[12,16,4608]{2,1,0:T(8,128)(2,1)} %bitcast.28), calls=%async_computation | async-start | bytes 3538944 | tf_op jit(solution)/shard_map/pack/all_to_all | solution.py:210
  45.8 50.8 %all-gather.2.cloned.1.call-start = ((), (), s32[]{:S(2)}) async-start(), calls=%async_computation.3 | async-start | bytes 2359296 | tf_op jit(solution)/shard_map/pack/all_gather | solution.py:209
  74.5 31.2 %all-to-all-start.1 = ((bf16[12,16,4096]{2,1,0:T(8,128)(2,1)}), bf16[12,16,4096]{2,1,0:T(8,128)(2,1)}, u32[]{:S(2)}, u32[]{:S(2)}) async-start(bf16[12,16,4096]{2,1,0:T(8,128)(2,1)} %bitcast.13), calls=%async_computation.1 | async-start | bytes 3145728 | tf_op jit(solution)/shard_map/adapters/all_to_all | solution.py:238
  80.5 6.2 %copy-start.2 = (s32[3]{0:T(128)}, s32[3]{0:T(128)S(1)}, u32[]{:S(2)}) copy-start(s32[3]{0:T(128)S(1)} %pad_add_fusion.place_ref) | copy-start | bytes 40
  82.7 4.0 %collective-permute-start.2 = (f32[2,640,128]{2,1,0:T(8,128)S(1)}, f32[2,640,128]{2,1,0:T(8,128)S(1)}, u32[]{:S(2)}, u32[]{:S(2)}) collective-permute-start(f32[2,640,128]{2,1,0:T(8,128)S(1)} %bitcast.27), channel_id=1, source_target_pairs={{0,12},{12,0},{1,13},{13,1},{2,14},{14,2},{3,15},{15,3},{4,16},{16... | collective-permute-start | bytes 1966088 | tf_op jit(solution)/shard_map/weight_grads/ppermute | solution.py:243
  86.7 9.2 %collective-permute-start.3 = (bf16[640,128]{1,0:T(8,128)(2,1)S(1)}, bf16[640,128]{1,0:T(8,128)(2,1)S(1)}, u32[]{:S(2)}, u32[]{:S(2)}) collective-permute-start(bf16[640,128]{1,0:T(8,128)(2,1)S(1)} %get-tuple-element.18), channel_id=1, source_target_pairs={{0,24},{24,0},{1,25},{25,1},{2,26},{26,2},{3,27},{27,3},{4,28},{28... | collective-permute-start | bytes 491528 | tf_op jit(solution)/shard_map/weight_grads/ppermute | solution.py:259
  96.6 20.9 %collective-permute-start.4 = (bf16[2048,512]{1,0:T(8,128)(2,1)}, bf16[2048,512]{1,0:T(8,128)(2,1)S(1)}, u32[]{:S(2)}, u32[]{:S(2)}) collective-permute-start(bf16[2048,512]{1,0:T(8,128)(2,1)} %all-gather.2.cloned.1.call-done), channel_id=1, source_target_pairs={{0,12},{12,0},{1,13},{13,1},{2,14},{14,2},{3,15},{15,3},{4,16},{16... | collective-permute-start | bytes 6291464 | tf_op jit(solution)/shard_map/weight_grads/ppermute | solution.py:261
  105.6 26.9 %all-to-all-start.2 = ((bf16[16,40,128]{2,1,0:T(8,128)(2,1)}), bf16[16,40,128]{2,1,0:T(8,128)(2,1)S(1)}, u32[]{:S(2)}, u32[]{:S(2)}) async-start(bf16[16,40,128]{2,1,0:T(8,128)(2,1)} %bitcast.15), calls=%async_computation.2 | async-start | bytes 327680 | tf_op jit(solution)/shard_map/weight_grads/all_to_all | solution.py:263
  117.5 1.3 copy-start.3
Sparse Core Ops, SparseCore 0:
  49.0 45.8 all-gather.1

commit v10 on v9

--- a/solution.py
+++ b/solution.py
@@ -9,7 +9,7 @@
 from jax.sharding import Mesh, PartitionSpec as P
 
 ADAPTER_SCALING = 2.0
-FSDP = ("zh", "yh", "yl", "c")
+FSDP = ("zh", "ya", "yb", "yl", "c")
 DP = ("zl", "x")
 VMEM_LIMIT = 16 * 1024 * 1024
 WHOLE_VMEM = 60 * 1024 * 1024
@@ -76,7 +76,7 @@
 
 def weight_grad_kernel(place_ref, recv_ref, down_t_ref, up_ref, keep_ref, send_ref):
     rank, features = down_t_ref.shape
-    blocks = 2 * keep_ref.shape[1]
+    blocks = 4 * keep_ref.shape[1]
     first = place_ref[0] == 0
     wide = features // blocks
     half = wide // 2
@@ -85,33 +85,33 @@
     proj = dot(grads, up_ref[...], NT).astype(jnp.bfloat16)
     total = jnp.zeros((recv_ref.shape[0], rank), jnp.float32)
     step = 1024
-    turn = [lax.bitwise_xor(place_ref[1], yl) for yl in range(2)]
+    turn = [2 * lax.bitwise_xor(place_ref[1], y % 2) + lax.bitwise_xor(place_ref[3], y // 2) for y in range(4)]
     for at in range(0, features, step):
         rows = recv_ref[:, at : at + step]
         part = down_t_ref[:, at : at + step]
         total = total + dot(rows, part, NT)
         down = ADAPTER_SCALING * dot(rows, proj, TN)
         for b in range(step // wide):
-            pair_at, yl = divmod(at // wide + b, 2)
+            pair_at, y = divmod(at // wide + b, 4)
             pair = []
             for c in range(2):
                 lo = b * wide + c * half
                 pair.append(jnp.concatenate([down[lo : lo + quarter], down[lo + quarter : lo + half]], axis=1))
-            keep_ref[turn[yl], pair_at, :quarter, :] = jnp.where(first, pair[0], pair[1])
-            send_ref[turn[yl], pair_at, :quarter, :] = jnp.where(first, pair[1], pair[0])
+            keep_ref[turn[y], pair_at, :quarter, :] = jnp.where(first, pair[0], pair[1])
+            send_ref[turn[y], pair_at, :quarter, :] = jnp.where(first, pair[1], pair[0])
     up_t = ADAPTER_SCALING * dot(grads, total.astype(jnp.bfloat16), TN)
     up_t = jnp.concatenate([up_t, jnp.zeros_like(up_t)], axis=1)
     few = grads.shape[1] // (2 * blocks)
     for b in range(blocks):
-        pair_at, yl = divmod(b, 2)
+        pair_at, y = divmod(b, 4)
         low, high = up_t[2 * b * few : (2 * b + 1) * few], up_t[(2 * b + 1) * few : (2 * b + 2) * few]
-        keep_ref[turn[yl], pair_at, quarter:, :] = jnp.where(first, low, high)
-        send_ref[turn[yl], pair_at, quarter:, :] = jnp.where(first, high, low)
+        keep_ref[turn[y], pair_at, quarter:, :] = jnp.where(first, low, high)
+        send_ref[turn[y], pair_at, quarter:, :] = jnp.where(first, high, low)
 
 
 def half_kernel(held_ref, got_ref, keep_ref, send_ref):
-    keep_ref[...] = held_ref[0] + got_ref[0]
-    send_ref[...] = (held_ref[1] + got_ref[1]).astype(send_ref.dtype)
+    keep_ref[...] = held_ref[0] + got_ref[0].astype(jnp.float32)
+    send_ref[...] = (held_ref[1] + got_ref[1].astype(jnp.float32)).astype(send_ref.dtype)
 
 
 def add_kernel(held_ref, got_ref, out_ref):
@@ -172,15 +172,15 @@
     kv_width = output_gradient_rows.shape[1]
     tasks = lax.axis_size("zl") * lax.axis_size("x")
     slot = per_device // tasks
-    n_zh, n_yh = lax.axis_size("zh"), lax.axis_size("yh")
-    pairs = n_zh * n_yh
-    blocks = 2 * pairs
+    n_zh, n_ya = lax.axis_size("zh"), lax.axis_size("ya")
+    pairs = n_zh * n_ya
+    blocks = 4 * pairs
     part = fixed_value_weight.shape[0]
     down_t = task_down_adapters[0].T
     up = task_up_adapters[0]
     rank = up.shape[0]
     bf16, f32 = jnp.bfloat16, jnp.float32
-    place = jnp.stack([lax.axis_index("c"), lax.axis_index("yl"), lax.axis_index("zh")]).astype(jnp.int32)
+    place = jnp.stack([lax.axis_index("c"), lax.axis_index("yl"), lax.axis_index("zh"), lax.axis_index("yb")]).astype(jnp.int32)
 
     with jax.named_scope("frozen_gather"):
         along_z = fixed_value_weight
@@ -206,7 +206,7 @@
             compiler_params=params(WHOLE_VMEM),
         )(live_row_counts, row_packing_order, inputs, output_gradient_rows)
         packed, got = lax.optimization_barrier((packed, got))
-        own = lax.all_gather(along_z, ("yh", "yl"), axis=0, tiled=True)
+        own = lax.all_gather(along_z, ("ya", "yb", "yl"), axis=0, tiled=True)
         recv = lax.all_to_all(packed.reshape(tasks, slot, features + kv_width), DP, 0, 0, tiled=True)
         recv = recv.reshape(per_device, features + kv_width)
 
@@ -214,7 +214,7 @@
         quarter = features // (4 * blocks)
         few = kv_width // (2 * blocks)
         deep = quarter + few
-        terms = jax.ShapeDtypeStruct((2, pairs, deep, 2 * rank), f32)
+        terms = jax.ShapeDtypeStruct((4, pairs, deep, 2 * rank), f32)
         dx = pl.pallas_call(
             input_grad_kernel,
             out_shape=jax.ShapeDtypeStruct((per_device, features), bf16),
@@ -239,16 +239,21 @@
         back = back.reshape(per_device, features)
 
     with jax.named_scope("weight_grads"):
-        flat = (pairs * deep, 2 * rank)
+        flat = (2 * pairs * deep, 2 * rank)
         held, got = keep.reshape(2, *flat), lax.ppermute(send.reshape(2, *flat), "c", [(0, 1), (1, 0)])
-        held, away = pl.pallas_call(
-            half_kernel,
-            out_shape=(jax.ShapeDtypeStruct(flat, f32), jax.ShapeDtypeStruct(flat, bf16)),
-            grid=(1,),
-            in_specs=[one(2, *flat), one(2, *flat)],
-            out_specs=(one(*flat), one(*flat)),
-            compiler_params=params(),
-        )(held, got)
+        for axis in ("yl", "yb"):
+            held, away = pl.pallas_call(
+                half_kernel,
+                out_shape=(jax.ShapeDtypeStruct(flat, f32), jax.ShapeDtypeStruct(flat, bf16)),
+                grid=(1,),
+                in_specs=[one(2, *flat), one(2, *flat)],
+                out_specs=(one(*flat), one(*flat)),
+                compiler_params=params(),
+            )(held, got)
+            got = lax.ppermute(away, axis, [(0, 1), (1, 0)])
+            if axis == "yl":
+                flat = (pairs * deep, 2 * rank)
+                held, got = held.reshape(2, *flat), got.reshape(2, *flat)
         column = pl.pallas_call(
             add_kernel,
             out_shape=jax.ShapeDtypeStruct(flat, bf16),
@@ -256,11 +261,11 @@
             in_specs=[one(*flat), one(*flat)],
             out_specs=one(*flat),
             compiler_params=params(),
-        )(held, lax.ppermute(away, "yl", [(0, 1), (1, 0)]))
+        )(held, got)
         column, own = lax.optimization_barrier((column, own))
         other = lax.ppermute(own, "c", [(0, 1), (1, 0)])
         column, back = lax.optimization_barrier((column, back))
-        shares = lax.all_to_all(column.reshape(pairs, deep, 2 * rank), ("zh", "yh"), 0, 0, tiled=True)
+        shares = lax.all_to_all(column.reshape(pairs, deep, 2 * rank), ("zh", "ya"), 0, 0, tiled=True)
         down_share, up_t_share = pl.pallas_call(
             last_sum_kernel,
             out_shape=(jax.ShapeDtypeStruct((2 * quarter, rank), f32), jax.ShapeDtypeStruct((few, rank), f32)),
@@ -272,7 +277,7 @@
         up_share = up_t_share.T
 
     with jax.named_scope("input_grad"):
-        n_y = 2 * n_yh
+        n_y = 4 * n_ya
         wide = n_y * 2 * part
         order = (n_y, n_zh, part, kv_width)
 
@@ -315,7 +320,7 @@
     return (input_grad, down_share[None], up_share[None])
 
 
-def solution(mesh, parts=(4, 4, 2, 2, 3, 4)):
+def solution(mesh, parts=(4, 2, 2, 2, 2, 3, 4)):
     fine = Mesh(np.asarray(mesh.devices).reshape(parts), FSDP + DP)
     rows = P(FSDP + DP, None)
     in_specs = (

time: 141 us -> 141 us (level)
  starting transfers between devices: 53.2 us -> 56.1 us
  waiting for transfers between devices: 54.6 us -> 52.2 us
    all_to_all x1, waiting for transfers between devices: 7.1 us -> 0.01 us  [on_device(): lax.all_to_all(dx.reshape(tasks, slot, features), DP, 0, 0, tiled=True)]
    ppermute x1 -> x2, waiting for transfers between devices: 5.69 us -> 10.3 us  [on_device(): got = lax.ppermute(away, axis, [(0, 1), (1, 0)])]
    ppermute x1 -> x2, starting transfers between devices: 3.49 us -> 7.62 us  [on_device(): got = lax.ppermute(away, axis, [(0, 1), (1, 0)])]
  transfers between devices with their start and end apart: 9 -> 10, of which waited for: 7 -> 7; matrix products, arithmetic and copies ran while one was open for 1% -> 1% of each run, Pallas kernels for 10% -> 10%
where the time goes in v10:
time: 141 us
  starting transfers between devices  56.1 us (40%)
  waiting for transfers between devices  52.2 us (37%)
  Pallas kernels  15.2 us (11%)
  between operations  14.1 us (10%)
  other arithmetic  1.64 us (1%)
    all_to_all x1, waiting for transfers between devices, on_device(): lax.all_to_all(packed.reshape(tasks, slot, features + kv_width), DP, 0, 0...  26 us
    ppermute x2, starting transfers between devices, on_device(): got = lax.ppermute(along_z, 'zh', [(i, i ^ apart) for i in range(n_zh)])  21.6 us
    all_to_all x1, starting transfers between devices, on_device(): lax.all_to_all(column.reshape(pairs, deep, 2 * rank), ('zh', 'ya'), 0, 0,...  10.6 us
    ppermute x2, waiting for transfers between devices, on_device(): got = lax.ppermute(away, axis, [(0, 1), (1, 0)])  10.3 us
    ppermute x2, starting transfers between devices, on_device(): got = lax.ppermute(away, axis, [(0, 1), (1, 0)])  7.62 us
    all_to_all x1, waiting for transfers between devices, on_device(): lax.all_to_all(column.reshape(pairs, deep, 2 * rank), ('zh', 'ya'), 0, 0,...  7.38 us
    all_to_all x1, starting transfers between devices, on_device(): lax.all_to_all(packed.reshape(tasks, slot, features + kv_width), DP, 0, 0...  6.47 us
    ppermute x2, waiting for transfers between devices, on_device(): got = lax.ppermute(along_z, 'zh', [(i, i ^ apart) for i in range(n_zh)])  6.43 us
  transfers between devices with their start and end apart: 10, of which 7 were waited for; matrix products, arithmetic and copies ran while one was open for 1% of the time, Pallas kernels for 10%

profile of v10, /device:TPU:6, one launch (start us, length us, event | category | flops | bytes accessed | tf_op | source)
XLA Modules:
  0.0 140.6 jit_solution(14300866634261438164)
XLA Ops:
  7.2 7.9 %collective-permute-start = (bf16[64,512]{1,0:T(8,128)(2,1)}, bf16[64,512]{1,0:T(8,128)(2,1)S(1)}, u32[]{:S(2)}, u32[]{:S(2)}) collective-permute-start(bf16[64,512]{1,0:T(8,128)(2,1)} %param.9), channel_id=1, source_target_pairs={{0,192},{192,0},{384,576},{576,384},{1,193},{193,1},{385,577},{577... | collective-permute-start | bytes 196616 | tf_op jit(solution)/shard_map/frozen_gather/ppermute | solution.py:188
  15.1 2.4 %collective-permute-done = bf16[64,512]{1,0:T(8,128)(2,1)S(1)} collective-permute-done((bf16[64,512]{1,0:T(8,128)(2,1)}, bf16[64,512]{1,0:T(8,128)(2,1)S(1)}, u32[]{:S(2)}, u32[]{:S(2)}) %collective-permute-start) | collective-permute-done | bytes 65568 | tf_op jit(solution)/shard_map/frozen_gather/ppermute | solution.py:188
  17.5 0.8 pad_maximum_fusion.1
  18.4 13.7 %collective-permute-start.1 = (bf16[128,512]{1,0:T(8,128)(2,1)S(1)}, bf16[128,512]{1,0:T(8,128)(2,1)S(1)}, u32[]{:S(2)}, u32[]{:S(2)}) collective-permute-start(bf16[128,512]{1,0:T(8,128)(2,1)S(1)} %pad_maximum_fusion.1), channel_id=1, source_target_pairs={{0,576},{192,384},{384,192},{576,0},{1,577},{193,385},{385,193},{5... | collective-permute-start | bytes 393224 | tf_op jit(solution)/shard_map/frozen_gather/ppermute | solution.py:188
  32.1 3.3 %pack.1 = bf16[192,4608]{1,0:T(8,128)(2,1)} custom-call(s32[1,12]{1,0:T(1,128)} %counts_ref.1, s32[1,192]{1,0:T(1,128)} %packing_ref.1, bf16[192,4096]{1,0:T(8,128)(2,1)} %rows_hbm.1, bf16[192,512]{1,0:T(8,128)(2,1)} %grads_ref.1), custom_call_target="tpu_custom_call" | custom-call | tf_op jit(solution)/shard_map/pack/pallas_call | solution.py:192
  35.4 4.0 %collective-permute-done.1 = bf16[128,512]{1,0:T(8,128)(2,1)S(1)} collective-permute-done((bf16[128,512]{1,0:T(8,128)(2,1)S(1)}, bf16[128,512]{1,0:T(8,128)(2,1)S(1)}, u32[]{:S(2)}, u32[]{:S(2)}) %collective-permute-start.1) | collective-permute-done | bytes 131104 | tf_op jit(solution)/shard_map/frozen_gather/ppermute | solution.py:188
  39.3 0.0 copy-start.4
  39.3 0.0 copy-start
  39.3 0.0 copy-start.1
  39.3 6.5 %all-to-all-start = ((bf16[12,16,4608]{2,1,0:T(8,128)(2,1)}), bf16[12,16,4608]{2,1,0:T(8,128)(2,1)S(1)}, u32[]{:S(2)}, u32[]{:S(2)}) async-start(bf16[12,16,4608]{2,1,0:T(8,128)(2,1)} %bitcast.33), calls=%async_computation | async-start | bytes 3538944 | tf_op jit(solution)/shard_map/pack/all_to_all | solution.py:210
  45.8 0.0 all-gather.2.cloned.1.call-start
  45.8 0.0 copy-done.4
  45.8 0.7 pad_maximum_fusion
  46.5 0.0 all-gather.2.cloned.1.call-update
  46.6 26.0 %all-to-all-done = bf16[12,16,4608]{2,1,0:T(8,128)(2,1)S(1)} async-done(((bf16[12,16,4608]{2,1,0:T(8,128)(2,1)}), bf16[12,16,4608]{2,1,0:T(8,128)(2,1)S(1)}, u32[]{:S(2)}, u32[]{:S(2)}) %all-to-all-start) | async-done | bytes 1769504 | tf_op jit(solution)/shard_map/pack/all_to_all | solution.py:210
  72.5 0.0 copy-done
  72.5 0.0 copy-done.1
  72.5 1.9 %adapters.3 = bf16[192,4096]{1,0:T(8,128)(2,1)} custom-call(bf16[192,4608]{1,0:T(8,128)(2,1)S(1)} %bitcast.23, bf16[64,4096]{1,0:T(8,128)(2,1)S(1)} %bitcast.25, bf16[64,512]{1,0:T(8,128)(2,1)S(1)} %bitcast.29), custom_call_target="tpu_custom_call" | custom-call | tf_op jit(solution)/shard_map/adapters/pallas_call | solution.py:218
  74.5 6.0 %all-to-all-start.1 = ((bf16[12,16,4096]{2,1,0:T(8,128)(2,1)}), bf16[12,16,4096]{2,1,0:T(8,128)(2,1)}, u32[]{:S(2)}, u32[]{:S(2)}) async-start(bf16[12,16,4096]{2,1,0:T(8,128)(2,1)} %bitcast.16), calls=%async_computation.1 | async-start | bytes 3145728 | tf_op jit(solution)/shard_map/adapters/all_to_all | solution.py:238
  80.5 0.1 pad_add_fusion.place_ref
  80.5 0.0 copy-start.2
  80.5 2.1 %adapters.2 = (f32[4,8,40,128]{3,2,1,0:T(8,128)S(1)}, f32[4,8,40,128]{3,2,1,0:T(8,128)S(1)}) custom-call(s32[4]{0:T(128)S(1)} %pad_add_fusion.place_ref, bf16[192,4608]{1,0:T(8,128)(2,1)S(1)} %bitcast.24, bf16[64,4096]{1,0:T(8,128)(2,1)S(1)} %bitcast.26, bf16[64,512]{1,0:T(8,128)(2,1)S(1)} %bitcast.30), custom_call_target="tpu_custom_call" | custom-call | tf_op jit(solution)/shard_map/adapters/pallas_call | solution.py:230
  82.7 1.9 %collective-permute-start.2 = (f32[2,640,128]{2,1,0:T(8,128)S(1)}, f32[2,640,128]{2,1,0:T(8,128)S(1)}, u32[]{:S(2)}, u32[]{:S(2)}) collective-permute-start(f32[2,640,128]{2,1,0:T(8,128)S(1)} %bitcast.32), channel_id=1, source_target_pairs={{0,12},{12,0},{1,13},{13,1},{2,14},{14,2},{3,15},{15,3},{4,16},{16... | collective-permute-start | bytes 1966088 | tf_op jit(solution)/shard_map/weight_grads/ppermute | solution.py:243
  84.6 2.1 %collective-permute-done.2.got_ref = f32[2,640,128]{2,1,0:T(8,128)S(1)} collective-permute-done((f32[2,640,128]{2,1,0:T(8,128)S(1)}, f32[2,640,128]{2,1,0:T(8,128)S(1)}, u32[]{:S(2)}, u32[]{:S(2)}) %collective-permute-start.2) | collective-permute-done | bytes 655392 | tf_op jit(solution)/shard_map/weight_grads/ppermute | solution.py:243
  86.7 0.1 weight_grads.4
  86.7 0.0 copy-done.2
  86.7 3.5 %collective-permute-start.3 = (bf16[640,128]{1,0:T(8,128)(2,1)S(1)}, bf16[640,128]{1,0:T(8,128)(2,1)S(1)}, u32[]{:S(2)}, u32[]{:S(2)}) collective-permute-start(bf16[640,128]{1,0:T(8,128)(2,1)S(1)} %get-tuple-element.20), channel_id=1, source_target_pairs={{0,24},{24,0},{1,25},{25,1},{2,26},{26,2},{3,27},{27,3},{4,28},{28... | collective-permute-start | bytes 491528 | tf_op jit(solution)/shard_map/weight_grads/ppermute | solution.py:253
  90.2 5.7 %collective-permute-done.3 = bf16[640,128]{1,0:T(8,128)(2,1)S(1)} collective-permute-done((bf16[640,128]{1,0:T(8,128)(2,1)S(1)}, bf16[640,128]{1,0:T(8,128)(2,1)S(1)}, u32[]{:S(2)}, u32[]{:S(2)}) %collective-permute-start.3) | collective-permute-done | bytes 163872 | tf_op jit(solution)/shard_map/weight_grads/ppermute | solution.py:253
  96.0 4.1 %collective-permute-start.4 = (bf16[320,128]{1,0:T(8,128)(2,1)S(1)}, bf16[320,128]{1,0:T(8,128)(2,1)S(1)}, u32[]{:S(2)}, u32[]{:S(2)}) collective-permute-start(bf16[320,128]{1,0:T(8,128)(2,1)S(1)} %get-tuple-element.22), channel_id=1, source_target_pairs={{0,48},{48,0},{1,49},{49,1},{2,50},{50,2},{3,51},{51,3},{4,52},{52... | collective-permute-start | bytes 245768 | tf_op jit(solution)/shard_map/weight_grads/ppermute | solution.py:253
  100.1 4.6 %collective-permute-done.4.got_ref = bf16[320,128]{1,0:T(8,128)(2,1)S(1)} collective-permute-done((bf16[320,128]{1,0:T(8,128)(2,1)S(1)}, bf16[320,128]{1,0:T(8,128)(2,1)S(1)}, u32[]{:S(2)}, u32[]{:S(2)}) %collective-permute-start.4) | collective-permute-done | bytes 81952 | tf_op jit(solution)/shard_map/weight_grads/ppermute | solution.py:253
  104.8 0.6 weight_grads.6
  105.4 0.0 all-gather.2.cloned.1.call-done
  105.4 1.9 %collective-permute-start.5 = (bf16[2048,512]{1,0:T(8,128)(2,1)}, bf16[2048,512]{1,0:T(8,128)(2,1)S(1)}, u32[]{:S(2)}, u32[]{:S(2)}) collective-permute-start(bf16[2048,512]{1,0:T(8,128)(2,1)} %all-gather.2.cloned.1.call-done), channel_id=1, source_target_pairs={{0,12},{12,0},{1,13},{13,1},{2,14},{14,2},{3,15},{15,3},{4,16},{16... | collective-permute-start | bytes 6291464 | tf_op jit(solution)/shard_map/weight_grads/ppermute | solution.py:266
  107.3 0.0 all-to-all-done.1
  107.3 10.6 %all-to-all-start.2 = ((bf16[8,40,128]{2,1,0:T(8,128)(2,1)}), bf16[8,40,128]{2,1,0:T(8,128)(2,1)S(1)}, u32[]{:S(2)}, u32[]{:S(2)}) async-start(bf16[8,40,128]{2,1,0:T(8,128)(2,1)} %bitcast.18), calls=%async_computation.2 | async-start | bytes 163840 | tf_op jit(solution)/shard_map/weight_grads/all_to_all | solution.py:268
  118.0 0.0 collective-permute-done.5
  118.0 0.0 copy-start.3
  118.0 1.3 copy-done.3
  119.3 6.4 %input_grad.1 = bf16[192,4096]{1,0:T(8,128)(2,1)} custom-call(s32[4]{0:T(128)} %copy-done.2, s32[1,12]{1,0:T(1,128)} %counts_ref.1, s32[1,192]{1,0:T(1,128)} %packing_ref.1, bf16[192,512]{1,0:T(8,128)(2,1)} %grads_ref.1, bf16[8,4,64,512]{3,2,1,0:T(8,128)(2,1)} %bitcast.34, bf16[8,4,64,512]{3,2,1,0:T(8,128)(2,1)} %bitcast.35, bf16[192,4096]{1,0:T(8,128)(2,1)} %bitcast.17.back_ref), custom_call_target="tpu_custom_call" | custom-call | tf_op jit(solution)/shard_map/input_grad/pallas_call | solution.py:293
  125.7 7.4 %all-to-all-done.2.got_ref = bf16[8,40,128]{2,1,0:T(8,128)(2,1)S(1)} async-done(((bf16[8,40,128]{2,1,0:T(8,128)(2,1)}), bf16[8,40,128]{2,1,0:T(8,128)(2,1)S(1)}, u32[]{:S(2)}, u32[]{:S(2)}) %all-to-all-start.2) | async-done | bytes 81952 | tf_op jit(solution)/shard_map/weight_grads/all_to_all | solution.py:268
  133.1 0.7 weight_grads.7
  (1 shorter events, 0.0 us)
Async XLA Ops:
  7.2 10.3 %collective-permute-start = (bf16[64,512]{1,0:T(8,128)(2,1)}, bf16[64,512]{1,0:T(8,128)(2,1)S(1)}, u32[]{:S(2)}, u32[]{:S(2)}) collective-permute-start(bf16[64,512]{1,0:T(8,128)(2,1)} %param.9), channel_id=1, source_target_pairs={{0,192},{192,0},{384,576},{576,384},{1,193},{193,1},{385,577},{577... | collective-permute-start | bytes 196616 | tf_op jit(solution)/shard_map/frozen_gather/ppermute | solution.py:188
  18.4 21.0 %collective-permute-start.1 = (bf16[128,512]{1,0:T(8,128)(2,1)S(1)}, bf16[128,512]{1,0:T(8,128)(2,1)S(1)}, u32[]{:S(2)}, u32[]{:S(2)}) collective-permute-start(bf16[128,512]{1,0:T(8,128)(2,1)S(1)} %pad_maximum_fusion.1), channel_id=1, source_target_pairs={{0,576},{192,384},{384,192},{576,0},{1,577},{193,385},{385,193},{5... | collective-permute-start | bytes 393224 | tf_op jit(solution)/shard_map/frozen_gather/ppermute | solution.py:188
  39.3 6.5 %copy-start.4 = (bf16[64,512]{1,0:T(8,128)(2,1)S(1)}, bf16[64,512]{1,0:T(8,128)(2,1)}, u32[]{:S(2)}) copy-start(bf16[64,512]{1,0:T(8,128)(2,1)} %param.9) | copy-start | bytes 196612
  39.3 33.2 %copy-start = (bf16[1,4096,64]{1,2,0:T(8,128)(2,1)S(1)}, bf16[1,4096,64]{1,2,0:T(8,128)(2,1)}, u32[]{:S(2)}) copy-start(bf16[1,4096,64]{1,2,0:T(8,128)(2,1)} %param.10) | copy-start | bytes 1572868
  39.3 33.2 %copy-start.1 = (bf16[1,64,512]{2,1,0:T(8,128)(2,1)S(1)}, bf16[1,64,512]{2,1,0:T(8,128)(2,1)}, u32[]{:S(2)}) copy-start(bf16[1,64,512]{2,1,0:T(8,128)(2,1)} %param.11) | copy-start | bytes 196612
  39.3 33.2 %all-to-all-start = ((bf16[12,16,4608]{2,1,0:T(8,128)(2,1)}), bf16[12,16,4608]{2,1,0:T(8,128)(2,1)S(1)}, u32[]{:S(2)}, u32[]{:S(2)}) async-start(bf16[12,16,4608]{2,1,0:T(8,128)(2,1)} %bitcast.33), calls=%async_computation | async-start | bytes 3538944 | tf_op jit(solution)/shard_map/pack/all_to_all | solution.py:210
  45.8 59.6 %all-gather.2.cloned.1.call-start = ((), (), s32[]{:S(2)}) async-start(), calls=%async_computation.3 | async-start | bytes 2359296 | tf_op jit(solution)/shard_map/pack/all_gather | solution.py:209
  74.5 32.8 %all-to-all-start.1 = ((bf16[12,16,4096]{2,1,0:T(8,128)(2,1)}), bf16[12,16,4096]{2,1,0:T(8,128)(2,1)}, u32[]{:S(2)}, u32[]{:S(2)}) async-start(bf16[12,16,4096]{2,1,0:T(8,128)(2,1)} %bitcast.16), calls=%async_computation.1 | async-start | bytes 3145728 | tf_op jit(solution)/shard_map/adapters/all_to_all | solution.py:238
  80.5 6.2 %copy-start.2 = (s32[4]{0:T(128)}, s32[4]{0:T(128)S(1)}, u32[]{:S(2)}) copy-start(s32[4]{0:T(128)S(1)} %pad_add_fusion.place_ref) | copy-start | bytes 52
  82.7 4.0 %collective-permute-start.2 = (f32[2,640,128]{2,1,0:T(8,128)S(1)}, f32[2,640,128]{2,1,0:T(8,128)S(1)}, u32[]{:S(2)}, u32[]{:S(2)}) collective-permute-start(f32[2,640,128]{2,1,0:T(8,128)S(1)} %bitcast.32), channel_id=1, source_target_pairs={{0,12},{12,0},{1,13},{13,1},{2,14},{14,2},{3,15},{15,3},{4,16},{16... | collective-permute-start | bytes 1966088 | tf_op jit(solution)/shard_map/weight_grads/ppermute | solution.py:243
  86.7 9.2 %collective-permute-start.3 = (bf16[640,128]{1,0:T(8,128)(2,1)S(1)}, bf16[640,128]{1,0:T(8,128)(2,1)S(1)}, u32[]{:S(2)}, u32[]{:S(2)}) collective-permute-start(bf16[640,128]{1,0:T(8,128)(2,1)S(1)} %get-tuple-element.20), channel_id=1, source_target_pairs={{0,24},{24,0},{1,25},{25,1},{2,26},{26,2},{3,27},{27,3},{4,28},{28... | collective-permute-start | bytes 491528 | tf_op jit(solution)/shard_map/weight_grads/ppermute | solution.py:253
  96.0 8.8 %collective-permute-start.4 = (bf16[320,128]{1,0:T(8,128)(2,1)S(1)}, bf16[320,128]{1,0:T(8,128)(2,1)S(1)}, u32[]{:S(2)}, u32[]{:S(2)}) collective-permute-start(bf16[320,128]{1,0:T(8,128)(2,1)S(1)} %get-tuple-element.22), channel_id=1, source_target_pairs={{0,48},{48,0},{1,49},{49,1},{2,50},{50,2},{3,51},{51,3},{4,52},{52... | collective-permute-start | bytes 245768 | tf_op jit(solution)/shard_map/weight_grads/ppermute | solution.py:253
  105.4 12.6 %collective-permute-start.5 = (bf16[2048,512]{1,0:T(8,128)(2,1)}, bf16[2048,512]{1,0:T(8,128)(2,1)S(1)}, u32[]{:S(2)}, u32[]{:S(2)}) collective-permute-start(bf16[2048,512]{1,0:T(8,128)(2,1)} %all-gather.2.cloned.1.call-done), channel_id=1, source_target_pairs={{0,12},{12,0},{1,13},{13,1},{2,14},{14,2},{3,15},{15,3},{4,16},{16... | collective-permute-start | bytes 6291464 | tf_op jit(solution)/shard_map/weight_grads/ppermute | solution.py:266
  107.3 25.7 %all-to-all-start.2 = ((bf16[8,40,128]{2,1,0:T(8,128)(2,1)}), bf16[8,40,128]{2,1,0:T(8,128)(2,1)S(1)}, u32[]{:S(2)}, u32[]{:S(2)}) async-start(bf16[8,40,128]{2,1,0:T(8,128)(2,1)} %bitcast.18), calls=%async_computation.2 | async-start | bytes 163840 | tf_op jit(solution)/shard_map/weight_grads/all_to_all | solution.py:268
  118.0 1.3 copy-start.3
Sparse Core Ops, SparseCore 0:
  49.0 45.8 all-gather.1
